TPU v7x, 128 devices: a whole 4x4x4 slice. The times are simulated.
128 devices in a mesh: shard: 4 (over y_lo, core), blk: 32 (over y_hi, z, x).
Axes of the slice: x: 4, y: 4 (y_hi: 2, y_lo: 2; y = y_hi * 2 + y_lo), z: 4, core: 2. Of those that a mesh axis runs over, the one named last changes fastest.
Arguments:
- hidden: float32 [4, 4096, 960], P('shard', 'blk'), may hold values from -6 to 6
- chosen: int32 [4, 4096], P('shard', 'blk'), may hold values from 0 to 1, as said below
- positions: int32 [4, 4096], P('shard', 'blk'), may hold values from 0 to 6142, as said below
- w_query: bfloat16 [960, 960], P('shard'), may hold values from -0.375 to 0.375
- w_key: bfloat16 [960, 320], P('shard'), may hold values from -0.1875 to 0.1875
- w_value: bfloat16 [960, 320], P('shard'), may hold values from -0.1875 to 0.1875
- w_output: bfloat16 [960, 960], P('shard'), may hold values from -6 to 6
- w_gate: bfloat16 [960, 2560], P('shard'), may hold values from -0.1875 to 0.1875
- w_up: bfloat16 [960, 2560], P('shard'), may hold values from -0.1875 to 0.1875
- w_down: bfloat16 [2560, 960], P('shard'), may hold values from -0.15625 to 0.15625
- gain_attn: bfloat16 [960], P('shard'), may hold values from 0.25 to 1.75
- gain_ffn: bfloat16 [960], P('shard'), may hold values from 0.25 to 1.75
- router: bfloat16 [960], P('shard'), may hold values from -0.1875 to 0.1875
- d_out: float32 [4, 4096, 960], P('shard', 'blk'), may hold values from -6 to 6
Outputs:
- output: float32 [4, 4096, 960], P('shard', 'blk')
- d_hidden: float32 [4, 4096, 960], P('shard', 'blk')
- g_query: float32 [960, 960], P('shard')
- g_key: float32 [960, 320], P('shard')
- g_value: float32 [960, 320], P('shard')
- g_output: float32 [960, 960], P('shard')
- g_gate: float32 [960, 2560], P('shard')
- g_up: float32 [960, 2560], P('shard')
- g_down: float32 [2560, 960], P('shard')
- g_gain_attn: float32 [960], P('shard')
- g_gain_ffn: float32 [960], P('shard')
- g_router: float32 [960], P('shard')
Inputs may be any that keep to these rules, and one draw needn't show every extreme that they name: `chosen`: in each aligned block of 256 tokens of a sequence exactly 128 tokens are 1 and the others 0. Along each sequence the positions start at 0 and rise by 1 or 2 from token to token; the last token of every sequence has position 6142.
All inputs are finite; a program needn't handle non-finite values.
Results may differ from a plain program's by a relative error of at most 0.035.
Values may be sent and summed in bfloat16 or wider, within the bound.
A program may use at most 192 MiB of HBM per device.

v0:
```python
import functools

import jax
import jax.numpy as jnp
from jax import lax
from jax.experimental import pallas as pl
from jax.experimental.pallas import tpu as pltpu
from jax.sharding import Mesh
from jax.sharding import PartitionSpec as P

D = 960
HEADS = 15
KV_HEADS = 5
GROUPS = 3
HEAD_DIM = 64
FF = 2560
EPS = 1e-05
THETA = 10000.0
SCALE = HEAD_DIM ** (-0.5)
T = 64
PAIR = 128
SLOTS = 32
KEYS = SLOTS * T
AX = ("ylo", "core", "yhi", "z", "x")
DIMS = (2, 2, 2, 4, 4)
MESH = pl.DeviceIdType.MESH
BF = jnp.bfloat16
F32 = jnp.float32
VMEM_LIMIT = 56 * 2**20


def dot(a, b, dims=(((1,), (0,)), ((), ()))):
    return lax.dot_general(a, b, dims, preferred_element_type=F32)


NT = (((1,), (1,)), ((), ()))
TN = (((0,), (0,)), ((), ()))


def moved(place, dy, dcore, dz, dx):
    ylo, core, yhi, z, x = place
    y = (yhi * 2 + ylo + dy) % 4
    return (y % 2, (core + dcore) % 2, y // 2, (z + dz) % 4, (x + dx) % 4)


def flat(place):
    at = 0
    for size, c in zip(DIMS, place):
        at = at * size + c
    return at


def places():
    for ylo in range(2):
        for core in range(2):
            for yhi in range(2):
                for z in range(4):
                    for x in range(4):
                        yield (ylo, core, yhi, z, x)


def permute(value, dy=0, dcore=0, dz=0, dx=0):
    return lax.ppermute(value, AX, [(flat(p), flat(moved(p, dy, dcore, dz, dx))) for p in places()])


def swap_x(value):
    return lax.ppermute(
        value, AX, [(flat(p), flat(p[:4] + (p[4] ^ 1,))) for p in places()]
    )


def here():
    return tuple(lax.axis_index(a) for a in AX)


def neighbour(me, axis, step):
    ylo, core, yhi, z, x = me
    if axis == "z":
        z = lax.rem(z + step + 4, 4)
    elif axis == "x":
        x = lax.rem(x + step + 4, 4)
    elif axis == "pair":
        x = x + 1 - 2 * lax.rem(x, 2)
    elif axis == "yhi":
        yhi = 1 - yhi
    elif axis == "ylo":
        ylo = 1 - ylo
    elif axis == "core":
        core = 1 - core
    else:
        y = lax.rem(yhi * 2 + ylo + step + 4, 4)
        ylo, yhi = lax.rem(y, 2), y // 2
    return (ylo, core, yhi, z, x)


NEAR = (("x", 1), ("x", -1), ("z", 1), ("z", -1), ("yhi", 1))
WEIGHT = (("y", 1), ("y", -1), ("core", 1))
SMALL = (("core", 1), ("ylo", 1), ("x", 2), ("z", 2))


def greet(me, partners):
    barrier = pltpu.get_barrier_semaphore()
    for axis, step in partners:
        pl.semaphore_signal(
            barrier, inc=1, device_id=neighbour(me, axis, step), device_id_type=MESH
        )
    pl.semaphore_wait(barrier, len(partners))


class Sends:
    def __init__(self, me, send_sems, recv_sems):
        self.me, self.send_sems, self.recv_sems, self.all = me, send_sems, recv_sems, []

    def start(self, src, dst, axis, step):
        k = len(self.all)
        copy = pltpu.make_async_remote_copy(
            src_ref=src,
            dst_ref=dst,
            send_sem=self.send_sems.at[k],
            recv_sem=self.recv_sems.at[k],
            device_id=neighbour(self.me, axis, step),
            device_id_type=MESH,
        )
        copy.start()
        self.all.append(copy)
        return copy

    def finish(self):
        for copy in self.all:
            copy.wait_send()


def together(*steps):
    steps = list(steps)
    while steps:
        for step in list(steps):
            try:
                next(step)
            except StopIteration:
                steps.remove(step)


def sems(count):
    return [pltpu.SemaphoreType.DMA((count,)), pltpu.SemaphoreType.DMA((count,))]


def plus(*terms):
    total = terms[0].astype(F32)
    for term in terms[1:]:
        total = total + term.astype(F32)
    return total


class Shards:
    def __init__(self, sends):
        self.sends, self.arrived, self.last = sends, [], []

    def near(self, own, out):
        self.last.append(self.sends.start(own, out.at[out.shape[0] - 3], "core", 1))

    def far(self, own, out, step, row, rows):
        r = pl.ds(row, rows)
        self.arrived.append((out, r, self.sends.start(own.at[r], out.at[out.shape[0] - 2, r], "y", step)))

    def relay(self):
        for out, r, copy in self.arrived:
            copy.wait_recv()
            self.last.append(self.sends.start(out.at[out.shape[0] - 2, r], out.at[out.shape[0] - 1, r], "core", 1))
        self.arrived = []

    def finish(self):
        self.relay()
        for copy in self.last:
            copy.wait_recv()
        self.last = []


def gather_steps(me, sends, kv_ref, out_ref):
    _, _, yh, z, x = me
    oy = 1 - yh
    half, quarter = T // 2, T // 4
    streams = (("x", "z", 0), ("z", "x", half))

    def slot(y, axis, step, rows, count):
        zz = lax.rem(z + step + 4, 4) if axis == "z" else z
        xx = lax.rem(x + step + 4, 4) if axis == "x" else x
        return out_ref.at[y, zz, xx, pl.ds(rows, count)]

    def line(y, axis, step, rows, count):
        if axis == "z":
            return out_ref.at[y, lax.rem(z + step + 4, 4), :, pl.ds(rows, count)]
        return out_ref.at[y, :, lax.rem(x + step + 4, 4), pl.ds(rows, count)]

    own = out_ref.at[yh, z, x]
    own[...] = kv_ref[...]
    first = sends.start(kv_ref, own, "yhi", 1)
    got = {}
    for y, tag in ((yh, 0), (oy, 1)):
        if tag:
            yield
            first.wait_recv()
        for axis, _, row in streams:
            src = slot(y, axis, 0, row, half)
            for step in (1, -1):
                got[tag, row, step] = sends.start(src, src, axis, step)
    far = {}
    for y, tag in ((yh, 0), (oy, 1)):
        yield
        for axis, _, row in streams:
            for step, off in ((1, 0), (-1, quarter)):
                got[tag, row, step].wait_recv()
                src = slot(y, axis, -step, row + off, quarter)
                far[tag, row, step] = sends.start(src, src, axis, step)
    wide = {}
    for y, tag in ((yh, 0), (oy, 1)):
        yield
        for _, axis, row in streams:
            for step in (1, -1):
                far[tag, row, step].wait_recv()
            src = line(y, axis, 0, row, half)
            for step in (1, -1):
                wide[tag, row, step] = sends.start(src, src, axis, step)
    last = []
    for y, tag in ((yh, 0), (oy, 1)):
        yield
        for _, axis, row in streams:
            for step, off in ((1, 0), (-1, quarter)):
                wide[tag, row, step].wait_recv()
                src = line(y, axis, -step, row + off, quarter)
                last.append(sends.start(src, src, axis, step))
    yield
    for copy in last:
        copy.wait_recv()


def swapped(x):
    lane = lax.broadcasted_iota(jnp.int32, x.shape, 1)
    return jnp.where(lane < HEAD_DIM // 2, pltpu.roll(x, 96, 1), pltpu.roll(x, 32, 1))


def front_kernel(
    hidden_ref, d_out_ref, chosen_ref, pos_ref, freq_ref, vec_ref, wq_ref, wk_ref, wv_ref,
    wo_ref, wg_ref, wu_ref, wd_ref,
    mix_ref, prob_ref, q_ref, kv_ref, h_ref, up_ref, x1_ref, cos_ref, sin_ref, place_ref, vec_out_ref,
    wq, wk, wv, wos_ref, wgs_ref, wus_ref, wds_ref,
    compact_h, compact_d, compact_p, got_h, got_d, got_p, vecs, q_pre, kv_own,
    load_sems, send_sems, recv_sems,
):
    me = here()
    yhi, z, x = me[2:]
    loads = []
    for k, (own, to) in enumerate(((wq_ref, wq), (wk_ref, wk), (wv_ref, wv))):
        loads.append(pltpu.make_async_copy(own, to.at[0], load_sems.at[k]))
        loads[-1].start()
    greet(me, NEAR + WEIGHT + (("pair", 1),))
    sends = Sends(me, send_sems, recv_sems)
    early, late = Shards(sends), Shards(sends)
    vec_far = sends.start(vec_ref, vecs.at[2], "y", 1)
    for own, to in ((wq_ref, wq), (wk_ref, wk), (wv_ref, wv)):
        early.far(own, to, 1, 0, 128)
        early.far(own, to, -1, 128, 112)
    vec_near = sends.start(vec_ref, vecs.at[1], "core", 1)
    for own, to in ((wq_ref, wq), (wk_ref, wk), (wv_ref, wv)):
        early.near(own, to)
    vecs[0] = vec_ref[...]

    odd = lax.rem(x, 2)
    flag = jnp.where(chosen_ref[...] > 0, 1.0, 0.0)
    token = lax.broadcasted_iota(jnp.int32, (PAIR, PAIR), 0)
    lane = lax.broadcasted_iota(jnp.int32, (PAIR, PAIR), 1)
    upto = jnp.where(token <= lane, 1.0, 0.0).astype(BF)
    count = dot(jnp.broadcast_to(flag, (16, PAIR)).astype(BF), upto)[0:1]
    total = jnp.sum(flag, axis=1, keepdims=True)
    rank = count - 1.0 + jnp.where(odd == 1, PAIR - total, 0.0)
    place = jnp.where(token.astype(F32) == rank, flag, 0.0)
    place_low = place.astype(BF)
    place_ref[...] = place_low
    compact_p[...] = jnp.broadcast_to(
        jnp.sum(place * pos_ref[...].astype(F32), axis=1, keepdims=True), (PAIR, PAIR)
    )
    compact_h[...] = dot(place_low, hidden_ref[...].astype(BF)).astype(BF)
    compact_d[...] = dot(place_low, d_out_ref[...].astype(BF)).astype(BF)
    give = pl.ds(pl.multiple_of((1 - odd) * T, T), T)
    keep = pl.ds(pl.multiple_of(odd * T, T), T)
    swaps = [
        sends.start(c.at[give], g, "pair", 1)
        for c, g in ((compact_h, got_h), (compact_p, got_p), (compact_d, got_d))
    ]
    vec_far.wait_recv()
    vec_last = sends.start(vecs.at[2], vecs.at[3], "core", 1)
    swaps[0].wait_recv()
    h = plus(compact_h[keep], got_h[...])
    h_ref[...] = h
    swaps[1].wait_recv()
    angle = (compact_p[keep] + got_p[...]) * freq_ref[...]
    turn = lax.broadcasted_iota(jnp.int32, (T, PAIR), 1)
    cosine = jnp.where(turn < HEAD_DIM, jnp.cos(angle), 1.0)
    sine = jnp.sin(angle)
    sine = jnp.where(turn < HEAD_DIM // 2, -sine, jnp.where(turn < HEAD_DIM, sine, 0.0))
    cos_ref[...], sin_ref[...] = cosine, sine
    vec_near.wait_recv()
    vec_last.wait_recv()
    vec_out_ref[...] = jnp.zeros_like(vec_out_ref)
    for k, v in enumerate(our_order(me, [vecs[k, :, :240] for k in range(4)])):
        vec_out_ref[:, 240 * k : 240 * (k + 1)] = v
    r1 = lax.rsqrt(jnp.mean(h * h, axis=-1, keepdims=True) + EPS)
    x1_ref[...] = (h * r1 * vec_out_ref[0:1, :D]).astype(BF)
    x1_k = our_order(me, cut_four(x1_ref))
    for copy in loads:
        copy.wait()
    early.relay()
    late.far(wo_ref, wos_ref, 1, 0, 128)
    late.far(wo_ref, wos_ref, -1, 128, 112)
    late.far(wg_ref, wgs_ref, 1, 0, 64)
    late.far(wg_ref, wgs_ref, -1, 128, 64)
    late.near(wo_ref, wos_ref)
    swaps[2].wait_recv()
    up_ref[...] = plus(compact_d[keep], got_d[...])
    early.finish()
    k_pre = sum(dot(x1_k[k], wk[k]) for k in range(4))
    v_pre = sum(dot(x1_k[k], wv[k]) for k in range(4))
    for j in range(KV_HEADS):
        run = slice(HEAD_DIM * j, HEAD_DIM * (j + 1))
        tile = jnp.concatenate([k_pre[:, run], v_pre[:, run]], axis=1)
        kv_own[:, 128 * j : 128 * (j + 1)] = (tile * cosine + swapped(tile) * sine).astype(BF)
    gather = gather_steps(me, sends, kv_own, kv_ref)
    next(gather)
    q_pre[...] = sum(dot(x1_k[k], wq[k]) for k in range(4))
    zero = jnp.zeros((T, HEAD_DIM), F32)
    for j in range(KV_HEADS):
        for g in range(GROUPS):
            at = HEAD_DIM * (GROUPS * j + g)
            tile = jnp.concatenate([q_pre[:, at : at + HEAD_DIM], zero], axis=1)
            q_ref[j, g * T : (g + 1) * T] = (tile * cosine + swapped(tile) * sine).astype(BF)
    next(gather)
    late.far(wg_ref, wgs_ref, 1, 64, 64)
    late.far(wg_ref, wgs_ref, -1, 192, 48)
    late.far(wu_ref, wus_ref, 1, 0, 128)
    late.far(wu_ref, wus_ref, -1, 128, 112)
    late.far(wd_ref, wds_ref, 1, 0, 320)
    late.far(wd_ref, wds_ref, -1, 320, 320)
    for own, out in ((wg_ref, wgs_ref), (wu_ref, wus_ref), (wd_ref, wds_ref)):
        late.near(own, out)
    together(gather)
    limit = ((yhi * 16 + z * 4 + x) // 2 + 1) * PAIR

    @pl.loop(0, KV_HEADS)
    def _(j):
        c = pl.ds(pl.multiple_of(j * 128, 128), 128)
        tile = kv_ref[:, :, :, :, c].reshape(KEYS, 128)
        scores = dot(q_ref[j], tile, NT) * SCALE
        column = lax.broadcasted_iota(jnp.int32, scores.shape, 1)
        scores = jnp.where(column < limit, scores, -1e30)
        exponent = jnp.exp(scores - jnp.max(scores, axis=-1, keepdims=True))
        prob = (exponent * (1.0 / jnp.sum(exponent, axis=-1, keepdims=True))).astype(BF)
        prob_ref[j] = prob
        mix_ref[j] = dot(prob, tile)

    late.finish()
    sends.finish()


def front(hidden, d_out, chosen, pos, freq, vec, w_query, w_key, w_value, *later):
    vmem, hbm = pl.BlockSpec(memory_space=pltpu.VMEM), pl.BlockSpec(memory_space=pl.ANY)
    rows = GROUPS * T
    return pl.pallas_call(
        front_kernel,
        name="front",
        out_shape=(
            jax.ShapeDtypeStruct((KV_HEADS, rows, 128), F32),
            jax.ShapeDtypeStruct((KV_HEADS, rows, KEYS), BF),
            jax.ShapeDtypeStruct((KV_HEADS, rows, 128), BF),
            jax.ShapeDtypeStruct((2, 4, 4, T, 640), BF),
            jax.ShapeDtypeStruct((T, D), F32),
            jax.ShapeDtypeStruct((T, D), F32),
            jax.ShapeDtypeStruct((T, D), BF),
            jax.ShapeDtypeStruct((T, 128), F32),
            jax.ShapeDtypeStruct((T, 128), F32),
            jax.ShapeDtypeStruct((PAIR, PAIR), BF),
            jax.ShapeDtypeStruct((8, 1024), F32),
            jax.ShapeDtypeStruct((4, 240, 960), BF),
            jax.ShapeDtypeStruct((4, 240, 320), BF),
            jax.ShapeDtypeStruct((4, 240, 320), BF),
        )
        + tuple(jax.ShapeDtypeStruct((3,) + w.shape, BF) for w in later),
        in_specs=[vmem] * 6 + [hbm] * 7,
        out_specs=(vmem,) * 14 + (hbm,) * 4,
        scratch_shapes=[
            pltpu.VMEM((PAIR, D), BF),
            pltpu.VMEM((PAIR, D), BF),
            pltpu.VMEM((PAIR, PAIR), F32),
            pltpu.VMEM((T, D), BF),
            pltpu.VMEM((T, D), BF),
            pltpu.VMEM((T, PAIR), F32),
            pltpu.VMEM((4, 8, 256), F32),
            pltpu.VMEM((T, D), F32),
            pltpu.VMEM((T, 640), BF),
            pltpu.SemaphoreType.DMA((3,)),
        ]
        + sems(84),
        compiler_params=pltpu.CompilerParams(
            collective_id=1, has_side_effects=True, vmem_limit_bytes=VMEM_LIMIT
        ),
        cost_estimate=pl.CostEstimate(flops=5_000_000_000, bytes_accessed=90_000_000, transcendentals=0),
    )(hidden, d_out, chosen, pos, freq, vec, w_query, w_key, w_value, *later)


def key_steps(me, sends, part_ref, out_ref, low, out_b, full, sums, nlow, nout, nfull, mine, y_in):
    _, _, yh, z, x = me
    half, quarter = T // 2, T // 4
    streams = (("x", "z", 0), ("z", "x", half))

    def line(axis, step, row, count):
        if axis == "z":
            return part_ref.at[:, lax.rem(z + step + 4, 4), :, pl.ds(row, count)]
        return part_ref.at[:, :, lax.rem(x + step + 4, 4), pl.ds(row, count)]

    near = {}
    for s, (axis, _, row) in enumerate(streams):
        near[s, 1] = sends.start(line(axis, 2, row, quarter), low.at[s, 0], axis, 1)
        near[s, -1] = sends.start(line(axis, 2, row + quarter, quarter), low.at[s, 1], axis, -1)
    whole = {}
    yield
    for s, (axis, _, row) in enumerate(streams):
        for d, step in enumerate((1, -1)):
            near[s, step].wait_recv()
            lo, hi = (0, quarter) if step == 1 else (quarter, 0)
            out_b[s, d, :, :, pl.ds(lo, quarter)] = plus(
                line(axis, step, row + lo, quarter)[...], low[s, d]
            ).astype(BF)
            out_b[s, d, :, :, pl.ds(hi, quarter)] = line(axis, step, row + hi, quarter)[...]
            whole[s, step] = sends.start(out_b.at[s, d], full.at[s, d], axis, step)
    yield
    near = {}
    for s, (axis, other, row) in enumerate(streams):
        for step in (1, -1):
            whole[s, step].wait_recv()
        sums[s] = plus(line(axis, 0, row, half)[...], full[s, 0], full[s, 1]).astype(BF)
        far = lax.rem((z if other == "z" else x) + 2, 4)
        near[s, 1] = sends.start(sums.at[s, :, far, pl.ds(0, quarter)], nlow.at[s, 0], other, 1)
        near[s, -1] = sends.start(
            sums.at[s, :, far, pl.ds(quarter, quarter)], nlow.at[s, 1], other, -1
        )
    yield
    for s, (axis, other, row) in enumerate(streams):
        at = z if other == "z" else x
        for d, step in enumerate((1, -1)):
            near[s, step].wait_recv()
            to = lax.rem(at + step + 4, 4)
            lo, hi = (0, quarter) if step == 1 else (quarter, 0)
            nout[s, d, :, pl.ds(lo, quarter)] = plus(
                sums[s, :, to, pl.ds(lo, quarter)], nlow[s, d]
            ).astype(BF)
            nout[s, d, :, pl.ds(hi, quarter)] = sums[s, :, to, pl.ds(hi, quarter)]
            whole[s, step] = sends.start(nout.at[s, d], nfull.at[s, d], other, step)
    yield
    swap = {}
    for s, (axis, other, row) in enumerate(streams):
        at = z if other == "z" else x
        for step in (1, -1):
            whole[s, step].wait_recv()
        mine[s] = plus(sums[s, :, at], nfull[s, 0], nfull[s, 1]).astype(BF)
        swap[s] = sends.start(mine.at[s, 1 - yh], y_in.at[s], "yhi", 1)
    yield
    for s, (axis, other, row) in enumerate(streams):
        swap[s].wait_recv()
        out_ref[pl.ds(row, half)] = plus(mine[s, yh], y_in[s])


def key_scratch():
    half, quarter, w = T // 2, T // 4, 640
    return [
        pltpu.VMEM((2, 2, 2, 4, quarter, w), BF),
        pltpu.VMEM((2, 2, 2, 4, half, w), BF),
        pltpu.VMEM((2, 2, 2, 4, half, w), BF),
        pltpu.VMEM((2, 2, 4, half, w), BF),
        pltpu.VMEM((2, 2, 2, quarter, w), BF),
        pltpu.VMEM((2, 2, 2, half, w), BF),
        pltpu.VMEM((2, 2, 2, half, w), BF),
        pltpu.VMEM((2, 2, half, w), BF),
        pltpu.VMEM((2, half, w), BF),
    ]


ROWS = 256
HALF = ROWS // 2
STREAMS = (("x", "z", 0), ("z", "x", HALF))
RUN = HALF // 4
CUT = HALF // 2


def spots(me):
    return {"z": me[3], "x": me[4]}


def around(me, axis, step):
    return lax.rem(spots(me)[axis] + step + 4, 4)


def columns(me, axis, step, big):
    return pl.ds(pl.multiple_of(around(me, axis, step) * big, 128), big)


def sum_steps(me, sends, g_ref, mine, low, out_b, full, sums, nlow, nout, nfull, y_in):
    big = mine.shape[-1]
    near, whole = {}, {}

    def parts(step):
        return (0, CUT) if step == 1 else (CUT, 0)

    for s, (axis, _, row) in enumerate(STREAMS):
        c = columns(me, axis, 2, big)
        for step in (1, -1):
            r = pl.ds(row + parts(step)[0], CUT)
            near[s, step] = sends.start(g_ref.at[r, c], low.at[r], axis, step)
    yield
    for s, (axis, _, row) in enumerate(STREAMS):
        for d, step in enumerate((1, -1)):
            near[s, step].wait_recv()
            add, keep = (pl.ds(row + p, CUT) for p in parts(step))
            c = columns(me, axis, step, big)
            out_b[d, add] = plus(g_ref[add, c], low[add]).astype(BF)
            out_b[d, keep] = g_ref[keep, c]
            r = pl.ds(row, HALF)
            whole[s, step] = sends.start(out_b.at[d, r], full.at[d, r], axis, step)
    yield
    half = RUN // 2

    def run(row, other, step, off, count):
        return pl.ds(pl.multiple_of(row + around(me, other, step) * RUN + off, 16), count)

    for s, (axis, other, row) in enumerate(STREAMS):
        for step in (1, -1):
            whole[s, step].wait_recv()
        r = pl.ds(row, HALF)
        sums[r] = plus(g_ref[r, columns(me, axis, 0, big)], full[0, r], full[1, r]).astype(BF)
        for d, step in enumerate((1, -1)):
            near[s, step] = sends.start(
                sums.at[run(row, other, 2, d * half, half)], nlow.at[s, d], other, step
            )
    yield
    for s, (axis, other, row) in enumerate(STREAMS):
        for d, step in enumerate((1, -1)):
            near[s, step].wait_recv()
            add, keep = (0, half) if step == 1 else (half, 0)
            nout[s, d, pl.ds(add, half)] = plus(
                sums[run(row, other, step, add, half)], nlow[s, d]
            ).astype(BF)
            nout[s, d, pl.ds(keep, half)] = sums[run(row, other, step, keep, half)]
            whole[s, step] = sends.start(nout.at[s, d], nfull.at[s, d], other, step)
    yield
    swap = {}
    for s, (axis, other, row) in enumerate(STREAMS):
        for step in (1, -1):
            whole[s, step].wait_recv()
        y_in[0, s] = plus(sums[run(row, other, 0, 0, RUN)], nfull[s, 0], nfull[s, 1]).astype(BF)
        swap[s] = sends.start(y_in.at[0, s], y_in.at[1, s], "yhi", 1)
    yield
    for s in range(2):
        swap[s].wait_recv()
        mine[s] = plus(y_in[0, s], y_in[1, s]).astype(BF)


def sum_scratch(width):
    big = width // 4
    return [
        pltpu.VMEM((ROWS, big), BF),
        pltpu.VMEM((2, ROWS, big), BF),
        pltpu.VMEM((2, ROWS, big), BF),
        pltpu.VMEM((ROWS, big), BF),
        pltpu.VMEM((2, 2, RUN // 2, big), BF),
        pltpu.VMEM((2, 2, RUN, big), BF),
        pltpu.VMEM((2, 2, RUN, big), BF),
        pltpu.VMEM((2, 2, RUN, big), BF),
    ]


def spread_steps(me, sends, mine, out_ref):
    big = mine.shape[-1]
    half = RUN // 2
    near, whole = {}, {}

    def run(row, other, step, off, count):
        return pl.ds(pl.multiple_of(row + around(me, other, step) * RUN + off, 16), count)

    for s, (axis, other, row) in enumerate(STREAMS):
        ref = out_ref.at[run(row, other, 0, 0, RUN), columns(me, axis, 0, big)]
        ref[...] = mine[s]
        for step in (1, -1):
            near[s, step] = sends.start(ref, ref, other, step)
    yield
    for s, (axis, other, row) in enumerate(STREAMS):
        for d, step in enumerate((1, -1)):
            near[s, step].wait_recv()
            ref = out_ref.at[run(row, other, -step, d * half, half), columns(me, axis, 0, big)]
            whole[s, step] = sends.start(ref, ref, other, step)
    yield
    for s, (axis, other, row) in enumerate(STREAMS):
        for step in (1, -1):
            whole[s, step].wait_recv()
        ref = out_ref.at[pl.ds(row, HALF), columns(me, axis, 0, big)]
        for step in (1, -1):
            near[s, step] = sends.start(ref, ref, axis, step)
    yield
    last = []
    for s, (axis, other, row) in enumerate(STREAMS):
        for d, step in enumerate((1, -1)):
            near[s, step].wait_recv()
            ref = out_ref.at[pl.ds(row + d * CUT, CUT), columns(me, axis, -step, big)]
            last.append(sends.start(ref, ref, axis, step))
    yield
    for copy in last:
        copy.wait_recv()


def vector_steps(sends, vec_ref, out_ref, keep, got):
    rounds = ((("core", 1),), (("ylo", 1),), (("x", 1), ("x", -1), ("x", 2)), (("z", 1), ("z", -1), ("z", 2)), (("yhi", 1),))
    keep[0] = vec_ref[...]
    k = 0
    for at, partners in enumerate(rounds):
        copies = []
        for axis, step in partners:
            copies.append((k, sends.start(keep.at[at], got.at[k], axis, step)))
            k += 1
        yield
        total = keep[at]
        for slot, copy in copies:
            copy.wait_recv()
            total = total + got[slot]
        keep[at + 1] = total
    out_ref[...] = keep[len(rounds)]


KEY_N, SUM_N = 9, 8


def scatter_kernel(part_ref, g_ref, own_ref, mine_ref, *scratch):
    me = here()
    greet(me, NEAR)
    sends = Sends(me, *scratch[-2:])
    together(
        key_steps(me, sends, part_ref, own_ref, *scratch[:KEY_N]),
        sum_steps(me, sends, g_ref, mine_ref, *scratch[KEY_N:-2]),
    )
    sends.finish()


def scatter_keys(part, g):
    vmem = pl.BlockSpec(memory_space=pltpu.VMEM)
    width = g.shape[1]
    return pl.pallas_call(
        scatter_kernel,
        name="scatter_keys",
        out_shape=(
            jax.ShapeDtypeStruct((T, 640), F32),
            jax.ShapeDtypeStruct((2, RUN, width // 4), BF),
        ),
        in_specs=[vmem, vmem],
        out_specs=(vmem, vmem),
        scratch_shapes=key_scratch() + sum_scratch(width) + sems(36),
        compiler_params=pltpu.CompilerParams(
            collective_id=2, has_side_effects=True, vmem_limit_bytes=VMEM_LIMIT
        ),
        cost_estimate=pl.CostEstimate(flops=0, bytes_accessed=120_000_000, transcendentals=0),
    )(part, g)


def last_kernel(mine_ref, g_ref, vec_ref, one_ref, two_ref, out_vec_ref, keep, got, own, *scratch):
    me = here()
    greet(me, NEAR + SMALL)
    sends = Sends(me, *scratch[-2:])

    def second():
        yield from sum_steps(me, sends, g_ref, own, *scratch[:-2])
        yield from spread_steps(me, sends, own, two_ref)

    together(
        vector_steps(sends, vec_ref, out_vec_ref, keep, got),
        second(),
        spread_steps(me, sends, mine_ref, one_ref),
    )
    sends.finish()


def reduce_last(mine, g, vec):
    vmem = pl.BlockSpec(memory_space=pltpu.VMEM)
    width = g.shape[1]
    return pl.pallas_call(
        last_kernel,
        name="reduce_last",
        out_shape=(
            jax.ShapeDtypeStruct((ROWS, mine.shape[2] * 4), BF),
            jax.ShapeDtypeStruct(g.shape, BF),
            jax.ShapeDtypeStruct(vec.shape, F32),
        ),
        in_specs=[vmem] * 3,
        out_specs=(vmem,) * 3,
        scratch_shapes=[
            pltpu.VMEM((6,) + vec.shape, F32),
            pltpu.VMEM((9,) + vec.shape, F32),
            pltpu.VMEM((2, RUN, width // 4), BF),
        ]
        + sum_scratch(width)
        + sems(64),
        compiler_params=pltpu.CompilerParams(
            collective_id=3, has_side_effects=True, vmem_limit_bytes=VMEM_LIMIT
        ),
        cost_estimate=pl.CostEstimate(flops=0, bytes_accessed=120_000_000, transcendentals=0),
    )(mine, g, vec)


def shard_of(me, k):
    ylo, core = me[0], me[1]
    return (ylo if k < 2 else 1 - ylo) * 2 + (core if k % 2 == 0 else 1 - core)


def our_order(me, p):
    core, ylo = me[1] == 1, me[0] == 1
    p = [jnp.where(core, p[k ^ 1], p[k]) for k in range(4)]
    return [jnp.where(ylo, p[k ^ 2], p[k]) for k in range(4)]


def cut_four(ref):
    return [ref[:, 240 * k : 240 * (k + 1)] for k in range(4)]


def norm_back_rows(z, r, gain, dy):
    dz = r * (gain * dy) - z * (r * r * r) * jnp.mean(gain * dy * z, axis=-1, keepdims=True)
    return dz, jnp.sum(dy * z * r, axis=0, keepdims=True)


def everyone_steps(sends, pieces):
    half = T // 2
    arrived, last = [], []
    for kind, source, whole, relay in pieces:
        near = source if kind == "all" else source[1]
        last.append(sends.start(near, whole.at[pl.ds(T, T)], "core", 1))
    for step, at in ((1, 0), (-1, half)):
        r = pl.ds(at, half)
        for kind, source, whole, relay in pieces:
            far = source if kind == "all" else source[2]
            arrived.append((sends.start(far.at[r], whole.at[pl.ds(2 * T + at, half)], "y", step), None))
            if kind == "all":
                arrived[-1] = (arrived[-1][0], (whole.at[pl.ds(2 * T + at, half)], whole.at[pl.ds(3 * T + at, half)]))
            else:
                copy = sends.start(source[3].at[r], relay.at[r], "y", step)
                arrived.append((copy, (relay.at[r], whole.at[pl.ds(3 * T + at, half)])))
    yield
    for copy, onward in arrived:
        copy.wait_recv()
        if onward is not None:
            last.append(sends.start(onward[0], onward[1], "core", 1))
    yield
    for copy in last:
        copy.wait_recv()


def dense_kernel(
    mix_ref, q_ref, prob_ref, kv_ref, h_ref, up_ref, vec_ref,
    wo_ref, wg_ref, wu_ref, wd_ref, wos_ref, wgs_ref, wus_ref, wds_ref,
    dq_ref, dkv_ref, g_ref, d_attn_ref, mixture_ref, d_mid_ref, out_ref, logit_ref, vec_out_ref,
    wo, wg, wu, wd, mixf, gate_s, up_s, inner, dgu, dffn, xs, do_s, d_mix_s,
    dgu_all, dffn_all, xs_all, inner_all, xs_relay, inner_relay,
    load_sems, send_sems, recv_sems,
):
    me = here()
    loads = []
    for k, (own, rest, to) in enumerate(
        ((wo_ref, wos_ref, wo), (wg_ref, wgs_ref, wg), (wu_ref, wus_ref, wu), (wd_ref, wds_ref, wd))
    ):
        pair = (
            pltpu.make_async_copy(own, to.at[0], load_sems.at[2 * k]),
            pltpu.make_async_copy(rest, to.at[pl.ds(1, 3)], load_sems.at[2 * k + 1]),
        )
        for copy in pair:
            copy.start()
        loads.append(pair)
    greet(me, WEIGHT)
    sends = Sends(me, send_sems, recv_sems)
    shards = [shard_of(me, k) for k in range(4)]

    def run640(k):
        return pl.ds(pl.multiple_of(shards[k] * 640, 128), 640)

    def run640_up(k):
        return pl.ds(pl.multiple_of(FF + shards[k] * 640, 128), 640)

    def loaded(k):
        for copy in loads[k]:
            copy.wait()

    for j in range(KV_HEADS):
        for g in range(GROUPS):
            h = GROUPS * j + g
            mixf[:, HEAD_DIM * h : HEAD_DIM * (h + 1)] = mix_ref[j, g * T : (g + 1) * T, HEAD_DIM:]
    mixture_ref[...] = mixf[...].astype(BF)
    mix_k = our_order(me, cut_four(mixture_ref))
    loaded(0)
    attn_out = sum(dot(mix_k[k], wo[k]) for k in range(4))
    hidden = h_ref[...]
    gain_f = vec_ref[1:2, :D]
    route_w = vec_ref[2:3, :D]
    middle = hidden + attn_out
    r2 = lax.rsqrt(jnp.mean(middle * middle, axis=-1, keepdims=True) + EPS)
    x2 = middle * r2 * gain_f
    x2_k = our_order(me, [x2[:, 240 * k : 240 * (k + 1)].astype(BF) for k in range(4)])
    xs[...] = jnp.zeros_like(xs)
    for k in range(4):
        xs[k, :, :240] = x2_k[k]
    loaded(1)
    gate_s[...] = sum(dot(x2_k[k], wg[k]) for k in range(4))
    loaded(2)
    up_s[...] = sum(dot(x2_k[k], wu[k]) for k in range(4))
    gate = gate_s[...]
    inner[...] = (gate * jax.nn.sigmoid(gate) * up_s[...]).astype(BF)
    loaded(3)
    ffn_out = sum(dot(inner[:, run640(k)], wd[k]) for k in range(4))
    route = jax.nn.sigmoid(jnp.sum(hidden * route_w, axis=-1, keepdims=True))
    branch = attn_out + ffn_out
    out_ref[...] = (route * branch).astype(BF)
    upstream = up_ref[...]
    d_branch = upstream * route
    d_logit = route * (1.0 - route) * jnp.sum(upstream * branch, axis=-1, keepdims=True)
    logit_ref[...] = jnp.broadcast_to(d_logit, logit_ref.shape)
    vec_out_ref[...] = jnp.zeros_like(vec_out_ref)
    vec_out_ref[2:3, :D] = jnp.sum(d_logit * hidden, axis=0, keepdims=True)
    d_ffn = d_branch.astype(BF)
    dffn[...] = jnp.zeros_like(dffn)
    for k in range(4):
        dffn[:, 256 * k : 256 * k + 240] = d_branch[:, 240 * k : 240 * (k + 1)].astype(BF)
    for k in range(4):
        d_inner = dot(d_ffn, wd[k], NT)
        gate, up = gate_s[:, run640(k)], up_s[:, run640(k)]
        sg = jax.nn.sigmoid(gate)
        dgu[:, run640(k)] = (d_inner * up * (sg + gate * sg * (1.0 - sg))).astype(BF)
        dgu[:, run640_up(k)] = (d_inner * (gate * sg)).astype(BF)
    pieces = (
        ("all", dgu, dgu_all, None),
        ("all", dffn, dffn_all, None),
        ("one", [xs.at[k] for k in range(4)], xs_all, xs_relay),
        ("one", [inner.at[:, run640(k)] for k in range(4)], inner_all, inner_relay),
    )
    share = everyone_steps(sends, pieces)
    next(share)
    own = pl.ds(0, T)
    dgu_all[own], dffn_all[own] = dgu[...], dffn[...]
    xs_all[own], inner_all[own] = xs[0], inner[:, run640(0)]
    d_gate, d_up = dgu[:, :FF], dgu[:, FF:]
    d_x2 = jnp.concatenate(
        our_order(me, [dot(d_gate, wg[k], NT) + dot(d_up, wu[k], NT) for k in range(4)]), axis=1
    )
    d_mid, g_gain_f = norm_back_rows(middle, r2, gain_f, d_x2)
    d_mid_ref[...] = d_mid
    vec_out_ref[1:2, :D] = g_gain_f
    d_attn = (d_branch + d_mid).astype(BF)
    d_attn_ref[...] = d_attn
    d_mix_s[...] = jnp.concatenate(our_order(me, [dot(d_attn, wo[k], NT) for k in range(4)]), axis=1)
    do_s[...] = jnp.zeros_like(do_s)
    for j in range(KV_HEADS):
        for g in range(GROUPS):
            h = GROUPS * j + g
            do_s[j, g * T : (g + 1) * T, HEAD_DIM:] = d_mix_s[:, HEAD_DIM * h : HEAD_DIM * (h + 1)].astype(BF)

    @pl.loop(0, KV_HEADS)
    def _(j):
        c = pl.ds(pl.multiple_of(j * 128, 128), 128)
        tile = kv_ref[:, :, :, :, c].reshape(KEYS, 128)
        prob, d_out = prob_ref[j], do_s[j]
        d_prob = dot(d_out, tile, NT)
        delta = jnp.sum(d_out.astype(F32) * mix_ref[j], axis=-1, keepdims=True)
        d_score = (prob.astype(F32) * (d_prob - delta)).astype(BF)
        dq_ref[j] = dot(d_score, tile) * SCALE
        grad = dot(d_score, q_ref[j], TN) * SCALE + dot(prob, d_out, TN)
        dkv_ref[:, :, :, :, c] = grad.astype(BF).reshape(2, 4, 4, T, 128)

    together(share)
    for c in range(0, 2 * FF, 1280):
        g_ref[:, c : c + 1280] = dot(xs_all[...], dgu_all[:, c : c + 1280], TN).astype(BF)
    for k in range(4):
        g_ref[:, 2 * FF + 640 * k : 2 * FF + 640 * (k + 1)] = dot(
            dffn_all[:, 256 * k : 256 * (k + 1)], inner_all[...], TN
        ).astype(BF)
    sends.finish()


def dense(mix, q, prob, kv, h, up_c, vec, own, rest):
    vmem, hbm = pl.BlockSpec(memory_space=pltpu.VMEM), pl.BlockSpec(memory_space=pl.ANY)
    rows = GROUPS * T
    return pl.pallas_call(
        dense_kernel,
        name="dense",
        out_shape=(
            jax.ShapeDtypeStruct((KV_HEADS, rows, 128), F32),
            jax.ShapeDtypeStruct((2, 4, 4, T, 640), BF),
            jax.ShapeDtypeStruct((ROWS, 3 * FF), BF),
            jax.ShapeDtypeStruct((T, D), BF),
            jax.ShapeDtypeStruct((T, D), BF),
            jax.ShapeDtypeStruct((T, D), F32),
            jax.ShapeDtypeStruct((T, D), BF),
            jax.ShapeDtypeStruct((T, 128), F32),
            jax.ShapeDtypeStruct((8, 1024), F32),
        ),
        in_specs=[vmem] * 7 + [hbm] * 8,
        out_specs=(vmem,) * 9,
        scratch_shapes=[
            pltpu.VMEM((4, 240, D), BF),
            pltpu.VMEM((4, 240, FF), BF),
            pltpu.VMEM((4, 240, FF), BF),
            pltpu.VMEM((4, 640, D), BF),
            pltpu.VMEM((T, D), F32),
            pltpu.VMEM((T, FF), F32),
            pltpu.VMEM((T, FF), F32),
            pltpu.VMEM((T, FF), BF),
            pltpu.VMEM((T, 2 * FF), BF),
            pltpu.VMEM((T, 1024), BF),
            pltpu.VMEM((4, T, 256), BF),
            pltpu.VMEM((KV_HEADS, rows, 128), BF),
            pltpu.VMEM((T, D), F32),
            pltpu.VMEM((4 * T, 2 * FF), BF),
            pltpu.VMEM((4 * T, 1024), BF),
            pltpu.VMEM((4 * T, 256), BF),
            pltpu.VMEM((4 * T, 640), BF),
            pltpu.VMEM((T, 256), BF),
            pltpu.VMEM((T, 640), BF),
            pltpu.SemaphoreType.DMA((8,)),
        ]
        + sems(28),
        compiler_params=pltpu.CompilerParams(
            collective_id=4, has_side_effects=True, vmem_limit_bytes=VMEM_LIMIT
        ),
        cost_estimate=pl.CostEstimate(
            flops=20_000_000_000, bytes_accessed=40_000_000, transcendentals=0
        ),
    )(mix, q, prob, kv, h, up_c, vec, *own, *rest)


def by_shard(x, width):
    core, ylo = lax.axis_index("core") == 1, lax.axis_index("ylo") == 1
    p = [x[..., k * width : (k + 1) * width] for k in range(4)]
    return ordered(p)


def ordered(p):
    core, ylo = lax.axis_index("core") == 1, lax.axis_index("ylo") == 1
    p = [jnp.where(core, p[k ^ 1], p[k]) for k in range(4)]
    return [jnp.where(ylo, p[k ^ 2], p[k]) for k in range(4)]


def rotate(values, cosine, sine):
    a, b = values[..., : HEAD_DIM // 2], values[..., HEAD_DIM // 2 :]
    return jnp.concatenate([a * cosine - b * sine, b * cosine + a * sine], axis=-1)


def norm_back(z, r, gain, dy):
    dz = r * (gain * dy) - z * (r * r * r) * jnp.mean(gain * dy * z, axis=-1, keepdims=True)
    return dz, jnp.sum(dy * z * r, axis=0)


def everyone(rows, slices):
    half = T // 2
    far = jnp.concatenate([rows, slices[2], slices[3]], axis=1)
    near = permute(jnp.concatenate([rows, slices[1]], axis=1), dcore=1)
    got = jnp.concatenate([permute(far[:half], dy=1), permute(far[half:], dy=-1)], axis=0)
    n, m = rows.shape[1], slices[0].shape[1]
    relay = permute(jnp.concatenate([got[:, :n], got[:, n + m :]], axis=1), dcore=1)
    every = jnp.concatenate([rows, near[:, :n], got[:, :n], relay[:, :n]], axis=0)
    some = jnp.concatenate([slices[0], near[:, n:], got[:, n : n + m], relay[:, n:]], axis=0)
    return every, some


def padded(a):
    return jnp.pad(a, ((0, 0), (0, ROWS - a.shape[1])))


def per_device(hidden, chosen, positions, w_query, w_key, w_value, w_output, w_gate, w_up, w_down, gain_attn, gain_ffn, router, d_out):
    tokens, upstream = hidden[0], d_out[0]
    odd = lax.rem(lax.axis_index("x"), 2) == 1
    own_w = (w_output, w_gate, w_up, w_down)
    frequency = THETA ** (-jnp.arange(0, HEAD_DIM // 2).astype(F32) * 2.0 / HEAD_DIM)
    vec = jnp.stack([gain_attn, gain_ffn, router]).astype(F32)
    vec = jnp.pad(vec, ((0, 5), (0, 16)))
    (
        mix_heads, prob, q_heads, kv_all, h, up_c, x1, cosine, sine, place, vec_in, wq, wk, wv, *rest_w
    ) = front(
        tokens, upstream, chosen, positions, jnp.tile(frequency, 4)[None, :], vec,
        w_query, w_key, w_value, *own_w
    )
    gain_a, route_w = vec_in[0, :D], vec_in[2, :D]
    r1 = lax.rsqrt(jnp.mean(h * h, axis=-1, keepdims=True) + EPS)
    x1_s = by_shard(x1, 240)
    cosine, sine = cosine[:, None, : HEAD_DIM // 2], -sine[:, None, : HEAD_DIM // 2]

    def tokens_first(a):
        return a.reshape(KV_HEADS, GROUPS, T, HEAD_DIM).transpose(2, 0, 1, 3).reshape(T, D)

    d_q_heads, d_kv, g_one, d_attn, mixture, d_mid, out_c, d_logit, vec_out = dense(
        mix_heads, q_heads, prob, kv_all, h, up_c, vec_in, own_w, rest_w
    )
    d_logit = d_logit[:, :1]
    mix_s = by_shard(mixture, 240)
    d_own, mine_one = scatter_keys(d_kv, g_one)
    d_own = d_own.reshape(T, KV_HEADS, 2 * HEAD_DIM)
    d_q = rotate(tokens_first(d_q_heads[..., :HEAD_DIM]).reshape(T, HEADS, HEAD_DIM), cosine, -sine)
    d_q = d_q.reshape(T, D).astype(BF)
    d_k = rotate(d_own[..., :HEAD_DIM], cosine, -sine).reshape(T, 320).astype(BF)
    d_v = d_own[..., HEAD_DIM:].reshape(T, 320).astype(BF)
    d_kv_low = jnp.concatenate([d_k, d_v], axis=1)
    d_x1 = jnp.concatenate(
        ordered([dot(d_q, wq[k], NT) + dot(d_k, wk[k], NT) + dot(d_v, wv[k], NT) for k in range(4)]), axis=1
    )
    d_first, g_gain_a = norm_back(h, r1, gain_a, d_x1)
    d_h = d_mid + d_first + d_logit * route_w[None, :]

    back = jnp.concatenate([out_c, d_h.astype(BF)], axis=1)
    other = swap_x(back)
    both = jnp.concatenate([jnp.where(odd, other, back), jnp.where(odd, back, other)], axis=0)
    spread = dot(place, both, TN)
    output = tokens + spread[:, :D]
    d_tokens = upstream + spread[:, D:]

    rows_2, some_2 = everyone(
        jnp.concatenate([d_q, d_kv_low, d_attn], axis=1),
        [jnp.concatenate([x1_s[k], mix_s[k]], axis=1) for k in range(4)],
    )
    g_two = jnp.concatenate(
        [
            dot(padded(some_2[:, :240]), rows_2[:, :1600], TN).astype(BF),
            dot(padded(some_2[:, 240:]), rows_2[:, 1600:], TN).astype(BF),
        ],
        axis=1,
    )
    vector = vec_out.at[0, :D].set(g_gain_a)
    s_one, s_two, vector = reduce_last(mine_one, g_two, vector)
    shard = lax.axis_index("ylo") * 2 + lax.axis_index("core")
    vector = lax.dynamic_slice_in_dim(vector, shard * 240, 240, axis=1)
    s_one, s_two = s_one[:240], s_two[:240]
    g_down = s_one[:, 2 * FF :].reshape(240, 4, 640).transpose(2, 1, 0).reshape(640, D)
    return (
        output[None],
        d_tokens[None],
        s_two[:, :960].astype(F32),
        s_two[:, 960:1280].astype(F32),
        s_two[:, 1280:1600].astype(F32),
        s_two[:, 1600:].astype(F32),
        s_one[:, :FF].astype(F32),
        s_one[:, FF : 2 * FF].astype(F32),
        g_down.astype(F32),
        vector[0],
        vector[1],
        vector[2],
    )


def solution(mesh):
    finer = Mesh(mesh.devices.reshape(DIMS), AX)
    shard, blk = ("ylo", "core"), ("yhi", "z", "x")
    act, row, weight, vec = P(shard, blk, None), P(shard, blk), P(shard, None), P(shard)
    return jax.shard_map(
        per_device,
        mesh=finer,
        in_specs=(act, row, row) + (weight,) * 7 + (vec,) * 3 + (act,),
        out_specs=(act, act) + (weight,) * 7 + (vec,) * 3,
        check_vma=False,
    )
```

profile of v0, /device:TPU:0, one launch (start us, length us, event | category | flops | bytes accessed | tf_op | source)
XLA Modules:
  0.0 270.5 jit_solution(12707341482701847135)
XLA Ops:
  0.7 2.5 copy.66.wd_ref
  3.3 1.0 copy.62
  4.3 1.0 copy.63
  5.2 0.8 copy.64.wk_ref
  6.1 0.8 copy.65.wv_ref
  6.9 0.6 broadcast_in_dim_tile.3.freq_ref
  7.5 0.6 fusion.54.vec_ref
  8.1 78.2 %front.1 = (f32[5,192,128]{2,1,0:T(8,128)}, bf16[5,192,2048]{2,1,0:T(8,128)(2,1)}, bf16[5,192,128]{2,1,0:T(8,128)(2,1)}, bf16[2,4,4,64,640]{4,3,2,1,0:T(8,128)(2...) custom-call(f32[128,960]{1,0:T(8,128)} %bitcast.89, ...), custom_call_target="tpu_custom_call" | custom-call | flops 5000000000 | bytes 90000000 | tf_op jit(solution)/shard_map/front/pallas_call | solution.py:366
  86.3 33.0 %dense.1 = (f32[5,192,128]{2,1,0:T(8,128)}, bf16[2,4,4,64,640]{4,3,2,1,0:T(8,128)(2,1)}, bf16[256,7680]{1,0:T(8,128)(2,1)}, bf16[64,960]{1,0:T(8,128)(2,1)}, bf1...) custom-call(f32[5,192,128]{2,1,0:T(8,128)} %get-tuple-element.57.mix, ...), custom_call_target="tpu_custom_call" | custom-call | flops 20000000000 | bytes 40000000 | tf_op jit(solution)/shard_map/dense/pallas_call | solution.py:889
  119.3 51.6 %scatter_keys.1 = (f32[64,640]{1,0:T(8,128)}, bf16[2,32,1920]{2,1,0:T(8,128)(2,1)}) custom-call(bf16[2,4,4,64,640]{4,3,2,1,0:T(8,128)(2,1)} %get-tuple-element.74.part_ref, bf16[256,7680]{1,0:T(8,128)(2,1)} %get-tuple-element.75.g_ref), custom_call_target="tpu_custom_call" | custom-call | bytes 120000000 | tf_op jit(solution)/shard_map/scatter_keys/pallas_call | solution.py:651
  170.9 1.0 reshape.141
  172.2 0.2 multiply_subtract_fusion
  174.2 0.2 concatenate.53
  174.5 0.8 fusion.60
  175.2 1.0 collective-permute-start.2
  176.3 2.2 collective-permute-start.3
  178.5 0.3 fusion.20
  178.8 0.3 fusion.14
  179.0 0.3 fusion.16
  179.3 0.3 fusion.18
  179.7 0.8 fusion.63
  182.4 0.2 multiply_reduce_fusion
  183.0 0.8 pad_maximum_fusion.5
  183.8 1.0 collective-permute-start
  184.9 1.4 scatter.4.vec_ref
  186.4 1.0 constant_dynamic-update-slice_fusion.1
  187.3 1.0 constant_dynamic-update-slice_fusion
  188.4 0.8 pad_maximum_fusion.2
  189.2 2.6 collective-permute-done
  191.9 0.3 fusion.10
  192.5 1.0 copy.83
  193.5 1.0 copy.84
  194.5 1.0 slice.270
  195.5 0.8 slice.262
  196.4 0.8 slice.273
  197.3 0.5 convolution_convert_fusion
  197.8 0.9 copy.80
  198.7 1.5 convolution_convert_fusion.1
  200.5 1.3 pad_maximum_fusion.1.g_ref
  201.8 53.0 %reduce_last.1 = (bf16[256,7680]{1,0:T(8,128)(2,1)}, bf16[256,2560]{1,0:T(8,128)(2,1)}, f32[8,1024]{1,0:T(8,128)}) custom-call(bf16[2,32,1920]{2,1,0:T(8,128)(2,1)} %get-tuple-element.80.mine_ref, bf16[256,2560]{1,0:T(8,128)(2,1)} %pad_maximum_fusion.1.g_ref, f32[8,1024]{1,0:T(8,128)} %scatter.4.vec_ref), custom_call_target="tpu_custom_call" | custom-call | bytes 120000000 | tf_op jit(solution)/shard_map/reduce_last/pallas_call | solution.py:688
  254.8 2.9 %slice_convert_fusion.3 = (f32[240,960]{1,0:T(8,128)}, f32[240,960]{1,0:T(8,128)}) fusion(bf16[256,2560]{1,0:T(8,128)(2,1)} %get-tuple-element.85), kind=kLoop, calls=%fused_computation.40 | loop fusion | flops 460800 | bytes 2764800 | tf_op jit(solution)/shard_map/convert_element_type | solution.py:1044
  257.7 1.2 slice_convert_fusion.5
  258.8 3.2 %slice_convert_fusion = (f32[240,2560]{1,0:T(8,128)S(1)}, f32[240,2560]{1,0:T(8,128)}, f32[240,2560]{1,0:T(8,128)}) fusion(bf16[256,7680]{1,0:T(8,128)(2,1)S(1)} %copy-done), kind=kLoop, calls=%fused_computation.4 | loop fusion | flops 1843200 | bytes 11059200 | tf_op jit(solution)/shard_map/convert_element_type | solution.py:1047
  262.1 1.9 reshape.144
  264.0 3.3 %copy.82 = f32[640,4,240]{0,2,1:T(8,128)} copy(f32[640,4,240]{0,1,2:T(4,128)} %bitcast.77) | data formatting | bytes 4915200 | tf_op jit(solution)/shard_map/convert_element_type | solution.py:1047
  267.3 0.9 copy.85
  268.2 0.9 copy.86
  269.1 1.5 fusion.62
  (99 shorter events, 5.2 us)
Async XLA Ops:
  0.6 2.6 copy-start.10
  0.7 3.6 %copy-start.11 = (f32[1,128,960]{1,2,0:T(8,128)S(1)}, f32[1,128,960]{1,2,0:T(8,128)}, u32[]{:S(2)}) copy-start(f32[1,128,960]{1,2,0:T(8,128)} %param.29) | copy-start | bytes 1474564
  0.7 4.6 %copy-start.13 = (bf16[240,320]{0,1:T(8,128)(2,1)S(1)}, bf16[240,320]{0,1:T(8,128)(2,1)}, u32[]{:S(2)}) copy-start(bf16[240,320]{0,1:T(8,128)(2,1)} %param.20) | copy-start | bytes 460804
  0.7 5.4 %copy-start.14 = (bf16[240,320]{0,1:T(8,128)(2,1)S(1)}, bf16[240,320]{0,1:T(8,128)(2,1)}, u32[]{:S(2)}) copy-start(bf16[240,320]{0,1:T(8,128)(2,1)} %param.21) | copy-start | bytes 460804
  3.2 3.6 %copy-start.22 = (bf16[240]{0:T(256)(128)(2,1)S(1)}, bf16[240]{0:T(256)(128)(2,1)}, u32[]{:S(2)}) copy-start(bf16[240]{0:T(256)(128)(2,1)} %param.26) | copy-start | bytes 1444
  3.2 3.6 %copy-start.23 = (bf16[240]{0:T(256)(128)(2,1)S(1)}, bf16[240]{0:T(256)(128)(2,1)}, u32[]{:S(2)}) copy-start(bf16[240]{0:T(256)(128)(2,1)} %param.27) | copy-start | bytes 1444
  3.2 3.7 %copy-start.24 = (bf16[240]{0:T(256)(128)(2,1)S(1)}, bf16[240]{0:T(256)(128)(2,1)}, u32[]{:S(2)}) copy-start(bf16[240]{0:T(256)(128)(2,1)} %param.28) | copy-start | bytes 1444
  119.3 52.9 %copy-start.15 = (f32[64,128]{1,0:T(8,128)S(1)}, f32[64,128]{1,0:T(8,128)}, u32[]{:S(2)}) copy-start(f32[64,128]{1,0:T(8,128)} %get-tuple-element.71) | copy-start | bytes 98308
  119.3 52.9 %copy-start.16 = (f32[64,128]{1,0:T(8,128)S(1)}, f32[64,128]{1,0:T(8,128)}, u32[]{:S(2)}) copy-start(f32[64,128]{1,0:T(8,128)} %get-tuple-element.72) | copy-start | bytes 98308
  170.9 1.3 copy-start.5
  172.4 1.2 copy-start.18
  172.4 1.3 copy-start.17
  172.5 1.4 copy-start.6
  173.3 5.2 %copy-start.4 = (bf16[4,240,960]{2,1,0:T(8,128)(2,1)S(1)}, bf16[4,240,960]{2,1,0:T(8,128)(2,1)}, u32[]{:S(2)}) copy-start(bf16[4,240,960]{2,1,0:T(8,128)(2,1)} %get-tuple-element.73) | copy-start | bytes 5529604
  174.1 20.4 %collective-permute-start.1 = (bf16[64,3040]{1,0:T(8,128)(2,1)S(1)}, bf16[64,3040]{1,0:T(8,128)(2,1)}, u32[]{:S(2)}, u32[]{:S(2)}) collective-permute-start(bf16[64,3040]{1,0:T(8,128)(2,1)S(1)} %concatenate.52), channel_id=1, source_target_pairs={{0,32},{1,33},{2,34},{3,35},{4,36},{5,37},{6,38},{7,39},{8,40},{9,... | collective-permute-start | bytes 1167368 | tf_op jit(solution)/shard_map/ppermute | solution.py:63
  174.4 5.2 %copy-start.1 = (f32[64,960]{1,0:T(8,128)S(1)}, f32[64,960]{1,0:T(8,128)}, u32[]{:S(2)}) copy-start(f32[64,960]{1,0:T(8,128)} %get-tuple-element.61.h_ref) | copy-start | bytes 737284
  174.4 6.1 %copy-start.8 = (bf16[4,240,320]{2,1,0:T(8,128)(2,1)S(1)}, bf16[4,240,320]{2,1,0:T(8,128)(2,1)}, u32[]{:S(2)}) copy-start(bf16[4,240,320]{2,1,0:T(8,128)(2,1)} %get-tuple-element.77) | copy-start | bytes 1843204
  175.2 11.1 %collective-permute-start.2 = (bf16[32,3520]{1,0:T(8,128)(2,1)}, bf16[32,3520]{1,0:T(8,128)(2,1)}, u32[]{:S(2)}, u32[]{:S(2)}) collective-permute-start(bf16[32,3520]{1,0:T(8,128)(2,1)} %get-tuple-element.144), channel_id=1, source_target_pairs={{0,64},{1,65},{2,66},{3,67},{4,68},{5,69},{6,70},{7,71},{8,72},{9,... | collective-permute-start | bytes 675848 | tf_op jit(solution)/shard_map/ppermute | solution.py:63
  176.3 11.0 %collective-permute-start.3 = (bf16[32,3520]{1,0:T(8,128)(2,1)}, bf16[32,3520]{1,0:T(8,128)(2,1)}, u32[]{:S(2)}, u32[]{:S(2)}) collective-permute-start(bf16[32,3520]{1,0:T(8,128)(2,1)} %get-tuple-element.143), channel_id=1, source_target_pairs={{0,80},{1,81},{2,82},{3,83},{4,84},{5,85},{6,86},{7,87},{8,88},{9,... | collective-permute-start | bytes 675848 | tf_op jit(solution)/shard_map/ppermute | solution.py:63
  178.5 2.8 %copy-start.7 = (bf16[4,240,320]{2,1,0:T(8,128)(2,1)S(1)}, bf16[4,240,320]{2,1,0:T(8,128)(2,1)}, u32[]{:S(2)}) copy-start(bf16[4,240,320]{2,1,0:T(8,128)(2,1)} %get-tuple-element.78) | copy-start | bytes 1843204
  180.6 2.0 copy-start.20
  180.8 1.9 copy-start.12
  181.3 1.7 copy-start.9
  183.8 8.0 %collective-permute-start = (bf16[64,1920]{1,0:T(8,128)(2,1)}, bf16[64,1920]{1,0:T(8,128)(2,1)S(1)}, u32[]{:S(2)}, u32[]{:S(2)}) collective-permute-start(bf16[64,1920]{1,0:T(8,128)(2,1)} %pad_maximum_fusion.5), channel_id=1, source_target_pairs={{0,1},{1,0},{2,3},{3,2},{4,5},{5,4},{6,7},{7,6},{8,9},{9,8},{10,11... | collective-permute-start | bytes 737288 | tf_op jit(solution)/shard_map/ppermute | solution.py:67
  184.9 7.0 %copy-start.19 = (bf16[128,128]{1,0:T(8,128)(2,1)S(1)}, bf16[128,128]{1,0:T(8,128)(2,1)}, u32[]{:S(2)}) copy-start(bf16[128,128]{1,0:T(8,128)(2,1)} %get-tuple-element.56) | copy-start | bytes 98308
  188.3 4.0 %copy-start.2 = (f32[1,128,960]{2,1,0:T(8,128)S(1)}, f32[1,128,960]{2,1,0:T(8,128)}, u32[]{:S(2)}) copy-start(f32[1,128,960]{2,1,0:T(8,128)} %copy.62) | copy-start | bytes 1474564
  188.3 4.0 %copy-start.3 = (f32[1,128,960]{2,1,0:T(8,128)S(1)}, f32[1,128,960]{2,1,0:T(8,128)}, u32[]{:S(2)}) copy-start(f32[1,128,960]{2,1,0:T(8,128)} %copy.63) | copy-start | bytes 1474564
  189.2 7.1 %collective-permute-start.4 = (bf16[64,3040]{1,0:T(8,128)(2,1)}, bf16[64,3040]{1,0:T(8,128)(2,1)S(1)}, u32[]{:S(2)}, u32[]{:S(2)}) collective-permute-start(bf16[64,3040]{1,0:T(8,128)(2,1)} %pad_maximum_fusion.2), channel_id=1, source_target_pairs={{0,32},{1,33},{2,34},{3,35},{4,36},{5,37},{6,38},{7,39},{8,40},{9,... | collective-permute-start | bytes 1167368 | tf_op jit(solution)/shard_map/ppermute | solution.py:63
  196.3 1.0 copy-start.21
  254.8 4.0 %copy-start = (bf16[256,7680]{1,0:T(8,128)(2,1)S(1)}, bf16[256,7680]{1,0:T(8,128)(2,1)}, u32[]{:S(2)}) copy-start(bf16[256,7680]{1,0:T(8,128)(2,1)} %get-tuple-element.86) | copy-start | bytes 11796484
where the time goes:
time: 271 us
  Pallas kernels  216 us (80%)
  local copies, waits for them, and re-layouts  28.8 us (11%)
  other arithmetic  12.6 us (5%)
  matrix products  5.17 us (2%)
  starting transfers between devices  4.3 us (2%)
    pallas_call x1, Pallas kernels, front(): pl.pallas_call(front_kernel, name='front', out_shape=(jax.ShapeDtypeStruc...  78.2 us
    pallas_call x1, Pallas kernels, reduce_last(): pl.pallas_call(last_kernel, name='reduce_last', out_shape=(jax.ShapeDtype...  53 us
    pallas_call x1, Pallas kernels, scatter_keys(): pl.pallas_call(scatter_kernel, name='scatter_keys', out_shape=(jax.ShapeD...  51.6 us
    pallas_call x1, Pallas kernels, dense(): pl.pallas_call(dense_kernel, name='dense', out_shape=(jax.ShapeDtypeStruc...  33 us
    unnamed x61, local copies, waits for them, and re-layouts  10.9 us
  transfers between devices with their start and end apart: 5, of which 1 were waited for; matrix products, arithmetic and copies ran while one was open for 6% of the time, Pallas kernels for 0%

commit v1 on v0

--- a/solution.py
+++ b/solution.py
@@ -37,38 +37,6 @@
 TN = (((0,), (0,)), ((), ()))
 
 
-def moved(place, dy, dcore, dz, dx):
-    ylo, core, yhi, z, x = place
-    y = (yhi * 2 + ylo + dy) % 4
-    return (y % 2, (core + dcore) % 2, y // 2, (z + dz) % 4, (x + dx) % 4)
-
-
-def flat(place):
-    at = 0
-    for size, c in zip(DIMS, place):
-        at = at * size + c
-    return at
-
-
-def places():
-    for ylo in range(2):
-        for core in range(2):
-            for yhi in range(2):
-                for z in range(4):
-                    for x in range(4):
-                        yield (ylo, core, yhi, z, x)
-
-
-def permute(value, dy=0, dcore=0, dz=0, dx=0):
-    return lax.ppermute(value, AX, [(flat(p), flat(moved(p, dy, dcore, dz, dx))) for p in places()])
-
-
-def swap_x(value):
-    return lax.ppermute(
-        value, AX, [(flat(p), flat(p[:4] + (p[4] ^ 1,))) for p in places()]
-    )
-
-
 def here():
     return tuple(lax.axis_index(a) for a in AX)
 
@@ -154,18 +122,21 @@
 class Shards:
     def __init__(self, sends):
         self.sends, self.arrived, self.last = sends, [], []
+        self.color = lax.rem(sends.me[3] + sends.me[4], 2)
 
     def near(self, own, out):
         self.last.append(self.sends.start(own, out.at[out.shape[0] - 3], "core", 1))
 
-    def far(self, own, out, step, row, rows):
-        r = pl.ds(row, rows)
-        self.arrived.append((out, r, self.sends.start(own.at[r], out.at[out.shape[0] - 2, r], "y", step)))
+    def far(self, own, out, cut):
+        for step, row, rows in ((1, 0, cut), (-1, cut, own.shape[0] - cut)):
+            r = pl.ds(row, rows)
+            ref = out.at[out.shape[0] - 2, r]
+            self.arrived.append((ref, out.at[out.shape[0] - 1, r], self.sends.start(own.at[r], ref, "y", step)))
 
     def relay(self):
-        for out, r, copy in self.arrived:
+        for ref, to, copy in self.arrived:
             copy.wait_recv()
-            self.last.append(self.sends.start(out.at[out.shape[0] - 2, r], out.at[out.shape[0] - 1, r], "core", 1))
+            self.last.append(self.sends.start(ref, to, "core", 1))
         self.arrived = []
 
     def finish(self):
@@ -173,6 +144,35 @@
         for copy in self.last:
             copy.wait_recv()
         self.last = []
+
+    def half(self, own, out, block, cuts):
+        rows, slots = own.shape[0], out.shape[0]
+        sub = block // 2
+        mine = self.color * (rows - block)
+
+        def part(slot, start, count):
+            return out.at[slot, pl.ds(pl.multiple_of(start, 16), count)]
+
+        copies = []
+        for step, off in ((1, 0), (-1, sub)):
+            src = own.at[pl.ds(pl.multiple_of(mine + off, 16), sub)]
+            copies.append(self.sends.start(src, part(slots - 2, mine + off, sub), "y", step))
+        yield
+        for copy in copies:
+            copy.wait_recv()
+        copies, off = [], 0
+        for (axis, step), count in zip((("x", 1), ("x", -1), ("z", 1), ("z", -1)), cuts):
+            ref = part(slots - 2, self.color * block + off, count)
+            copies.append(self.sends.start(ref, ref, axis, step))
+            off += count
+        self.last.append(self.sends.start(part(slots - 2, mine, block), part(slots - 1, mine, block), "core", 1))
+        yield
+        for copy in copies:
+            copy.wait_recv()
+        rest = (1 - self.color) * block
+        self.last.append(
+            self.sends.start(part(slots - 2, rest, rows - block), part(slots - 1, rest, rows - block), "core", 1)
+        )
 
 
 def gather_steps(me, sends, kv_ref, out_ref):
@@ -254,14 +254,15 @@
         loads[-1].start()
     greet(me, NEAR + WEIGHT + (("pair", 1),))
     sends = Sends(me, send_sems, recv_sems)
-    early, late = Shards(sends), Shards(sends)
+    early, query, late = Shards(sends), Shards(sends), Shards(sends)
     vec_far = sends.start(vec_ref, vecs.at[2], "y", 1)
-    for own, to in ((wq_ref, wq), (wk_ref, wk), (wv_ref, wv)):
-        early.far(own, to, 1, 0, 128)
-        early.far(own, to, -1, 128, 112)
+    early.far(wk_ref, wk, 160)
+    early.far(wv_ref, wv, 160)
     vec_near = sends.start(vec_ref, vecs.at[1], "core", 1)
-    for own, to in ((wq_ref, wq), (wk_ref, wk), (wv_ref, wv)):
-        early.near(own, to)
+    early.near(wk_ref, wk)
+    early.near(wv_ref, wv)
+    query.far(wq_ref, wq, 128)
+    query.near(wq_ref, wq)
     vecs[0] = vec_ref[...]
 
     odd = lax.rem(x, 2)
@@ -278,8 +279,8 @@
     compact_p[...] = jnp.broadcast_to(
         jnp.sum(place * pos_ref[...].astype(F32), axis=1, keepdims=True), (PAIR, PAIR)
     )
-    compact_h[...] = dot(place_low, hidden_ref[...].astype(BF)).astype(BF)
-    compact_d[...] = dot(place_low, d_out_ref[...].astype(BF)).astype(BF)
+    compact_h[...] = dot(place_low, hidden_ref[...].astype(BF), NT).astype(BF)
+    compact_d[...] = dot(place_low, d_out_ref[...].astype(BF), NT).astype(BF)
     give = pl.ds(pl.multiple_of((1 - odd) * T, T), T)
     keep = pl.ds(pl.multiple_of(odd * T, T), T)
     swaps = [
@@ -308,23 +309,18 @@
     x1_k = our_order(me, cut_four(x1_ref))
     for copy in loads:
         copy.wait()
-    early.relay()
-    late.far(wo_ref, wos_ref, 1, 0, 128)
-    late.far(wo_ref, wos_ref, -1, 128, 112)
-    late.far(wg_ref, wgs_ref, 1, 0, 64)
-    late.far(wg_ref, wgs_ref, -1, 128, 64)
-    late.near(wo_ref, wos_ref)
-    swaps[2].wait_recv()
-    up_ref[...] = plus(compact_d[keep], got_d[...])
     early.finish()
-    k_pre = sum(dot(x1_k[k], wk[k]) for k in range(4))
-    v_pre = sum(dot(x1_k[k], wv[k]) for k in range(4))
+    k_pre = sum(dot(x1_k[k], wk[k], NT) for k in range(4))
+    v_pre = sum(dot(x1_k[k], wv[k], NT) for k in range(4))
     for j in range(KV_HEADS):
         run = slice(HEAD_DIM * j, HEAD_DIM * (j + 1))
         tile = jnp.concatenate([k_pre[:, run], v_pre[:, run]], axis=1)
         kv_own[:, 128 * j : 128 * (j + 1)] = (tile * cosine + swapped(tile) * sine).astype(BF)
     gather = gather_steps(me, sends, kv_own, kv_ref)
     next(gather)
+    query.finish()
+    swaps[2].wait_recv()
+    up_ref[...] = plus(compact_d[keep], got_d[...])
     q_pre[...] = sum(dot(x1_k[k], wq[k]) for k in range(4))
     zero = jnp.zeros((T, HEAD_DIM), F32)
     for j in range(KV_HEADS):
@@ -333,15 +329,25 @@
             tile = jnp.concatenate([q_pre[:, at : at + HEAD_DIM], zero], axis=1)
             q_ref[j, g * T : (g + 1) * T] = (tile * cosine + swapped(tile) * sine).astype(BF)
     next(gather)
-    late.far(wg_ref, wgs_ref, 1, 64, 64)
-    late.far(wg_ref, wgs_ref, -1, 192, 48)
-    late.far(wu_ref, wus_ref, 1, 0, 128)
-    late.far(wu_ref, wus_ref, -1, 128, 112)
-    late.far(wd_ref, wds_ref, 1, 0, 320)
-    late.far(wd_ref, wds_ref, -1, 320, 320)
-    for own, out in ((wg_ref, wgs_ref), (wu_ref, wus_ref), (wd_ref, wds_ref)):
+    small, large = (128, (32, 32, 32, 16)), (480, (128, 128, 112, 112))
+    out_w = late.half(wo_ref, wos_ref, *small)
+    gate_w = late.half(wg_ref, wgs_ref, *small)
+    up_w = late.half(wu_ref, wus_ref, *small)
+    down_w = late.half(wd_ref, wds_ref, *large)
+    for w in (out_w, gate_w, up_w, down_w):
+        next(w)
+    for own, out in ((wo_ref, wos_ref), (wg_ref, wgs_ref), (wu_ref, wus_ref), (wd_ref, wds_ref)):
         late.near(own, out)
+    next(gather)
+    next(gather)
+    next(out_w)
+    next(gather)
+    next(gather)
+    next(gate_w)
     together(gather)
+    next(up_w)
+    together(out_w)
+    together(gate_w)
     limit = ((yhi * 16 + z * 4 + x) // 2 + 1) * PAIR
 
     @pl.loop(0, KV_HEADS)
@@ -356,6 +362,9 @@
         prob_ref[j] = prob
         mix_ref[j] = dot(prob, tile)
 
+    next(down_w)
+    together(up_w)
+    together(down_w)
     late.finish()
     sends.finish()
 
@@ -379,8 +388,8 @@
             jax.ShapeDtypeStruct((PAIR, PAIR), BF),
             jax.ShapeDtypeStruct((8, 1024), F32),
             jax.ShapeDtypeStruct((4, 240, 960), BF),
-            jax.ShapeDtypeStruct((4, 240, 320), BF),
-            jax.ShapeDtypeStruct((4, 240, 320), BF),
+            jax.ShapeDtypeStruct((4, 320, 240), BF),
+            jax.ShapeDtypeStruct((4, 320, 240), BF),
         )
         + tuple(jax.ShapeDtypeStruct((3,) + w.shape, BF) for w in later),
         in_specs=[vmem] * 6 + [hbm] * 7,
@@ -397,7 +406,7 @@
             pltpu.VMEM((T, 640), BF),
             pltpu.SemaphoreType.DMA((3,)),
         ]
-        + sems(84),
+        + sems(90),
         compiler_params=pltpu.CompilerParams(
             collective_id=1, has_side_effects=True, vmem_limit_bytes=VMEM_LIMIT
         ),
@@ -631,82 +640,194 @@
     out_ref[...] = keep[len(rounds)]
 
 
+def small_steps(me, sends, g_ref, out_ref, got_x, got_z, got_y, sum_z, sum_y):
+    x, z = me[4], me[3]
+    steps = (1, -1, 2)
+
+    def rows(at, step, count, base=0):
+        return pl.ds(pl.multiple_of(base + lax.rem(at + step + 4, 4) * count, 16), count)
+
+    copies = [
+        sends.start(g_ref.at[rows(x, step, 64)], got_x.at[k], "x", step) for k, step in enumerate(steps)
+    ]
+    yield
+    for copy in copies:
+        copy.wait_recv()
+    sum_z[...] = plus(g_ref[rows(x, 0, 64)], got_x[0], got_x[1], got_x[2]).astype(BF)
+    copies = [
+        sends.start(sum_z.at[rows(z, step, 16)], got_z.at[k], "z", step) for k, step in enumerate(steps)
+    ]
+    yield
+    for copy in copies:
+        copy.wait_recv()
+    sum_y[...] = plus(sum_z[rows(z, 0, 16)], got_z[0], got_z[1], got_z[2]).astype(BF)
+    copy = sends.start(sum_y, got_y, "yhi", 1)
+    yield
+    copy.wait_recv()
+    ref = out_ref.at[rows(z, 0, 16, x * 64)]
+    ref[...] = plus(sum_y[...], got_y[...]).astype(BF)
+    copies = [sends.start(ref, ref, "z", step) for step in steps]
+    yield
+    for copy in copies:
+        copy.wait_recv()
+    ref = out_ref.at[rows(x, 0, 64)]
+    copies = [sends.start(ref, ref, "x", step) for step in steps]
+    yield
+    for copy in copies:
+        copy.wait_recv()
+
+
 KEY_N, SUM_N = 9, 8
-
-
-def scatter_kernel(part_ref, g_ref, own_ref, mine_ref, *scratch):
+WIDE, REST = 2 * FF, 4608
+
+
+def back_kernel(
+    part_ref, g_ref, dq_ref, d_attn_ref, mixture_ref, x1_ref, h_ref, d_mid_ref, out_ref, logit_ref, vec_ref, vec_part_ref,
+    cos_ref, sin_ref, wq, wk, wv,
+    one_ref, two_ref, three_ref, vec_out_ref, both_ref,
+    own, ra, rb, xs, ra_all, rb_all, xs_all, xs_relay, g_two, g_three, d_x1_s, vec_all, keep_v, got_v,
+    mine_one, mine_two, got_x, got_z, got_y, sum_z, sum_y,
+    *scratch,
+):
     me = here()
-    greet(me, NEAR)
+    key_scr, one_scr, two_scr = scratch[:KEY_N], scratch[KEY_N : KEY_N + SUM_N], scratch[KEY_N + SUM_N : -2]
+    greet(me, NEAR + WEIGHT + SMALL + (("pair", 1),))
     sends = Sends(me, *scratch[-2:])
-    together(
-        key_steps(me, sends, part_ref, own_ref, *scratch[:KEY_N]),
-        sum_steps(me, sends, g_ref, mine_ref, *scratch[KEY_N:-2]),
-    )
+    odd = lax.rem(me[4], 2)
+    keep = pl.ds(pl.multiple_of(odd * T, T), T)
+    cosine, sine = cos_ref[...], sin_ref[...]
+    mine = pl.ds(0, T)
+
+    def turned_back(tile):
+        return tile * cosine - swapped(tile) * sine
+
+    def keys():
+        yield from key_steps(me, sends, part_ref, own, *key_scr)
+        for j in range(KV_HEADS):
+            tile = turned_back(own[:, 128 * j : 128 * (j + 1)]).astype(BF)
+            rb[:, HEAD_DIM * j : HEAD_DIM * (j + 1)] = tile[:, :HEAD_DIM]
+            rb[:, 320 + HEAD_DIM * j : 320 + HEAD_DIM * (j + 1)] = tile[:, HEAD_DIM:]
+        share = everyone_steps(sends, (("all", rb, rb_all, None),))
+        next(share)
+        rb_all[mine] = rb[...]
+        d_k, d_v = rb[:, :320], rb[:, 320:]
+        d_x1 = d_x1_s[...] + jnp.concatenate(
+            our_order(me, [dot(d_k, wk[k]) + dot(d_v, wv[k]) for k in range(4)]), axis=1
+        )
+        h = h_ref[...]
+        r1 = lax.rsqrt(jnp.mean(h * h, axis=-1, keepdims=True) + EPS)
+        d_first, g_gain_a = norm_back_rows(h, r1, vec_ref[0:1, :D], d_x1)
+        d_h = d_mid_ref[...] + d_first + logit_ref[:, 0:1] * vec_ref[2:3, :D]
+        both_ref[keep, :D] = out_ref[...]
+        both_ref[keep, D:] = d_h.astype(BF)
+        swap = sends.start(both_ref.at[keep], both_ref.at[keep], "pair", 1)
+        vec_all[...] = vec_part_ref[...]
+        vec_all[0:1, :D] = g_gain_a
+        vectors = vector_steps(sends, vec_all, vec_out_ref, keep_v, got_v)
+        next(vectors)
+        yield
+        next(share)
+        yield
+        together(share)
+        g_three[...] = dot(xs_all[:, :256], rb_all[...], TN).astype(BF)
+        small = small_steps(me, sends, g_three, three_ref, got_x, got_z, got_y, sum_z, sum_y)
+        while True:
+            for step in (small, vectors):
+                next(step, None)
+            if small.gi_frame is None and vectors.gi_frame is None:
+                break
+            yield
+        swap.wait_recv()
+
+    def queries():
+        for j in range(KV_HEADS):
+            for g in range(GROUPS):
+                at = HEAD_DIM * (GROUPS * j + g)
+                ra[:, at : at + HEAD_DIM] = turned_back(dq_ref[j, g * T : (g + 1) * T]).astype(BF)[:, :HEAD_DIM]
+        ra[:, D:] = d_attn_ref[...]
+        xs[...] = jnp.zeros_like(xs)
+        for k, (a, b) in enumerate(zip(our_order(me, cut_four(x1_ref)), our_order(me, cut_four(mixture_ref)))):
+            xs[k, :, :240] = a
+            xs[k, :, 256:496] = b
+        share = everyone_steps(
+            sends, (("all", ra, ra_all, None), ("one", [xs.at[k] for k in range(4)], xs_all, xs_relay))
+        )
+        next(share)
+        ra_all[mine] = ra[...]
+        xs_all[mine] = xs[0]
+        d_q = ra[:, :D]
+        d_x1_s[...] = jnp.concatenate(our_order(me, [dot(d_q, wq[k], NT) for k in range(4)]), axis=1)
+        g_two[:, :FF] = g_ref[:, WIDE:]
+        g_two[:, FF + 2 * D :] = jnp.zeros((ROWS, 128), BF)
+        yield
+        next(share)
+        yield
+        together(share)
+        g_two[:, FF : FF + D] = dot(xs_all[:, :256], ra_all[:, :D], TN).astype(BF)
+        g_two[:, FF + D : FF + 2 * D] = dot(xs_all[:, 256:], ra_all[:, D:], TN).astype(BF)
+        yield from sum_steps(me, sends, g_two, mine_two, *two_scr)
+        yield from spread_steps(me, sends, mine_two, two_ref)
+
+    def wide():
+        yield from sum_steps(me, sends, g_ref, mine_one, *one_scr)
+        yield from spread_steps(me, sends, mine_one, one_ref)
+
+    lanes = {"k": keys(), "q": queries(), "w": wide()}
+    for c in ORDER:
+        next(lanes[c], None)
+    together(*(lanes[c] for c in "kwq"))
     sends.finish()
 
 
-def scatter_keys(part, g):
+ORDER = "kwqkqqkwkkk"
+
+
+def back(*args):
     vmem = pl.BlockSpec(memory_space=pltpu.VMEM)
-    width = g.shape[1]
     return pl.pallas_call(
-        scatter_kernel,
-        name="scatter_keys",
+        back_kernel,
+        name="back",
         out_shape=(
-            jax.ShapeDtypeStruct((T, 640), F32),
-            jax.ShapeDtypeStruct((2, RUN, width // 4), BF),
+            jax.ShapeDtypeStruct((ROWS, WIDE), BF),
+            jax.ShapeDtypeStruct((ROWS, REST), BF),
+            jax.ShapeDtypeStruct((ROWS, 640), BF),
+            jax.ShapeDtypeStruct((8, 1024), F32),
+            jax.ShapeDtypeStruct((PAIR, 2 * D), BF),
         ),
-        in_specs=[vmem, vmem],
-        out_specs=(vmem, vmem),
-        scratch_shapes=key_scratch() + sum_scratch(width) + sems(36),
+        in_specs=[vmem] * len(args),
+        out_specs=(vmem,) * 5,
+        scratch_shapes=[
+            pltpu.VMEM((T, 640), F32),
+            pltpu.VMEM((T, 2 * D), BF),
+            pltpu.VMEM((T, 640), BF),
+            pltpu.VMEM((4, T, 512), BF),
+            pltpu.VMEM((4 * T, 2 * D), BF),
+            pltpu.VMEM((4 * T, 640), BF),
+            pltpu.VMEM((4 * T, 512), BF),
+            pltpu.VMEM((T, 512), BF),
+            pltpu.VMEM((ROWS, REST), BF),
+            pltpu.VMEM((ROWS, 640), BF),
+            pltpu.VMEM((T, D), F32),
+            pltpu.VMEM((8, 1024), F32),
+            pltpu.VMEM((6, 8, 1024), F32),
+            pltpu.VMEM((9, 8, 1024), F32),
+            pltpu.VMEM((2, RUN, WIDE // 4), BF),
+            pltpu.VMEM((2, RUN, REST // 4), BF),
+            pltpu.VMEM((3, 64, 640), BF),
+            pltpu.VMEM((3, 16, 640), BF),
+            pltpu.VMEM((16, 640), BF),
+            pltpu.VMEM((64, 640), BF),
+            pltpu.VMEM((16, 640), BF),
+        ]
+        + key_scratch()
+        + sum_scratch(WIDE)
+        + sum_scratch(REST)
+        + sems(140),
         compiler_params=pltpu.CompilerParams(
             collective_id=2, has_side_effects=True, vmem_limit_bytes=VMEM_LIMIT
         ),
-        cost_estimate=pl.CostEstimate(flops=0, bytes_accessed=120_000_000, transcendentals=0),
-    )(part, g)
-
-
-def last_kernel(mine_ref, g_ref, vec_ref, one_ref, two_ref, out_vec_ref, keep, got, own, *scratch):
-    me = here()
-    greet(me, NEAR + SMALL)
-    sends = Sends(me, *scratch[-2:])
-
-    def second():
-        yield from sum_steps(me, sends, g_ref, own, *scratch[:-2])
-        yield from spread_steps(me, sends, own, two_ref)
-
-    together(
-        vector_steps(sends, vec_ref, out_vec_ref, keep, got),
-        second(),
-        spread_steps(me, sends, mine_ref, one_ref),
-    )
-    sends.finish()
-
-
-def reduce_last(mine, g, vec):
-    vmem = pl.BlockSpec(memory_space=pltpu.VMEM)
-    width = g.shape[1]
-    return pl.pallas_call(
-        last_kernel,
-        name="reduce_last",
-        out_shape=(
-            jax.ShapeDtypeStruct((ROWS, mine.shape[2] * 4), BF),
-            jax.ShapeDtypeStruct(g.shape, BF),
-            jax.ShapeDtypeStruct(vec.shape, F32),
-        ),
-        in_specs=[vmem] * 3,
-        out_specs=(vmem,) * 3,
-        scratch_shapes=[
-            pltpu.VMEM((6,) + vec.shape, F32),
-            pltpu.VMEM((9,) + vec.shape, F32),
-            pltpu.VMEM((2, RUN, width // 4), BF),
-        ]
-        + sum_scratch(width)
-        + sems(64),
-        compiler_params=pltpu.CompilerParams(
-            collective_id=3, has_side_effects=True, vmem_limit_bytes=VMEM_LIMIT
-        ),
-        cost_estimate=pl.CostEstimate(flops=0, bytes_accessed=120_000_000, transcendentals=0),
-    )(mine, g, vec)
+        cost_estimate=pl.CostEstimate(flops=2_000_000_000, bytes_accessed=200_000_000, transcendentals=0),
+    )(*args)
 
 
 def shard_of(me, k):
@@ -814,7 +935,7 @@
     gate = gate_s[...]
     inner[...] = (gate * jax.nn.sigmoid(gate) * up_s[...]).astype(BF)
     loaded(3)
-    ffn_out = sum(dot(inner[:, run640(k)], wd[k]) for k in range(4))
+    ffn_out = sum(dot(inner[:, run640(k)], wd[k], NT) for k in range(4))
     route = jax.nn.sigmoid(jnp.sum(hidden * route_w, axis=-1, keepdims=True))
     branch = attn_out + ffn_out
     out_ref[...] = (route * branch).astype(BF)
@@ -829,7 +950,7 @@
     for k in range(4):
         dffn[:, 256 * k : 256 * k + 240] = d_branch[:, 240 * k : 240 * (k + 1)].astype(BF)
     for k in range(4):
-        d_inner = dot(d_ffn, wd[k], NT)
+        d_inner = dot(d_ffn, wd[k])
         gate, up = gate_s[:, run640(k)], up_s[:, run640(k)]
         sg = jax.nn.sigmoid(gate)
         dgu[:, run640(k)] = (d_inner * up * (sg + gate * sg * (1.0 - sg))).astype(BF)
@@ -906,7 +1027,7 @@
             pltpu.VMEM((4, 240, D), BF),
             pltpu.VMEM((4, 240, FF), BF),
             pltpu.VMEM((4, 240, FF), BF),
-            pltpu.VMEM((4, 640, D), BF),
+            pltpu.VMEM((4, D, 640), BF),
             pltpu.VMEM((T, D), F32),
             pltpu.VMEM((T, FF), F32),
             pltpu.VMEM((T, FF), F32),
@@ -934,117 +1055,41 @@
     )(mix, q, prob, kv, h, up_c, vec, *own, *rest)
 
 
-def by_shard(x, width):
-    core, ylo = lax.axis_index("core") == 1, lax.axis_index("ylo") == 1
-    p = [x[..., k * width : (k + 1) * width] for k in range(4)]
-    return ordered(p)
-
-
-def ordered(p):
-    core, ylo = lax.axis_index("core") == 1, lax.axis_index("ylo") == 1
-    p = [jnp.where(core, p[k ^ 1], p[k]) for k in range(4)]
-    return [jnp.where(ylo, p[k ^ 2], p[k]) for k in range(4)]
-
-
-def rotate(values, cosine, sine):
-    a, b = values[..., : HEAD_DIM // 2], values[..., HEAD_DIM // 2 :]
-    return jnp.concatenate([a * cosine - b * sine, b * cosine + a * sine], axis=-1)
-
-
-def norm_back(z, r, gain, dy):
-    dz = r * (gain * dy) - z * (r * r * r) * jnp.mean(gain * dy * z, axis=-1, keepdims=True)
-    return dz, jnp.sum(dy * z * r, axis=0)
-
-
-def everyone(rows, slices):
-    half = T // 2
-    far = jnp.concatenate([rows, slices[2], slices[3]], axis=1)
-    near = permute(jnp.concatenate([rows, slices[1]], axis=1), dcore=1)
-    got = jnp.concatenate([permute(far[:half], dy=1), permute(far[half:], dy=-1)], axis=0)
-    n, m = rows.shape[1], slices[0].shape[1]
-    relay = permute(jnp.concatenate([got[:, :n], got[:, n + m :]], axis=1), dcore=1)
-    every = jnp.concatenate([rows, near[:, :n], got[:, :n], relay[:, :n]], axis=0)
-    some = jnp.concatenate([slices[0], near[:, n:], got[:, n : n + m], relay[:, n:]], axis=0)
-    return every, some
-
-
-def padded(a):
-    return jnp.pad(a, ((0, 0), (0, ROWS - a.shape[1])))
-
-
 def per_device(hidden, chosen, positions, w_query, w_key, w_value, w_output, w_gate, w_up, w_down, gain_attn, gain_ffn, router, d_out):
     tokens, upstream = hidden[0], d_out[0]
-    odd = lax.rem(lax.axis_index("x"), 2) == 1
-    own_w = (w_output, w_gate, w_up, w_down)
+    own_w = (w_output, w_gate, w_up, w_down.T)
     frequency = THETA ** (-jnp.arange(0, HEAD_DIM // 2).astype(F32) * 2.0 / HEAD_DIM)
     vec = jnp.stack([gain_attn, gain_ffn, router]).astype(F32)
     vec = jnp.pad(vec, ((0, 5), (0, 16)))
     (
         mix_heads, prob, q_heads, kv_all, h, up_c, x1, cosine, sine, place, vec_in, wq, wk, wv, *rest_w
     ) = front(
-        tokens, upstream, chosen, positions, jnp.tile(frequency, 4)[None, :], vec,
-        w_query, w_key, w_value, *own_w
+        tokens.T, upstream.T, chosen, positions, jnp.tile(frequency, 4)[None, :], vec,
+        w_query, w_key.T, w_value.T, *own_w
     )
-    gain_a, route_w = vec_in[0, :D], vec_in[2, :D]
-    r1 = lax.rsqrt(jnp.mean(h * h, axis=-1, keepdims=True) + EPS)
-    x1_s = by_shard(x1, 240)
-    cosine, sine = cosine[:, None, : HEAD_DIM // 2], -sine[:, None, : HEAD_DIM // 2]
-
-    def tokens_first(a):
-        return a.reshape(KV_HEADS, GROUPS, T, HEAD_DIM).transpose(2, 0, 1, 3).reshape(T, D)
-
     d_q_heads, d_kv, g_one, d_attn, mixture, d_mid, out_c, d_logit, vec_out = dense(
         mix_heads, q_heads, prob, kv_all, h, up_c, vec_in, own_w, rest_w
     )
-    d_logit = d_logit[:, :1]
-    mix_s = by_shard(mixture, 240)
-    d_own, mine_one = scatter_keys(d_kv, g_one)
-    d_own = d_own.reshape(T, KV_HEADS, 2 * HEAD_DIM)
-    d_q = rotate(tokens_first(d_q_heads[..., :HEAD_DIM]).reshape(T, HEADS, HEAD_DIM), cosine, -sine)
-    d_q = d_q.reshape(T, D).astype(BF)
-    d_k = rotate(d_own[..., :HEAD_DIM], cosine, -sine).reshape(T, 320).astype(BF)
-    d_v = d_own[..., HEAD_DIM:].reshape(T, 320).astype(BF)
-    d_kv_low = jnp.concatenate([d_k, d_v], axis=1)
-    d_x1 = jnp.concatenate(
-        ordered([dot(d_q, wq[k], NT) + dot(d_k, wk[k], NT) + dot(d_v, wv[k], NT) for k in range(4)]), axis=1
+    s_one, s_two, s_three, vector, both = back(
+        d_kv, g_one, d_q_heads, d_attn, mixture, x1, h, d_mid, out_c, d_logit, vec_in, vec_out, cosine, sine, wq, wk, wv
     )
-    d_first, g_gain_a = norm_back(h, r1, gain_a, d_x1)
-    d_h = d_mid + d_first + d_logit * route_w[None, :]
-
-    back = jnp.concatenate([out_c, d_h.astype(BF)], axis=1)
-    other = swap_x(back)
-    both = jnp.concatenate([jnp.where(odd, other, back), jnp.where(odd, back, other)], axis=0)
-    spread = dot(place, both, TN)
-    output = tokens + spread[:, :D]
-    d_tokens = upstream + spread[:, D:]
-
-    rows_2, some_2 = everyone(
-        jnp.concatenate([d_q, d_kv_low, d_attn], axis=1),
-        [jnp.concatenate([x1_s[k], mix_s[k]], axis=1) for k in range(4)],
-    )
-    g_two = jnp.concatenate(
-        [
-            dot(padded(some_2[:, :240]), rows_2[:, :1600], TN).astype(BF),
-            dot(padded(some_2[:, 240:]), rows_2[:, 1600:], TN).astype(BF),
-        ],
-        axis=1,
-    )
-    vector = vec_out.at[0, :D].set(g_gain_a)
-    s_one, s_two, vector = reduce_last(mine_one, g_two, vector)
+    spread = dot(both, place, TN)
+    output = (tokens.T + spread[:D]).T
+    d_tokens = (upstream.T + spread[D:]).T
     shard = lax.axis_index("ylo") * 2 + lax.axis_index("core")
     vector = lax.dynamic_slice_in_dim(vector, shard * 240, 240, axis=1)
-    s_one, s_two = s_one[:240], s_two[:240]
-    g_down = s_one[:, 2 * FF :].reshape(240, 4, 640).transpose(2, 1, 0).reshape(640, D)
+    s_one, s_two, s_three = s_one[:240], s_two[:240], s_three[:240]
+    g_down = jnp.concatenate([s_two[:, 640 * k : 640 * (k + 1)] for k in range(4)], axis=0).astype(F32).T
     return (
         output[None],
         d_tokens[None],
-        s_two[:, :960].astype(F32),
-        s_two[:, 960:1280].astype(F32),
-        s_two[:, 1280:1600].astype(F32),
-        s_two[:, 1600:].astype(F32),
+        s_two[:, FF : FF + D].astype(F32),
+        s_three[:, :320].astype(F32),
+        s_three[:, 320:].astype(F32),
+        s_two[:, FF + D : FF + 2 * D].astype(F32),
         s_one[:, :FF].astype(F32),
-        s_one[:, FF : 2 * FF].astype(F32),
-        g_down.astype(F32),
+        s_one[:, FF:].astype(F32),
+        g_down,
         vector[0],
         vector[1],
         vector[2],

time: 271 us -> 221 us (0.82)
  local copies, waits for them, and re-layouts: 28.8 us -> 8.2 us
  Pallas kernels: 216 us -> 203 us
  matrix products: 5.17 us -> 0.33 us
  starting transfers between devices: 4.3 us -> 0 us
  other arithmetic: 12.6 us -> 9.09 us
    pallas_call x1, Pallas kernels: 78.2 us -> 64.4 us  [front(): pl.pallas_call(front_kernel, name='front', out_shape=(jax.ShapeDtypeStruc...]
    unnamed x61 -> x14, local copies, waits for them, and re-layouts: 10.9 us -> 2.79 us
    convert_element_type x10 -> x0, local copies, waits for them, and re-layouts: 7.14 us -> none  [the longest x2 5.23 us: per_device(): g_down.astype(F32)]
    dot_general x15 -> x1, matrix products: 5.17 us -> 0.33 us  [dot(): return lax.dot_general(a, b, dims, preferred_element_type=F32)]
    ppermute x5 -> x0, starting transfers between devices: 4.3 us -> none  [the longest x4 3.33 us: permute(): lax.ppermute(value, AX, [(flat(p), flat(moved(p, dy, dcore, dz, dx))) for...]
    slice x12 -> x1, local copies, waits for them, and re-layouts: 4.72 us -> 1.36 us  [per_device(): s_two[:, 640 * k:640 * (k + 1)]]
    concatenate x5 -> x0, other arithmetic: 3.07 us -> none  [the longest x1 1.32 us: per_device(): jnp.concatenate([dot(padded(some_2[:, :240]), rows_2[:, :1600], TN).astyp...]
    convert_element_type x6 -> x3, other arithmetic: 7.7 us -> 5.83 us  [the longest x1 2.87 us: per_device(): s_one[:, FF:].astype(F32)]
  transfers between devices with their start and end apart: 5 -> 0, of which waited for: 1 -> 0; matrix products, arithmetic and copies ran while one was open for 6% -> 0% of each run, Pallas kernels for 0% -> 0%
where the time goes in v1:
time: 221 us
  Pallas kernels  203 us (92%)
  other arithmetic  9.09 us (4%)
  local copies, waits for them, and re-layouts  8.2 us (4%)
    pallas_call x1, Pallas kernels, back(): pl.pallas_call(back_kernel, name='back', out_shape=(jax.ShapeDtypeStruct(...  106 us
    pallas_call x1, Pallas kernels, front(): pl.pallas_call(front_kernel, name='front', out_shape=(jax.ShapeDtypeStruc...  64.4 us
    pallas_call x1, Pallas kernels, dense(): pl.pallas_call(dense_kernel, name='dense', out_shape=(jax.ShapeDtypeStruc...  31.9 us

profile of v1, /device:TPU:0, one launch (start us, length us, event | category | flops | bytes accessed | tf_op | source)
XLA Modules:
  0.0 221.1 jit_solution(10446989968598570630)
XLA Ops:
  0.6 0.7 stack.12
  1.3 0.7 stack.13
  2.0 0.7 stack.14
  2.6 0.6 fusion.11.vec_ref
  3.2 0.6 broadcast_in_dim_tile.3.freq_ref
  3.8 64.4 %front.1 = (f32[5,192,128]{2,1,0:T(8,128)}, bf16[5,192,2048]{2,1,0:T(8,128)(2,1)}, bf16[5,192,128]{2,1,0:T(8,128)(2,1)}, bf16[2,4,4,64,640]{4,3,2,1,0:T(8,128)(2...) custom-call(f32[960,128]{1,0:T(8,128)} %bitcast.26, ...), custom_call_target="tpu_custom_call" | custom-call | flops 5000000000 | bytes 90000000 | tf_op jit(solution)/shard_map/front/pallas_call | solution.py:375
  68.3 31.9 %dense.1 = (f32[5,192,128]{2,1,0:T(8,128)}, bf16[2,4,4,64,640]{4,3,2,1,0:T(8,128)(2,1)}, bf16[256,7680]{1,0:T(8,128)(2,1)}, bf16[64,960]{1,0:T(8,128)(2,1)}, bf1...) custom-call(f32[5,192,128]{2,1,0:T(8,128)} %get-tuple-element.44.mix, ...), custom_call_target="tpu_custom_call" | custom-call | flops 20000000000 | bytes 40000000 | tf_op jit(solution)/shard_map/dense/pallas_call | solution.py:1010
  100.2 106.4 %back.1 = (bf16[256,5120]{1,0:T(8,128)(2,1)}, bf16[256,4608]{1,0:T(8,128)(2,1)}, bf16[256,640]{1,0:T(8,128)(2,1)}, f32[8,1024]{1,0:T(8,128)}, bf16[128,1920]{1,0:T(8,128)(2,1)}) custom-call(bf16[2,4,4,64,640]{4,3,2,1,0:T(8,128)(2,1)} %get-tuple-element.55.part_ref, bf16[256,7680]{1,0:T(8,128)(2,1)} %get-tuple-element.56.g_ref, ...), custom_call_target="tpu_custom_call" | custom-call | flops 2000000000 | bytes 200000000 | tf_op jit(solution)/shard_map/back/pallas_call | solution.py:787
  206.7 1.4 fusion.12
  208.0 0.0 copy-start
  208.0 1.6 convert_bitcast_fusion
  209.6 1.0 copy-done
  210.7 2.9 %slice_convert_fusion = (f32[240,2560]{1,0:T(8,128)}, f32[240,2560]{1,0:T(8,128)}) fusion(bf16[256,5120]{1,0:T(8,128)(2,1)S(1)} %copy-done), kind=kLoop, calls=%fused_computation.1 | loop fusion | flops 1228800 | bytes 7372800 | tf_op jit(solution)/shard_map/convert_element_type | solution.py:1091
  213.5 0.0 copy-start.3
  213.5 0.0 copy-start.5
  213.5 0.0 copy-start.1
  213.5 0.0 copy-start.2
  213.5 2.8 %slice_convert_fusion.2 = (f32[240,960]{1,0:T(8,128)}, f32[240,960]{1,0:T(8,128)}) fusion(bf16[256,4608]{1,0:T(8,128)(2,1)} %get-tuple-element.72), kind=kLoop, calls=%fused_computation.7 | loop fusion | flops 460800 | bytes 2764800 | tf_op jit(solution)/shard_map/convert_element_type | solution.py:1089
  216.4 0.0 copy-start.4
  216.4 0.0 copy-done.3
  216.4 0.0 copy-done.5
  216.4 0.3 fusion.14
  216.7 0.0 copy-done.1
  216.7 0.0 copy-done.2
  216.7 1.0 fusion
  217.8 0.0 copy-done.4
  217.8 0.1 slice_convert_fusion.4
  217.9 0.9 copy.26
  218.8 0.9 copy.27
  219.7 1.5 fusion.13
  (2 shorter events, 0.0 us)
Async XLA Ops:
  208.0 2.6 %copy-start = (bf16[256,5120]{1,0:T(8,128)(2,1)S(1)}, bf16[256,5120]{1,0:T(8,128)(2,1)}, u32[]{:S(2)}) copy-start(bf16[256,5120]{1,0:T(8,128)(2,1)} %get-tuple-element.74) | copy-start | bytes 7864324
  213.5 2.9 %copy-start.3 = (bf16[128,1920]{1,0:T(8,128)(2,1)S(1)}, bf16[128,1920]{1,0:T(8,128)(2,1)}, u32[]{:S(2)}) copy-start(bf16[128,1920]{1,0:T(8,128)(2,1)} %get-tuple-element.70) | copy-start | bytes 1474564
  213.5 2.9 %copy-start.5 = (bf16[128,128]{1,0:T(8,128)(2,1)S(1)}, bf16[128,128]{1,0:T(8,128)(2,1)}, u32[]{:S(2)}) copy-start(bf16[128,128]{1,0:T(8,128)(2,1)} %get-tuple-element.71) | copy-start | bytes 98308
  213.5 3.2 %copy-start.1 = (f32[1,128,960]{1,2,0:T(8,128)S(1)}, f32[1,128,960]{1,2,0:T(8,128)}, u32[]{:S(2)}) copy-start(f32[1,128,960]{1,2,0:T(8,128)} %param.14) | copy-start | bytes 1474564
  213.5 3.2 %copy-start.2 = (f32[1,128,960]{1,2,0:T(8,128)S(1)}, f32[1,128,960]{1,2,0:T(8,128)}, u32[]{:S(2)}) copy-start(f32[1,128,960]{1,2,0:T(8,128)} %param.27) | copy-start | bytes 1474564
  216.4 1.4 copy-start.4

commit v2 on v1

--- a/solution.py
+++ b/solution.py
@@ -63,7 +63,7 @@
 
 NEAR = (("x", 1), ("x", -1), ("z", 1), ("z", -1), ("yhi", 1))
 WEIGHT = (("y", 1), ("y", -1), ("core", 1))
-SMALL = (("core", 1), ("ylo", 1), ("x", 2), ("z", 2))
+FAR = (("x", 2), ("z", 2))
 
 
 def greet(me, partners):
@@ -108,6 +108,12 @@
                 steps.remove(step)
 
 
+def run_lanes(lanes, order):
+    for c in order:
+        next(lanes[c], None)
+    together(*lanes.values())
+
+
 def sems(count):
     return [pltpu.SemaphoreType.DMA((count,)), pltpu.SemaphoreType.DMA((count,))]
 
@@ -149,6 +155,8 @@
         rows, slots = own.shape[0], out.shape[0]
         sub = block // 2
         mine = self.color * (rows - block)
+        relay = slots > 1
+        other = slots - 2 if relay else 0
 
         def part(slot, start, count):
             return out.at[slot, pl.ds(pl.multiple_of(start, 16), count)]
@@ -156,23 +164,27 @@
         copies = []
         for step, off in ((1, 0), (-1, sub)):
             src = own.at[pl.ds(pl.multiple_of(mine + off, 16), sub)]
-            copies.append(self.sends.start(src, part(slots - 2, mine + off, sub), "y", step))
+            copies.append(self.sends.start(src, part(other, mine + off, sub), "y", step))
+        if relay:
+            self.near(own, out)
         yield
         for copy in copies:
             copy.wait_recv()
         copies, off = [], 0
         for (axis, step), count in zip((("x", 1), ("x", -1), ("z", 1), ("z", -1)), cuts):
-            ref = part(slots - 2, self.color * block + off, count)
+            ref = part(other, self.color * block + off, count)
             copies.append(self.sends.start(ref, ref, axis, step))
             off += count
-        self.last.append(self.sends.start(part(slots - 2, mine, block), part(slots - 1, mine, block), "core", 1))
+        if relay:
+            self.last.append(self.sends.start(part(other, mine, block), part(slots - 1, mine, block), "core", 1))
         yield
         for copy in copies:
             copy.wait_recv()
         rest = (1 - self.color) * block
-        self.last.append(
-            self.sends.start(part(slots - 2, rest, rows - block), part(slots - 1, rest, rows - block), "core", 1)
-        )
+        if relay:
+            self.last.append(
+                self.sends.start(part(other, rest, rows - block), part(slots - 1, rest, rows - block), "core", 1)
+            )
 
 
 def gather_steps(me, sends, kv_ref, out_ref):
@@ -241,10 +253,11 @@
 def front_kernel(
     hidden_ref, d_out_ref, chosen_ref, pos_ref, freq_ref, vec_ref, wq_ref, wk_ref, wv_ref,
     wo_ref, wg_ref, wu_ref, wd_ref,
-    mix_ref, prob_ref, q_ref, kv_ref, h_ref, up_ref, x1_ref, cos_ref, sin_ref, place_ref, vec_out_ref,
-    wq, wk, wv, wos_ref, wgs_ref, wus_ref, wds_ref,
+    mix_ref, prob_out, q_ref, kv_out, h_ref, up_ref, x1_ref, cos_ref, sin_ref, place_ref, vec_out_ref,
+    wq_out, wk_out, wv_out, wos_ref, wgs_ref, wus_ref, wds_ref,
     compact_h, compact_d, compact_p, got_h, got_d, got_p, vecs, q_pre, kv_own,
-    load_sems, send_sems, recv_sems,
+    prob_ref, kv_ref, wq, wk, wv,
+    load_sems, store_sems, send_sems, recv_sems,
 ):
     me = here()
     yhi, z, x = me[2:]
@@ -252,121 +265,129 @@
     for k, (own, to) in enumerate(((wq_ref, wq), (wk_ref, wk), (wv_ref, wv))):
         loads.append(pltpu.make_async_copy(own, to.at[0], load_sems.at[k]))
         loads[-1].start()
-    greet(me, NEAR + WEIGHT + (("pair", 1),))
+    greet(me, NEAR + WEIGHT)
     sends = Sends(me, send_sems, recv_sems)
     early, query, late = Shards(sends), Shards(sends), Shards(sends)
-    vec_far = sends.start(vec_ref, vecs.at[2], "y", 1)
-    early.far(wk_ref, wk, 160)
-    early.far(wv_ref, wv, 160)
-    vec_near = sends.start(vec_ref, vecs.at[1], "core", 1)
-    early.near(wk_ref, wk)
-    early.near(wv_ref, wv)
-    query.far(wq_ref, wq, 128)
-    query.near(wq_ref, wq)
-    vecs[0] = vec_ref[...]
-
     odd = lax.rem(x, 2)
-    flag = jnp.where(chosen_ref[...] > 0, 1.0, 0.0)
-    token = lax.broadcasted_iota(jnp.int32, (PAIR, PAIR), 0)
-    lane = lax.broadcasted_iota(jnp.int32, (PAIR, PAIR), 1)
-    upto = jnp.where(token <= lane, 1.0, 0.0).astype(BF)
-    count = dot(jnp.broadcast_to(flag, (16, PAIR)).astype(BF), upto)[0:1]
-    total = jnp.sum(flag, axis=1, keepdims=True)
-    rank = count - 1.0 + jnp.where(odd == 1, PAIR - total, 0.0)
-    place = jnp.where(token.astype(F32) == rank, flag, 0.0)
-    place_low = place.astype(BF)
-    place_ref[...] = place_low
-    compact_p[...] = jnp.broadcast_to(
-        jnp.sum(place * pos_ref[...].astype(F32), axis=1, keepdims=True), (PAIR, PAIR)
-    )
-    compact_h[...] = dot(place_low, hidden_ref[...].astype(BF), NT).astype(BF)
-    compact_d[...] = dot(place_low, d_out_ref[...].astype(BF), NT).astype(BF)
     give = pl.ds(pl.multiple_of((1 - odd) * T, T), T)
     keep = pl.ds(pl.multiple_of(odd * T, T), T)
-    swaps = [
-        sends.start(c.at[give], g, "pair", 1)
-        for c, g in ((compact_h, got_h), (compact_p, got_p), (compact_d, got_d))
-    ]
-    vec_far.wait_recv()
-    vec_last = sends.start(vecs.at[2], vecs.at[3], "core", 1)
-    swaps[0].wait_recv()
-    h = plus(compact_h[keep], got_h[...])
-    h_ref[...] = h
-    swaps[1].wait_recv()
-    angle = (compact_p[keep] + got_p[...]) * freq_ref[...]
-    turn = lax.broadcasted_iota(jnp.int32, (T, PAIR), 1)
-    cosine = jnp.where(turn < HEAD_DIM, jnp.cos(angle), 1.0)
-    sine = jnp.sin(angle)
-    sine = jnp.where(turn < HEAD_DIM // 2, -sine, jnp.where(turn < HEAD_DIM, sine, 0.0))
-    cos_ref[...], sin_ref[...] = cosine, sine
-    vec_near.wait_recv()
-    vec_last.wait_recv()
-    vec_out_ref[...] = jnp.zeros_like(vec_out_ref)
-    for k, v in enumerate(our_order(me, [vecs[k, :, :240] for k in range(4)])):
-        vec_out_ref[:, 240 * k : 240 * (k + 1)] = v
-    r1 = lax.rsqrt(jnp.mean(h * h, axis=-1, keepdims=True) + EPS)
-    x1_ref[...] = (h * r1 * vec_out_ref[0:1, :D]).astype(BF)
-    x1_k = our_order(me, cut_four(x1_ref))
-    for copy in loads:
+    limit = ((yhi * 16 + z * 4 + x) // 2 + 1) * PAIR
+    stores = []
+
+    def store(a, b):
+        stores.append(pltpu.make_async_copy(a, b, store_sems.at[len(stores)]))
+        stores[-1].start()
+
+    def main():
+        vec_far = sends.start(vec_ref, vecs.at[2], "y", 1)
+        early.far(wk_ref, wk, 160)
+        early.far(wv_ref, wv, 160)
+        vec_near = sends.start(vec_ref, vecs.at[1], "core", 1)
+        early.near(wk_ref, wk)
+        early.near(wv_ref, wv)
+        query.far(wq_ref, wq, 128)
+        query.near(wq_ref, wq)
+        vecs[0] = vec_ref[...]
+        flag = jnp.where(chosen_ref[...] > 0, 1.0, 0.0)
+        token = lax.broadcasted_iota(jnp.int32, (PAIR, PAIR), 0)
+        lane = lax.broadcasted_iota(jnp.int32, (PAIR, PAIR), 1)
+        upto = jnp.where(token <= lane, 1.0, 0.0).astype(BF)
+        count = dot(jnp.broadcast_to(flag, (16, PAIR)).astype(BF), upto)[0:1]
+        total = jnp.sum(flag, axis=1, keepdims=True)
+        rank = count - 1.0 + jnp.where(odd == 1, PAIR - total, 0.0)
+        place = jnp.where(token.astype(F32) == rank, flag, 0.0)
+        place_low = place.astype(BF)
+        place_ref[...] = place_low
+        compact_p[...] = jnp.broadcast_to(
+            jnp.sum(place * pos_ref[...].astype(F32), axis=1, keepdims=True), (PAIR, PAIR)
+        )
+        compact_h[...] = dot(place_low, hidden_ref[...].astype(BF), NT).astype(BF)
+        swaps = [sends.start(c.at[give], g, "pair", 1) for c, g in ((compact_h, got_h), (compact_p, got_p))]
+        yield
+        compact_d[...] = dot(place_low, d_out_ref[...].astype(BF), NT).astype(BF)
+        vec_far.wait_recv()
+        vec_last = sends.start(vecs.at[2], vecs.at[3], "core", 1)
+        early.relay()
+        yield
+        swaps[0].wait_recv()
+        h = plus(compact_h[keep], got_h[...])
+        h_ref[...] = h
+        swaps.append(sends.start(compact_d.at[give], got_d, "pair", 1))
+        swaps[1].wait_recv()
+        angle = (compact_p[keep] + got_p[...]) * freq_ref[...]
+        turn = lax.broadcasted_iota(jnp.int32, (T, PAIR), 1)
+        cosine = jnp.where(turn < HEAD_DIM, jnp.cos(angle), 1.0)
+        sine = jnp.sin(angle)
+        sine = jnp.where(turn < HEAD_DIM // 2, -sine, jnp.where(turn < HEAD_DIM, sine, 0.0))
+        cos_ref[...], sin_ref[...] = cosine, sine
+        vec_near.wait_recv()
+        vec_last.wait_recv()
+        vec_out_ref[...] = jnp.zeros_like(vec_out_ref)
+        for k, v in enumerate(our_order(me, [vecs[k, :, :240] for k in range(4)])):
+            vec_out_ref[:, 240 * k : 240 * (k + 1)] = v
+        r1 = lax.rsqrt(jnp.mean(h * h, axis=-1, keepdims=True) + EPS)
+        x1_ref[...] = (h * r1 * vec_out_ref[0:1, :D]).astype(BF)
+        x1_k = our_order(me, cut_four(x1_ref))
+        for copy in loads:
+            copy.wait()
+        early.finish()
+        k_pre = sum(dot(x1_k[k], wk[k], NT) for k in range(4))
+        v_pre = sum(dot(x1_k[k], wv[k], NT) for k in range(4))
+        for j in range(KV_HEADS):
+            run = slice(HEAD_DIM * j, HEAD_DIM * (j + 1))
+            tile = jnp.concatenate([k_pre[:, run], v_pre[:, run]], axis=1)
+            kv_own[:, 128 * j : 128 * (j + 1)] = (tile * cosine + swapped(tile) * sine).astype(BF)
+        gather = gather_steps(me, sends, kv_own, kv_ref)
+        next(gather)
+        yield
+        next(gather)
+        yield
+        query.relay()
+        yield
+        query.finish()
+        swaps[2].wait_recv()
+        up_ref[...] = plus(compact_d[keep], got_d[...])
+        q_pre[...] = sum(dot(x1_k[k], wq[k]) for k in range(4))
+        zero = jnp.zeros((T, HEAD_DIM), F32)
+        for j in range(KV_HEADS):
+            for g in range(GROUPS):
+                at = HEAD_DIM * (GROUPS * j + g)
+                tile = jnp.concatenate([q_pre[:, at : at + HEAD_DIM], zero], axis=1)
+                q_ref[j, g * T : (g + 1) * T] = (tile * cosine + swapped(tile) * sine).astype(BF)
+        yield
+        yield from gather
+        for a, b in ((kv_ref, kv_out), (wq, wq_out), (wk, wk_out), (wv, wv_out)):
+            store(a, b)
+        for j in range(KV_HEADS):
+            tile = kv_ref[:, :, :, :, 128 * j : 128 * (j + 1)].reshape(KEYS, 128)
+            scores = dot(q_ref[j], tile, NT) * SCALE
+            column = lax.broadcasted_iota(jnp.int32, scores.shape, 1)
+            scores = jnp.where(column < limit, scores, -1e30)
+            exponent = jnp.exp(scores - jnp.max(scores, axis=-1, keepdims=True))
+            prob = (exponent * (1.0 / jnp.sum(exponent, axis=-1, keepdims=True))).astype(BF)
+            prob_ref[j] = prob
+            store(prob_ref.at[j], prob_out.at[j])
+            mix_ref[j] = dot(prob, tile)
+            yield
+
+    small, large = (128, (32, 32, 32, 16)), (480, (128, 128, 112, 112))
+    lanes = {
+        "m": main(),
+        "o": late.half(wo_ref, wos_ref, *small),
+        "t": late.half(wg_ref, wgs_ref, *small),
+        "u": late.half(wu_ref, wus_ref, *small),
+        "d": late.half(wd_ref, wds_ref, *large),
+    }
+    run_lanes(lanes, FRONT_ORDER)
+    late.finish()
+    for copy in stores:
         copy.wait()
-    early.finish()
-    k_pre = sum(dot(x1_k[k], wk[k], NT) for k in range(4))
-    v_pre = sum(dot(x1_k[k], wv[k], NT) for k in range(4))
-    for j in range(KV_HEADS):
-        run = slice(HEAD_DIM * j, HEAD_DIM * (j + 1))
-        tile = jnp.concatenate([k_pre[:, run], v_pre[:, run]], axis=1)
-        kv_own[:, 128 * j : 128 * (j + 1)] = (tile * cosine + swapped(tile) * sine).astype(BF)
-    gather = gather_steps(me, sends, kv_own, kv_ref)
-    next(gather)
-    query.finish()
-    swaps[2].wait_recv()
-    up_ref[...] = plus(compact_d[keep], got_d[...])
-    q_pre[...] = sum(dot(x1_k[k], wq[k]) for k in range(4))
-    zero = jnp.zeros((T, HEAD_DIM), F32)
-    for j in range(KV_HEADS):
-        for g in range(GROUPS):
-            at = HEAD_DIM * (GROUPS * j + g)
-            tile = jnp.concatenate([q_pre[:, at : at + HEAD_DIM], zero], axis=1)
-            q_ref[j, g * T : (g + 1) * T] = (tile * cosine + swapped(tile) * sine).astype(BF)
-    next(gather)
-    small, large = (128, (32, 32, 32, 16)), (480, (128, 128, 112, 112))
-    out_w = late.half(wo_ref, wos_ref, *small)
-    gate_w = late.half(wg_ref, wgs_ref, *small)
-    up_w = late.half(wu_ref, wus_ref, *small)
-    down_w = late.half(wd_ref, wds_ref, *large)
-    for w in (out_w, gate_w, up_w, down_w):
-        next(w)
-    for own, out in ((wo_ref, wos_ref), (wg_ref, wgs_ref), (wu_ref, wus_ref), (wd_ref, wds_ref)):
-        late.near(own, out)
-    next(gather)
-    next(gather)
-    next(out_w)
-    next(gather)
-    next(gather)
-    next(gate_w)
-    together(gather)
-    next(up_w)
-    together(out_w)
-    together(gate_w)
-    limit = ((yhi * 16 + z * 4 + x) // 2 + 1) * PAIR
-
-    @pl.loop(0, KV_HEADS)
-    def _(j):
-        c = pl.ds(pl.multiple_of(j * 128, 128), 128)
-        tile = kv_ref[:, :, :, :, c].reshape(KEYS, 128)
-        scores = dot(q_ref[j], tile, NT) * SCALE
-        column = lax.broadcasted_iota(jnp.int32, scores.shape, 1)
-        scores = jnp.where(column < limit, scores, -1e30)
-        exponent = jnp.exp(scores - jnp.max(scores, axis=-1, keepdims=True))
-        prob = (exponent * (1.0 / jnp.sum(exponent, axis=-1, keepdims=True))).astype(BF)
-        prob_ref[j] = prob
-        mix_ref[j] = dot(prob, tile)
-
-    next(down_w)
-    together(up_w)
-    together(down_w)
-    late.finish()
     sends.finish()
+
+
+FRONT_ORDER = (
+    "mmmommtmmoumdmommmtummdmmtumdm"
+)
 
 
 def front(hidden, d_out, chosen, pos, freq, vec, w_query, w_key, w_value, *later):
@@ -391,9 +412,10 @@
             jax.ShapeDtypeStruct((4, 320, 240), BF),
             jax.ShapeDtypeStruct((4, 320, 240), BF),
         )
-        + tuple(jax.ShapeDtypeStruct((3,) + w.shape, BF) for w in later),
+        + tuple(jax.ShapeDtypeStruct((3,) + w.shape, BF) for w in later[:3])
+        + (jax.ShapeDtypeStruct((1,) + later[3].shape, BF),),
         in_specs=[vmem] * 6 + [hbm] * 7,
-        out_specs=(vmem,) * 14 + (hbm,) * 4,
+        out_specs=(vmem, hbm, vmem, hbm) + (vmem,) * 7 + (hbm,) * 7,
         scratch_shapes=[
             pltpu.VMEM((PAIR, D), BF),
             pltpu.VMEM((PAIR, D), BF),
@@ -404,7 +426,13 @@
             pltpu.VMEM((4, 8, 256), F32),
             pltpu.VMEM((T, D), F32),
             pltpu.VMEM((T, 640), BF),
+            pltpu.VMEM((KV_HEADS, rows, KEYS), BF),
+            pltpu.VMEM((2, 4, 4, T, 640), BF),
+            pltpu.VMEM((4, 240, 960), BF),
+            pltpu.VMEM((4, 320, 240), BF),
+            pltpu.VMEM((4, 320, 240), BF),
             pltpu.SemaphoreType.DMA((3,)),
+            pltpu.SemaphoreType.DMA((9,)),
         ]
         + sems(90),
         compiler_params=pltpu.CompilerParams(
@@ -429,8 +457,8 @@
         near[s, 1] = sends.start(line(axis, 2, row, quarter), low.at[s, 0], axis, 1)
         near[s, -1] = sends.start(line(axis, 2, row + quarter, quarter), low.at[s, 1], axis, -1)
     whole = {}
-    yield
     for s, (axis, _, row) in enumerate(streams):
+        yield
         for d, step in enumerate((1, -1)):
             near[s, step].wait_recv()
             lo, hi = (0, quarter) if step == 1 else (quarter, 0)
@@ -439,9 +467,9 @@
             ).astype(BF)
             out_b[s, d, :, :, pl.ds(hi, quarter)] = line(axis, step, row + hi, quarter)[...]
             whole[s, step] = sends.start(out_b.at[s, d], full.at[s, d], axis, step)
-    yield
     near = {}
     for s, (axis, other, row) in enumerate(streams):
+        yield
         for step in (1, -1):
             whole[s, step].wait_recv()
         sums[s] = plus(line(axis, 0, row, half)[...], full[s, 0], full[s, 1]).astype(BF)
@@ -450,8 +478,8 @@
         near[s, -1] = sends.start(
             sums.at[s, :, far, pl.ds(quarter, quarter)], nlow.at[s, 1], other, -1
         )
-    yield
     for s, (axis, other, row) in enumerate(streams):
+        yield
         at = z if other == "z" else x
         for d, step in enumerate((1, -1)):
             near[s, step].wait_recv()
@@ -462,9 +490,9 @@
             ).astype(BF)
             nout[s, d, :, pl.ds(hi, quarter)] = sums[s, :, to, pl.ds(hi, quarter)]
             whole[s, step] = sends.start(nout.at[s, d], nfull.at[s, d], other, step)
-    yield
     swap = {}
     for s, (axis, other, row) in enumerate(streams):
+        yield
         at = z if other == "z" else x
         for step in (1, -1):
             whole[s, step].wait_recv()
@@ -493,9 +521,7 @@
 
 ROWS = 256
 HALF = ROWS // 2
-STREAMS = (("x", "z", 0), ("z", "x", HALF))
-RUN = HALF // 4
-CUT = HALF // 2
+STREAMS = (("x", "z"), ("z", "x"))
 
 
 def spots(me):
@@ -510,116 +536,168 @@
     return pl.ds(pl.multiple_of(around(me, axis, step) * big, 128), big)
 
 
-def sum_steps(me, sends, g_ref, mine, low, out_b, full, sums, nlow, nout, nfull, y_in):
-    big = mine.shape[-1]
+def halves(big):
+    cut = (big // 2 + 127) // 128 * 128
+    return (0, cut), (cut, big - cut)
+
+
+def sum_steps(me, sends, g_ref, mine, swap_y, low, out_b, full, sums, nlow, nout, nfull, y_in):
+    run, big = mine.shape[-2:]
+    h = 4 * run
+    cut = h // 2
     near, whole = {}, {}
 
     def parts(step):
-        return (0, CUT) if step == 1 else (CUT, 0)
-
-    for s, (axis, _, row) in enumerate(STREAMS):
+        return (0, cut) if step == 1 else (cut, 0)
+
+    for s, (axis, _) in enumerate(STREAMS):
         c = columns(me, axis, 2, big)
         for step in (1, -1):
-            r = pl.ds(row + parts(step)[0], CUT)
+            r = pl.ds(s * h + parts(step)[0], cut)
             near[s, step] = sends.start(g_ref.at[r, c], low.at[r], axis, step)
-    yield
-    for s, (axis, _, row) in enumerate(STREAMS):
+    for s, (axis, _) in enumerate(STREAMS):
+        yield
         for d, step in enumerate((1, -1)):
             near[s, step].wait_recv()
-            add, keep = (pl.ds(row + p, CUT) for p in parts(step))
+            add, keep = (pl.ds(s * h + p, cut) for p in parts(step))
             c = columns(me, axis, step, big)
             out_b[d, add] = plus(g_ref[add, c], low[add]).astype(BF)
             out_b[d, keep] = g_ref[keep, c]
-            r = pl.ds(row, HALF)
+            r = pl.ds(s * h, h)
             whole[s, step] = sends.start(out_b.at[d, r], full.at[d, r], axis, step)
-    yield
-    half = RUN // 2
-
-    def run(row, other, step, off, count):
-        return pl.ds(pl.multiple_of(row + around(me, other, step) * RUN + off, 16), count)
-
-    for s, (axis, other, row) in enumerate(STREAMS):
+
+    def rows(s, other, step):
+        return pl.ds(pl.multiple_of(s * h + around(me, other, step) * run, 16), run)
+
+    for s, (axis, other) in enumerate(STREAMS):
+        yield
         for step in (1, -1):
             whole[s, step].wait_recv()
-        r = pl.ds(row, HALF)
+        r = pl.ds(s * h, h)
         sums[r] = plus(g_ref[r, columns(me, axis, 0, big)], full[0, r], full[1, r]).astype(BF)
         for d, step in enumerate((1, -1)):
-            near[s, step] = sends.start(
-                sums.at[run(row, other, 2, d * half, half)], nlow.at[s, d], other, step
-            )
-    yield
-    for s, (axis, other, row) in enumerate(STREAMS):
+            c = pl.ds(*halves(big)[d])
+            near[s, step] = sends.start(sums.at[rows(s, other, 2), c], nlow.at[s, :, c], other, step)
+    for s, (axis, other) in enumerate(STREAMS):
+        yield
         for d, step in enumerate((1, -1)):
             near[s, step].wait_recv()
-            add, keep = (0, half) if step == 1 else (half, 0)
-            nout[s, d, pl.ds(add, half)] = plus(
-                sums[run(row, other, step, add, half)], nlow[s, d]
-            ).astype(BF)
-            nout[s, d, pl.ds(keep, half)] = sums[run(row, other, step, keep, half)]
+            add, keep = pl.ds(*halves(big)[d]), pl.ds(*halves(big)[1 - d])
+            r = rows(s, other, step)
+            nout[s, d, :, add] = plus(sums[r, add], nlow[s, :, add]).astype(BF)
+            nout[s, d, :, keep] = sums[r, keep]
             whole[s, step] = sends.start(nout.at[s, d], nfull.at[s, d], other, step)
-    yield
     swap = {}
-    for s, (axis, other, row) in enumerate(STREAMS):
+    for s, (axis, other) in enumerate(STREAMS):
+        yield
         for step in (1, -1):
             whole[s, step].wait_recv()
-        y_in[0, s] = plus(sums[run(row, other, 0, 0, RUN)], nfull[s, 0], nfull[s, 1]).astype(BF)
-        swap[s] = sends.start(y_in.at[0, s], y_in.at[1, s], "yhi", 1)
-    yield
-    for s in range(2):
-        swap[s].wait_recv()
-        mine[s] = plus(y_in[0, s], y_in[1, s]).astype(BF)
-
-
-def sum_scratch(width):
-    big = width // 4
+        total = plus(sums[rows(s, other, 0)], nfull[s, 0], nfull[s, 1]).astype(BF)
+        if swap_y:
+            y_in[0, s] = total
+            swap[s] = sends.start(y_in.at[0, s], y_in.at[1, s], "yhi", 1)
+        else:
+            mine[s] = total
+    if swap_y:
+        for s in range(2):
+            yield
+            swap[s].wait_recv()
+            mine[s] = plus(y_in[0, s], y_in[1, s]).astype(BF)
+
+
+def sum_scratch(width, h):
+    big, run = width // 4, h // 4
     return [
-        pltpu.VMEM((ROWS, big), BF),
-        pltpu.VMEM((2, ROWS, big), BF),
-        pltpu.VMEM((2, ROWS, big), BF),
-        pltpu.VMEM((ROWS, big), BF),
-        pltpu.VMEM((2, 2, RUN // 2, big), BF),
-        pltpu.VMEM((2, 2, RUN, big), BF),
-        pltpu.VMEM((2, 2, RUN, big), BF),
-        pltpu.VMEM((2, 2, RUN, big), BF),
+        pltpu.VMEM((2 * h, big), BF),
+        pltpu.VMEM((2, 2 * h, big), BF),
+        pltpu.VMEM((2, 2 * h, big), BF),
+        pltpu.VMEM((2 * h, big), BF),
+        pltpu.VMEM((2, run, big), BF),
+        pltpu.VMEM((2, 2, run, big), BF),
+        pltpu.VMEM((2, 2, run, big), BF),
+        pltpu.VMEM((2, 2, run, big), BF),
     ]
 
 
-def spread_steps(me, sends, mine, out_ref):
-    big = mine.shape[-1]
-    half = RUN // 2
-    near, whole = {}, {}
-
-    def run(row, other, step, off, count):
-        return pl.ds(pl.multiple_of(row + around(me, other, step) * RUN + off, 16), count)
-
-    for s, (axis, other, row) in enumerate(STREAMS):
-        ref = out_ref.at[run(row, other, 0, 0, RUN), columns(me, axis, 0, big)]
-        ref[...] = mine[s]
+def spread_steps(me, sends, mine, out_ref, store_sems, to_y):
+    run, big = mine.shape[-2:]
+    h = 4 * run
+    cut = h // 2
+    near, whole, stored, last, over = {}, {}, [], {}, []
+
+    def base(s):
+        return s * HALF + (me[2] * h if to_y else 0)
+
+    def rows(s, off, count):
+        return pl.ds(pl.multiple_of(base(s) + off, 16), count)
+
+    def block(s, axis, step, off, count):
+        return out_ref.at[rows(s, off, count), columns(me, axis, step, big)]
+
+    def on(ref):
+        if to_y:
+            over.append(sends.start(ref, ref, "yhi", 1))
+
+    for s, (axis, other) in enumerate(STREAMS):
+        ref = block(s, axis, 0, around(me, other, 0) * run, run)
         for step in (1, -1):
-            near[s, step] = sends.start(ref, ref, other, step)
-    yield
-    for s, (axis, other, row) in enumerate(STREAMS):
+            near[s, step] = sends.start(mine.at[s], ref, other, step)
+        stored.append(pltpu.make_async_copy(mine.at[s], ref, store_sems.at[s]))
+        stored[-1].start()
+
+    def narrow(s, axis, other, step, d):
+        c0, n = halves(big)[d]
+        c = pl.ds(pl.multiple_of(around(me, axis, 0) * big + c0, 128), n)
+        return out_ref.at[rows(s, around(me, other, step) * run, run), c]
+
+    for s, (axis, other) in enumerate(STREAMS):
+        yield
         for d, step in enumerate((1, -1)):
             near[s, step].wait_recv()
-            ref = out_ref.at[run(row, other, -step, d * half, half), columns(me, axis, 0, big)]
+            ref = narrow(s, axis, other, -step, d)
             whole[s, step] = sends.start(ref, ref, other, step)
-    yield
-    for s, (axis, other, row) in enumerate(STREAMS):
+    for s, (axis, other) in enumerate(STREAMS):
+        yield
         for step in (1, -1):
             whole[s, step].wait_recv()
-        ref = out_ref.at[pl.ds(row, HALF), columns(me, axis, 0, big)]
+        stored[s].wait()
+        ref = block(s, axis, 0, 0, h)
         for step in (1, -1):
             near[s, step] = sends.start(ref, ref, axis, step)
-    yield
-    last = []
-    for s, (axis, other, row) in enumerate(STREAMS):
+        on(ref)
+    for s, (axis, other) in enumerate(STREAMS):
+        yield
         for d, step in enumerate((1, -1)):
             near[s, step].wait_recv()
-            ref = out_ref.at[pl.ds(row + d * CUT, CUT), columns(me, axis, -step, big)]
-            last.append(sends.start(ref, ref, axis, step))
+            ref = block(s, axis, -step, d * cut, cut)
+            last[s, step] = sends.start(ref, ref, axis, step)
+            on(block(s, axis, -step, 0, h))
+    for s, (axis, other) in enumerate(STREAMS):
+        yield
+        for step in (1, -1):
+            last[s, step].wait_recv()
+        on(block(s, axis, 2, 0, h))
+    if to_y:
+        yield
+        for copy in over:
+            copy.wait_recv()
+
+
+def halved_steps(me, sends, g_ref, mine, kept, got, out_ref, store_sems, *scratch):
+    h = HALF // 2
+    yh = me[2]
+    copies = []
+    for s in range(2):
+        give = pl.ds(pl.multiple_of(s * HALF + (1 - yh) * h, 16), h)
+        copies.append(sends.start(g_ref.at[give], got.at[pl.ds(s * h, h)], "yhi", 1))
+    for s in range(2):
+        yield
+        copies[s].wait_recv()
+        r = pl.ds(s * h, h)
+        kept[r] = plus(g_ref[pl.ds(pl.multiple_of(s * HALF + yh * h, 16), h)], got[r]).astype(BF)
     yield
-    for copy in last:
-        copy.wait_recv()
+    yield from sum_steps(me, sends, kept, mine, False, *scratch)
+    yield from spread_steps(me, sends, mine, out_ref, store_sems, True)
 
 
 def vector_steps(sends, vec_ref, out_ref, keep, got):
@@ -678,20 +756,37 @@
 
 
 KEY_N, SUM_N = 9, 8
-WIDE, REST = 2 * FF, 4608
+WIDE, REST = FF, 4608
 
 
 def back_kernel(
-    part_ref, g_ref, dq_ref, d_attn_ref, mixture_ref, x1_ref, h_ref, d_mid_ref, out_ref, logit_ref, vec_ref, vec_part_ref,
-    cos_ref, sin_ref, wq, wk, wv,
-    one_ref, two_ref, three_ref, vec_out_ref, both_ref,
+    part_ref, g_in, dq_ref, d_attn_ref, mixture_ref, x1_ref, h_ref, d_mid_ref, out_ref, logit_ref, vec_ref, vec_part_ref,
+    cos_ref, sin_ref, wq_in, wk_in, wv_in,
+    gate_ref, up_ref, two_ref, three_ref, vec_out_ref, both_ref,
     own, ra, rb, xs, ra_all, rb_all, xs_all, xs_relay, g_two, g_three, d_x1_s, vec_all, keep_v, got_v,
-    mine_one, mine_two, got_x, got_z, got_y, sum_z, sum_y,
+    mine_gate, mine_up, mine_two, got_x, got_z, got_y, sum_z, sum_y,
+    g_gate, g_up, kept, got_gate, wq, wk, wv, load_sems, store_sems,
     *scratch,
 ):
     me = here()
-    key_scr, one_scr, two_scr = scratch[:KEY_N], scratch[KEY_N : KEY_N + SUM_N], scratch[KEY_N + SUM_N : -2]
-    greet(me, NEAR + WEIGHT + SMALL + (("pair", 1),))
+    key_scr, rest = scratch[:KEY_N], scratch[KEY_N:-2]
+    gate_scr, up_scr, two_scr = rest[:SUM_N], rest[SUM_N : 2 * SUM_N], rest[2 * SUM_N :]
+    loads = [
+        pltpu.make_async_copy(a, b, load_sems.at[k])
+        for k, (a, b) in enumerate(
+            (
+                (g_in.at[:, pl.ds(0, WIDE)], g_gate),
+                (g_in.at[:, pl.ds(WIDE, WIDE)], g_up),
+                (g_in.at[:, pl.ds(2 * WIDE, FF)], g_two.at[:, pl.ds(0, FF)]),
+                (wq_in, wq),
+                (wk_in, wk),
+                (wv_in, wv),
+            )
+        )
+    ]
+    for copy in loads:
+        copy.start()
+    greet(me, NEAR + WEIGHT + FAR)
     sends = Sends(me, *scratch[-2:])
     odd = lax.rem(me[4], 2)
     keep = pl.ds(pl.multiple_of(odd * T, T), T)
@@ -756,8 +851,9 @@
         ra_all[mine] = ra[...]
         xs_all[mine] = xs[0]
         d_q = ra[:, :D]
+        for copy in loads[2:]:
+            copy.wait()
         d_x1_s[...] = jnp.concatenate(our_order(me, [dot(d_q, wq[k], NT) for k in range(4)]), axis=1)
-        g_two[:, :FF] = g_ref[:, WIDE:]
         g_two[:, FF + 2 * D :] = jnp.zeros((ROWS, 128), BF)
         yield
         next(share)
@@ -765,37 +861,45 @@
         together(share)
         g_two[:, FF : FF + D] = dot(xs_all[:, :256], ra_all[:, :D], TN).astype(BF)
         g_two[:, FF + D : FF + 2 * D] = dot(xs_all[:, 256:], ra_all[:, D:], TN).astype(BF)
-        yield from sum_steps(me, sends, g_two, mine_two, *two_scr)
-        yield from spread_steps(me, sends, mine_two, two_ref)
-
-    def wide():
-        yield from sum_steps(me, sends, g_ref, mine_one, *one_scr)
-        yield from spread_steps(me, sends, mine_one, one_ref)
-
-    lanes = {"k": keys(), "q": queries(), "w": wide()}
-    for c in ORDER:
-        next(lanes[c], None)
-    together(*(lanes[c] for c in "kwq"))
+        yield from sum_steps(me, sends, g_two, mine_two, True, *two_scr)
+        yield from spread_steps(me, sends, mine_two, two_ref, store_sems.at[pl.ds(4, 2)], False)
+
+    def gate():
+        loads[0].wait()
+        yield from halved_steps(
+            me, sends, g_gate, mine_gate, kept, got_gate, gate_ref, store_sems.at[pl.ds(0, 2)], *gate_scr
+        )
+
+    def up():
+        loads[1].wait()
+        yield from sum_steps(me, sends, g_up, mine_up, True, *up_scr)
+        yield from spread_steps(me, sends, mine_up, up_ref, store_sems.at[pl.ds(2, 2)], False)
+
+    run_lanes({"k": keys(), "g": gate(), "u": up(), "q": queries()}, ORDER)
     sends.finish()
 
 
-ORDER = "kwqkqqkwkkk"
+ORDER = (
+    "kuqgkkuuqgkkqkkgguuqkkguugqukqgkguqkuguq"
+    "gquqgukguqugqqgkgqqgukgqqkgguugqquqqgk"
+)
 
 
 def back(*args):
-    vmem = pl.BlockSpec(memory_space=pltpu.VMEM)
+    vmem, hbm = pl.BlockSpec(memory_space=pltpu.VMEM), pl.BlockSpec(memory_space=pl.ANY)
     return pl.pallas_call(
         back_kernel,
         name="back",
         out_shape=(
+            jax.ShapeDtypeStruct((ROWS, WIDE), BF),
             jax.ShapeDtypeStruct((ROWS, WIDE), BF),
             jax.ShapeDtypeStruct((ROWS, REST), BF),
             jax.ShapeDtypeStruct((ROWS, 640), BF),
             jax.ShapeDtypeStruct((8, 1024), F32),
             jax.ShapeDtypeStruct((PAIR, 2 * D), BF),
         ),
-        in_specs=[vmem] * len(args),
-        out_specs=(vmem,) * 5,
+        in_specs=[vmem, hbm] + [vmem] * (len(args) - 5) + [hbm] * 3,
+        out_specs=(hbm,) * 3 + (vmem,) * 3,
         scratch_shapes=[
             pltpu.VMEM((T, 640), F32),
             pltpu.VMEM((T, 2 * D), BF),
@@ -811,22 +915,111 @@
             pltpu.VMEM((8, 1024), F32),
             pltpu.VMEM((6, 8, 1024), F32),
             pltpu.VMEM((9, 8, 1024), F32),
-            pltpu.VMEM((2, RUN, WIDE // 4), BF),
-            pltpu.VMEM((2, RUN, REST // 4), BF),
+            pltpu.VMEM((2, HALF // 8, WIDE // 4), BF),
+            pltpu.VMEM((2, HALF // 4, WIDE // 4), BF),
+            pltpu.VMEM((2, HALF // 4, REST // 4), BF),
             pltpu.VMEM((3, 64, 640), BF),
             pltpu.VMEM((3, 16, 640), BF),
             pltpu.VMEM((16, 640), BF),
             pltpu.VMEM((64, 640), BF),
             pltpu.VMEM((16, 640), BF),
+            pltpu.VMEM((ROWS, WIDE), BF),
+            pltpu.VMEM((ROWS, WIDE), BF),
+            pltpu.VMEM((HALF, WIDE), BF),
+            pltpu.VMEM((HALF, WIDE), BF),
+            pltpu.VMEM((4, 240, 960), BF),
+            pltpu.VMEM((4, 320, 240), BF),
+            pltpu.VMEM((4, 320, 240), BF),
+            pltpu.SemaphoreType.DMA((6,)),
+            pltpu.SemaphoreType.DMA((6,)),
         ]
         + key_scratch()
-        + sum_scratch(WIDE)
-        + sum_scratch(REST)
-        + sems(140),
+        + sum_scratch(WIDE, HALF // 2)
+        + sum_scratch(WIDE, HALF)
+        + sum_scratch(REST, HALF)
+        + sems(190),
         compiler_params=pltpu.CompilerParams(
             collective_id=2, has_side_effects=True, vmem_limit_bytes=VMEM_LIMIT
         ),
         cost_estimate=pl.CostEstimate(flops=2_000_000_000, bytes_accessed=200_000_000, transcendentals=0),
+    )(*args)
+
+
+def finish_kernel(
+    g_gate_ref, g_up_ref, two_ref, three_ref, vec_ref, both_ref, place_ref, hidden_ref, d_out_ref,
+    out_ref, d_hidden_ref, query_ref, key_ref, value_ref, output_ref, gate_ref, up_ref, down_ref, vec_out_ref,
+    low_one, low_two, low_three, wide_one, wide_two, wide_down, wide_kv, rows, load_sems, store_sems,
+):
+    keep = pl.ds(0, 240)
+    runs_one = [pl.ds(1280 * k, 1280) for k in range(2)]
+    runs_two = [pl.ds(640 * k, 640) for k in range(4)] + [pl.ds(FF, 2 * D)]
+    loads = []
+    for src, dst, runs in (
+        (g_gate_ref, low_one.at[0], runs_one),
+        (g_up_ref, low_one.at[1], runs_one),
+        (two_ref, low_two, runs_two),
+        (three_ref, low_three, [pl.ds(0, 640)]),
+    ):
+        for c in runs:
+            loads.append(pltpu.make_async_copy(src.at[keep, c], dst.at[:, c], load_sems.at[len(loads)]))
+            loads[-1].start()
+    stores = []
+
+    def store(a, b):
+        stores.append(pltpu.make_async_copy(a, b, store_sems.at[len(stores)]))
+        stores[-1].start()
+
+    for k, (base, to) in enumerate(((hidden_ref, out_ref), (d_out_ref, d_hidden_ref))):
+        rows[k] = base[...] + dot(both_ref[:, D * k : D * (k + 1)], place_ref[...], TN)
+        store(rows.at[k], to)
+    for k in range(4):
+        loads[k].wait()
+        c = runs_one[k % 2]
+        wide_one[k // 2, :, c] = low_one[k // 2, :, c].astype(F32)
+        store(wide_one.at[k // 2, :, c], (gate_ref, up_ref)[k // 2].at[:, c])
+    for k in range(4):
+        loads[4 + k].wait()
+        r = pl.ds(240 * k, 240)
+        wide_down[r] = low_two[:, runs_two[k]].astype(F32)
+        store(wide_down.at[r], down_ref.at[r])
+    loads[8].wait()
+    for k, to in enumerate((query_ref, output_ref)):
+        wide_two[k] = low_two[:, FF + D * k : FF + D * (k + 1)].astype(F32)
+        store(wide_two.at[k], to)
+    loads[9].wait()
+    for k, to in enumerate((key_ref, value_ref)):
+        wide_kv[k] = low_three[:, 320 * k : 320 * (k + 1)].astype(F32).T
+        store(wide_kv.at[k], to)
+    core, ylo = lax.axis_index("core") == 1, lax.axis_index("ylo") == 1
+    p = [vec_ref[:, 240 * k : 240 * (k + 1)] for k in range(4)]
+    vec_out_ref[...] = jnp.where(ylo, jnp.where(core, p[3], p[2]), jnp.where(core, p[1], p[0]))
+    for copy in stores:
+        copy.wait()
+
+
+def finish(*args):
+    vmem, hbm = pl.BlockSpec(memory_space=pltpu.VMEM), pl.BlockSpec(memory_space=pl.ANY)
+    shapes = [(D, PAIR), (D, PAIR), (240, D), (320, 240), (320, 240), (240, D), (240, FF), (240, FF), (D, 640), (8, 240)]
+    return pl.pallas_call(
+        finish_kernel,
+        name="finish",
+        out_shape=tuple(jax.ShapeDtypeStruct(shape, F32) for shape in shapes),
+        in_specs=[hbm] * 4 + [vmem] * 5,
+        out_specs=(hbm,) * 9 + (vmem,),
+        scratch_shapes=[
+            pltpu.VMEM((2, 240, WIDE), BF),
+            pltpu.VMEM((240, REST), BF),
+            pltpu.VMEM((240, 640), BF),
+            pltpu.VMEM((2, 240, WIDE), F32),
+            pltpu.VMEM((2, 240, D), F32),
+            pltpu.VMEM((D, 640), F32),
+            pltpu.VMEM((2, 320, 240), F32),
+            pltpu.VMEM((2, D, PAIR), F32),
+            pltpu.SemaphoreType.DMA((10,)),
+            pltpu.SemaphoreType.DMA((14,)),
+        ],
+        compiler_params=pltpu.CompilerParams(vmem_limit_bytes=VMEM_LIMIT),
+        cost_estimate=pl.CostEstimate(flops=0, bytes_accessed=16_000_000, transcendentals=0),
     )(*args)
 
 
@@ -877,27 +1070,41 @@
 
 
 def dense_kernel(
-    mix_ref, q_ref, prob_ref, kv_ref, h_ref, up_ref, vec_ref,
+    mix_ref, q_ref, prob_in, kv_in, h_ref, up_ref, vec_ref,
     wo_ref, wg_ref, wu_ref, wd_ref, wos_ref, wgs_ref, wus_ref, wds_ref,
-    dq_ref, dkv_ref, g_ref, d_attn_ref, mixture_ref, d_mid_ref, out_ref, logit_ref, vec_out_ref,
+    dq_ref, dkv_out, g_out, d_attn_ref, mixture_ref, d_mid_ref, out_ref, logit_ref, vec_out_ref,
     wo, wg, wu, wd, mixf, gate_s, up_s, inner, dgu, dffn, xs, do_s, d_mix_s,
     dgu_all, dffn_all, xs_all, inner_all, xs_relay, inner_relay,
-    load_sems, send_sems, recv_sems,
+    prob_ref, kv_ref, dkv_ref, g_ref,
+    load_sems, store_sems, send_sems, recv_sems,
 ):
     me = here()
     loads = []
     for k, (own, rest, to) in enumerate(
         ((wo_ref, wos_ref, wo), (wg_ref, wgs_ref, wg), (wu_ref, wus_ref, wu), (wd_ref, wds_ref, wd))
     ):
+        there = to.at[pl.ds(1, 3)] if k < 3 else to.at[pl.ds(2, 1)]
         pair = (
             pltpu.make_async_copy(own, to.at[0], load_sems.at[2 * k]),
-            pltpu.make_async_copy(rest, to.at[pl.ds(1, 3)], load_sems.at[2 * k + 1]),
+            pltpu.make_async_copy(rest, there, load_sems.at[2 * k + 1]),
         )
         for copy in pair:
             copy.start()
         loads.append(pair)
+    loads.append(
+        (
+            pltpu.make_async_copy(prob_in, prob_ref, load_sems.at[8]),
+            pltpu.make_async_copy(kv_in, kv_ref, load_sems.at[9]),
+        )
+    )
+    for copy in loads[4]:
+        copy.start()
     greet(me, WEIGHT)
     sends = Sends(me, send_sems, recv_sems)
+    down = [
+        sends.start(wd_ref, wd.at[1], "core", 1),
+        sends.start(wds_ref.at[0], wd.at[3], "core", 1),
+    ]
     shards = [shard_of(me, k) for k in range(4)]
 
     def run640(k):
@@ -935,6 +1142,8 @@
     gate = gate_s[...]
     inner[...] = (gate * jax.nn.sigmoid(gate) * up_s[...]).astype(BF)
     loaded(3)
+    for copy in down:
+        copy.wait_recv()
     ffn_out = sum(dot(inner[:, run640(k)], wd[k], NT) for k in range(4))
     route = jax.nn.sigmoid(jnp.sum(hidden * route_w, axis=-1, keepdims=True))
     branch = attn_out + ffn_out
@@ -946,26 +1155,30 @@
     vec_out_ref[...] = jnp.zeros_like(vec_out_ref)
     vec_out_ref[2:3, :D] = jnp.sum(d_logit * hidden, axis=0, keepdims=True)
     d_ffn = d_branch.astype(BF)
+    own = pl.ds(0, T)
     dffn[...] = jnp.zeros_like(dffn)
     for k in range(4):
         dffn[:, 256 * k : 256 * k + 240] = d_branch[:, 240 * k : 240 * (k + 1)].astype(BF)
+    share_one = everyone_steps(
+        sends,
+        (
+            ("all", dffn, dffn_all, None),
+            ("one", [inner.at[:, run640(k)] for k in range(4)], inner_all, inner_relay),
+            ("one", [xs.at[k] for k in range(4)], xs_all, xs_relay),
+        ),
+    )
+    next(share_one)
+    dffn_all[own], xs_all[own], inner_all[own] = dffn[...], xs[0], inner[:, run640(0)]
     for k in range(4):
         d_inner = dot(d_ffn, wd[k])
         gate, up = gate_s[:, run640(k)], up_s[:, run640(k)]
         sg = jax.nn.sigmoid(gate)
         dgu[:, run640(k)] = (d_inner * up * (sg + gate * sg * (1.0 - sg))).astype(BF)
         dgu[:, run640_up(k)] = (d_inner * (gate * sg)).astype(BF)
-    pieces = (
-        ("all", dgu, dgu_all, None),
-        ("all", dffn, dffn_all, None),
-        ("one", [xs.at[k] for k in range(4)], xs_all, xs_relay),
-        ("one", [inner.at[:, run640(k)] for k in range(4)], inner_all, inner_relay),
-    )
-    share = everyone_steps(sends, pieces)
-    next(share)
-    own = pl.ds(0, T)
-    dgu_all[own], dffn_all[own] = dgu[...], dffn[...]
-    xs_all[own], inner_all[own] = xs[0], inner[:, run640(0)]
+    share_two = everyone_steps(sends, (("all", dgu, dgu_all, None),))
+    next(share_two)
+    next(share_one)
+    dgu_all[own] = dgu[...]
     d_gate, d_up = dgu[:, :FF], dgu[:, FF:]
     d_x2 = jnp.concatenate(
         our_order(me, [dot(d_gate, wg[k], NT) + dot(d_up, wu[k], NT) for k in range(4)]), axis=1
@@ -982,6 +1195,19 @@
             h = GROUPS * j + g
             do_s[j, g * T : (g + 1) * T, HEAD_DIM:] = d_mix_s[:, HEAD_DIM * h : HEAD_DIM * (h + 1)].astype(BF)
 
+    stores = []
+
+    def store(a, b):
+        stores.append(pltpu.make_async_copy(a, b, store_sems.at[KV_HEADS + len(stores)]))
+        stores[-1].start()
+
+    together(share_one)
+    for k in range(4):
+        c = pl.ds(2 * FF + 640 * k, 640)
+        g_ref[:, c] = dot(dffn_all[:, 256 * k : 256 * (k + 1)], inner_all[...], TN).astype(BF)
+        store(g_ref.at[:, c], g_out.at[:, c])
+    loaded(4)
+
     @pl.loop(0, KV_HEADS)
     def _(j):
         c = pl.ds(pl.multiple_of(j * 128, 128), 128)
@@ -993,14 +1219,18 @@
         dq_ref[j] = dot(d_score, tile) * SCALE
         grad = dot(d_score, q_ref[j], TN) * SCALE + dot(prob, d_out, TN)
         dkv_ref[:, :, :, :, c] = grad.astype(BF).reshape(2, 4, 4, T, 128)
-
-    together(share)
-    for c in range(0, 2 * FF, 1280):
-        g_ref[:, c : c + 1280] = dot(xs_all[...], dgu_all[:, c : c + 1280], TN).astype(BF)
-    for k in range(4):
-        g_ref[:, 2 * FF + 640 * k : 2 * FF + 640 * (k + 1)] = dot(
-            dffn_all[:, 256 * k : 256 * (k + 1)], inner_all[...], TN
-        ).astype(BF)
+        pltpu.make_async_copy(dkv_ref.at[:, :, :, :, c], dkv_out.at[:, :, :, :, c], store_sems.at[j]).start()
+
+    together(share_two)
+    for at in range(0, 2 * FF, 1280):
+        c = pl.ds(at, 1280)
+        g_ref[:, c] = dot(xs_all[...], dgu_all[:, c], TN).astype(BF)
+        store(g_ref.at[:, c], g_out.at[:, c])
+    for j in range(KV_HEADS):
+        c = pl.ds(j * 128, 128)
+        pltpu.make_async_copy(dkv_ref.at[:, :, :, :, c], dkv_out.at[:, :, :, :, c], store_sems.at[j]).wait()
+    for copy in stores:
+        copy.wait()
     sends.finish()
 
 
@@ -1021,8 +1251,8 @@
             jax.ShapeDtypeStruct((T, 128), F32),
             jax.ShapeDtypeStruct((8, 1024), F32),
         ),
-        in_specs=[vmem] * 7 + [hbm] * 8,
-        out_specs=(vmem,) * 9,
+        in_specs=[vmem] * 2 + [hbm] * 2 + [vmem] * 3 + [hbm] * 8,
+        out_specs=(vmem,) + (hbm,) * 2 + (vmem,) * 6,
         scratch_shapes=[
             pltpu.VMEM((4, 240, D), BF),
             pltpu.VMEM((4, 240, FF), BF),
@@ -1043,7 +1273,12 @@
             pltpu.VMEM((4 * T, 640), BF),
             pltpu.VMEM((T, 256), BF),
             pltpu.VMEM((T, 640), BF),
-            pltpu.SemaphoreType.DMA((8,)),
+            pltpu.VMEM((KV_HEADS, rows, KEYS), BF),
+            pltpu.VMEM((2, 4, 4, T, 640), BF),
+            pltpu.VMEM((2, 4, 4, T, 640), BF),
+            pltpu.VMEM((ROWS, 3 * FF), BF),
+            pltpu.SemaphoreType.DMA((10,)),
+            pltpu.SemaphoreType.DMA((13,)),
         ]
         + sems(28),
         compiler_params=pltpu.CompilerParams(
@@ -1070,29 +1305,25 @@
     d_q_heads, d_kv, g_one, d_attn, mixture, d_mid, out_c, d_logit, vec_out = dense(
         mix_heads, q_heads, prob, kv_all, h, up_c, vec_in, own_w, rest_w
     )
-    s_one, s_two, s_three, vector, both = back(
+    s_gate, s_up, s_two, s_three, vector, both = back(
         d_kv, g_one, d_q_heads, d_attn, mixture, x1, h, d_mid, out_c, d_logit, vec_in, vec_out, cosine, sine, wq, wk, wv
     )
-    spread = dot(both, place, TN)
-    output = (tokens.T + spread[:D]).T
-    d_tokens = (upstream.T + spread[D:]).T
-    shard = lax.axis_index("ylo") * 2 + lax.axis_index("core")
-    vector = lax.dynamic_slice_in_dim(vector, shard * 240, 240, axis=1)
-    s_one, s_two, s_three = s_one[:240], s_two[:240], s_three[:240]
-    g_down = jnp.concatenate([s_two[:, 640 * k : 640 * (k + 1)] for k in range(4)], axis=0).astype(F32).T
+    output, d_tokens, g_query, g_key, g_value, g_output, g_gate, g_up, g_down, vectors = finish(
+        s_gate, s_up, s_two, s_three, vector, both, place, tokens.T, upstream.T
+    )
     return (
-        output[None],
-        d_tokens[None],
-        s_two[:, FF : FF + D].astype(F32),
-        s_three[:, :320].astype(F32),
-        s_three[:, 320:].astype(F32),
-        s_two[:, FF + D : FF + 2 * D].astype(F32),
-        s_one[:, :FF].astype(F32),
-        s_one[:, FF:].astype(F32),
-        g_down,
-        vector[0],
-        vector[1],
-        vector[2],
+        output.T[None],
+        d_tokens.T[None],
+        g_query,
+        g_key.T,
+        g_value.T,
+        g_output,
+        g_gate,
+        g_up,
+        g_down.T,
+        vectors[0],
+        vectors[1],
+        vectors[2],
     )
 
 

time: 221 us -> 192 us (0.87)
  Pallas kernels: 203 us -> 186 us
  other arithmetic: 9.09 us -> 0.62 us
  local copies, waits for them, and re-layouts: 8.2 us -> 3.96 us
    pallas_call x1, Pallas kernels: 106 us -> 91 us  [back(): pl.pallas_call(back_kernel, name='back', out_shape=(jax.ShapeDtypeStruct(...]
    pallas_call x1, Pallas kernels: 64.4 us -> 55.4 us  [front(): pl.pallas_call(front_kernel, name='front', out_shape=(jax.ShapeDtypeStruc...]
    pallas_call x0 -> x1, Pallas kernels: none -> 7.78 us  [finish(): pl.pallas_call(finish_kernel, name='finish', out_shape=tuple((jax.ShapeDt...]
    convert_element_type x3 -> x0, other arithmetic: 5.83 us -> none  [the longest x1 2.87 us: per_device(): s_one[:, FF:].astype(F32)]
    unnamed x14 -> x0, local copies, waits for them, and re-layouts: 2.79 us -> none
where the time goes in v2:
time: 192 us
  Pallas kernels  186 us (97%)
  local copies, waits for them, and re-layouts  3.96 us (2%)
    pallas_call x1, Pallas kernels, back(): pl.pallas_call(back_kernel, name='back', out_shape=(jax.ShapeDtypeStruct(...  91 us
    pallas_call x1, Pallas kernels, front(): pl.pallas_call(front_kernel, name='front', out_shape=(jax.ShapeDtypeStruc...  55.4 us
    pallas_call x1, Pallas kernels, dense(): pl.pallas_call(dense_kernel, name='dense', out_shape=(jax.ShapeDtypeStruc...  32.2 us
    pallas_call x1, Pallas kernels, finish(): pl.pallas_call(finish_kernel, name='finish', out_shape=tuple((jax.ShapeDt...  7.78 us

profile of v2, /device:TPU:0, one launch (start us, length us, event | category | flops | bytes accessed | tf_op | source)
XLA Modules:
  0.0 191.6 jit_solution(7291359843493968299)
XLA Ops:
  0.7 0.7 stack.12
  1.3 0.7 stack.13
  2.0 0.7 stack.14
  2.6 0.6 broadcast_in_dim_tile.3.freq_ref
  3.2 0.6 fusion.9.vec_ref
  3.8 55.4 %front.1 = (f32[5,192,128]{2,1,0:T(8,128)}, bf16[5,192,2048]{2,1,0:T(8,128)(2,1)}, bf16[5,192,128]{2,1,0:T(8,128)(2,1)}, bf16[2,4,4,64,640]{4,3,2,1,0:T(8,128)(2...) custom-call(f32[960,128]{1,0:T(8,128)} %bitcast.21, ...), custom_call_target="tpu_custom_call" | custom-call | flops 5000000000 | bytes 90000000 | tf_op jit(solution)/shard_map/front/pallas_call | solution.py:396
  59.3 32.2 %dense.1 = (f32[5,192,128]{2,1,0:T(8,128)}, bf16[2,4,4,64,640]{4,3,2,1,0:T(8,128)(2,1)}, bf16[256,7680]{1,0:T(8,128)(2,1)}, bf16[64,960]{1,0:T(8,128)(2,1)}, bf1...) custom-call(f32[5,192,128]{2,1,0:T(8,128)} %get-tuple-element.55.mix, ...), custom_call_target="tpu_custom_call" | custom-call | flops 20000000000 | bytes 40000000 | tf_op jit(solution)/shard_map/dense/pallas_call | solution.py:1240
  91.5 91.0 %back.1 = (bf16[256,2560]{1,0:T(8,128)(2,1)}, bf16[256,2560]{1,0:T(8,128)(2,1)}, bf16[256,4608]{1,0:T(8,128)(2,1)}, bf16[256,640]{1,0:T(8,128)(2,1)}, f32[8,1024]{1,0:T(8,128)}, /*index=5*/bf16[128,1920]{1,0:T(8,128)(2,1)}) custom-call(bf16[2,4,4,64,640]{4,3,2,1,0:T(8,128)(2,1)} %get-tuple-element.66.part_ref, bf16[256,7680]{1,0:T(8,128)(2,1)} %get-tuple-element.67.g_in, ...), custom_call_target="tpu_custom_call" | custom-call | flops 2000000000 | bytes 200000000 | tf_op jit(solution)/shard_map/back/pallas_call | solution.py:890
  182.4 7.8 %finish.1 = (f32[960,128]{1,0:T(8,128)}, f32[960,128]{1,0:T(8,128)}, f32[240,960]{1,0:T(8,128)}, f32[320,240]{1,0:T(8,128)}, f32[320,240]{1,0:T(8,128)}, /*index...) custom-call(bf16[256,2560]{1,0:T(8,128)(2,1)} %get-tuple-element.81.g_gat, ...), custom_call_target="tpu_custom_call" | custom-call | bytes 16000000 | tf_op jit(solution)/shard_map/finish/pallas_call | solution.py:1003
  190.2 1.4 fusion.10
  (2 shorter events, 0.0 us)

commit v3 on v2

--- a/solution.py
+++ b/solution.py
@@ -2,6 +2,7 @@
 
 import jax
 import jax.numpy as jnp
+import numpy as np
 from jax import lax
 from jax.experimental import pallas as pl
 from jax.experimental.pallas import tpu as pltpu
@@ -378,7 +379,7 @@
         "u": late.half(wu_ref, wus_ref, *small),
         "d": late.half(wd_ref, wds_ref, *large),
     }
-    run_lanes(lanes, FRONT_ORDER)
+    run_lanes(lanes, "".join(FRONT_ORDER))
     late.finish()
     for copy in stores:
         copy.wait()
@@ -386,7 +387,7 @@
 
 
 FRONT_ORDER = (
-    "mmmommtmmoumdmommmtummdmmtumdm"
+    "mmmommtmmoumdmommmtummdmmtumdm",
 )
 
 
@@ -541,9 +542,8 @@
     return (0, cut), (cut, big - cut)
 
 
-def sum_steps(me, sends, g_ref, mine, swap_y, low, out_b, full, sums, nlow, nout, nfull, y_in):
-    run, big = mine.shape[-2:]
-    h = 4 * run
+def wide_steps(me, sends, g_ref, low, out_b, full, sums):
+    h, big = sums.shape[0] // 2, sums.shape[1]
     cut = h // 2
     near, whole = {}, {}
 
@@ -566,15 +566,23 @@
             r = pl.ds(s * h, h)
             whole[s, step] = sends.start(out_b.at[d, r], full.at[d, r], axis, step)
 
-    def rows(s, other, step):
-        return pl.ds(pl.multiple_of(s * h + around(me, other, step) * run, 16), run)
-
-    for s, (axis, other) in enumerate(STREAMS):
+    for s, (axis, _) in enumerate(STREAMS):
         yield
         for step in (1, -1):
             whole[s, step].wait_recv()
         r = pl.ds(s * h, h)
         sums[r] = plus(g_ref[r, columns(me, axis, 0, big)], full[0, r], full[1, r]).astype(BF)
+
+
+def narrow_steps(me, sends, sums, mine, swap_y, nlow, nout, nfull, y_in):
+    run, big = mine.shape[-2:]
+    h = 4 * run
+    near, whole = {}, {}
+
+    def rows(s, other, step):
+        return pl.ds(pl.multiple_of(s * h + around(me, other, step) * run, 16), run)
+
+    for s, (axis, other) in enumerate(STREAMS):
         for d, step in enumerate((1, -1)):
             c = pl.ds(*halves(big)[d])
             near[s, step] = sends.start(sums.at[rows(s, other, 2), c], nlow.at[s, :, c], other, step)
@@ -605,6 +613,11 @@
             mine[s] = plus(y_in[0, s], y_in[1, s]).astype(BF)
 
 
+def sum_steps(me, sends, g_ref, mine, swap_y, low, out_b, full, sums, *narrow):
+    yield from wide_steps(me, sends, g_ref, low, out_b, full, sums)
+    yield from narrow_steps(me, sends, sums, mine, swap_y, *narrow)
+
+
 def sum_scratch(width, h):
     big, run = width // 4, h // 4
     return [
@@ -719,21 +732,21 @@
 
 
 def small_steps(me, sends, g_ref, out_ref, got_x, got_z, got_y, sum_z, sum_y):
-    x, z = me[4], me[3]
+    x, z = me[3], me[4]
     steps = (1, -1, 2)
 
     def rows(at, step, count, base=0):
         return pl.ds(pl.multiple_of(base + lax.rem(at + step + 4, 4) * count, 16), count)
 
     copies = [
-        sends.start(g_ref.at[rows(x, step, 64)], got_x.at[k], "x", step) for k, step in enumerate(steps)
+        sends.start(g_ref.at[rows(x, step, 64)], got_x.at[k], "z", step) for k, step in enumerate(steps)
     ]
     yield
     for copy in copies:
         copy.wait_recv()
     sum_z[...] = plus(g_ref[rows(x, 0, 64)], got_x[0], got_x[1], got_x[2]).astype(BF)
     copies = [
-        sends.start(sum_z.at[rows(z, step, 16)], got_z.at[k], "z", step) for k, step in enumerate(steps)
+        sends.start(sum_z.at[rows(z, step, 16)], got_z.at[k], "x", step) for k, step in enumerate(steps)
     ]
     yield
     for copy in copies:
@@ -744,40 +757,39 @@
     copy.wait_recv()
     ref = out_ref.at[rows(z, 0, 16, x * 64)]
     ref[...] = plus(sum_y[...], got_y[...]).astype(BF)
+    copies = [sends.start(ref, ref, "x", step) for step in steps]
+    yield
+    for copy in copies:
+        copy.wait_recv()
+    ref = out_ref.at[rows(x, 0, 64)]
     copies = [sends.start(ref, ref, "z", step) for step in steps]
     yield
     for copy in copies:
         copy.wait_recv()
-    ref = out_ref.at[rows(x, 0, 64)]
-    copies = [sends.start(ref, ref, "x", step) for step in steps]
-    yield
-    for copy in copies:
-        copy.wait_recv()
 
 
 KEY_N, SUM_N = 9, 8
-WIDE, REST = FF, 4608
+WIDE, REST = FF, 2048
 
 
 def back_kernel(
-    part_ref, g_in, dq_ref, d_attn_ref, mixture_ref, x1_ref, h_ref, d_mid_ref, out_ref, logit_ref, vec_ref, vec_part_ref,
+    part_ref, g_in, sums_ref, dq_ref, d_attn_ref, mixture_ref, x1_ref, h_ref, d_mid_ref, out_ref, logit_ref, vec_ref, vec_part_ref,
     cos_ref, sin_ref, wq_in, wk_in, wv_in,
-    gate_ref, up_ref, two_ref, three_ref, vec_out_ref, both_ref,
+    gate_ref, up_ref, down_ref, two_ref, three_ref, vec_out_ref, both_ref,
     own, ra, rb, xs, ra_all, rb_all, xs_all, xs_relay, g_two, g_three, d_x1_s, vec_all, keep_v, got_v,
-    mine_gate, mine_up, mine_two, got_x, got_z, got_y, sum_z, sum_y,
+    mine_gate, mine_up, mine_down, mine_two, got_x, got_z, got_y, sum_z, sum_y,
     g_gate, g_up, kept, got_gate, wq, wk, wv, load_sems, store_sems,
     *scratch,
 ):
     me = here()
     key_scr, rest = scratch[:KEY_N], scratch[KEY_N:-2]
-    gate_scr, up_scr, two_scr = rest[:SUM_N], rest[SUM_N : 2 * SUM_N], rest[2 * SUM_N :]
+    gate_scr, up_scr, two_scr, down_scr = (rest[SUM_N * k : SUM_N * (k + 1)] for k in range(4))
     loads = [
         pltpu.make_async_copy(a, b, load_sems.at[k])
         for k, (a, b) in enumerate(
             (
                 (g_in.at[:, pl.ds(0, WIDE)], g_gate),
                 (g_in.at[:, pl.ds(WIDE, WIDE)], g_up),
-                (g_in.at[:, pl.ds(2 * WIDE, FF)], g_two.at[:, pl.ds(0, FF)]),
                 (wq_in, wq),
                 (wk_in, wk),
                 (wv_in, wv),
@@ -854,15 +866,15 @@
         for copy in loads[2:]:
             copy.wait()
         d_x1_s[...] = jnp.concatenate(our_order(me, [dot(d_q, wq[k], NT) for k in range(4)]), axis=1)
-        g_two[:, FF + 2 * D :] = jnp.zeros((ROWS, 128), BF)
+        g_two[:, 2 * D :] = jnp.zeros((ROWS, 128), BF)
         yield
         next(share)
         yield
         together(share)
-        g_two[:, FF : FF + D] = dot(xs_all[:, :256], ra_all[:, :D], TN).astype(BF)
-        g_two[:, FF + D : FF + 2 * D] = dot(xs_all[:, 256:], ra_all[:, D:], TN).astype(BF)
+        g_two[:, :D] = dot(xs_all[:, :256], ra_all[:, :D], TN).astype(BF)
+        g_two[:, D : 2 * D] = dot(xs_all[:, 256:], ra_all[:, D:], TN).astype(BF)
         yield from sum_steps(me, sends, g_two, mine_two, True, *two_scr)
-        yield from spread_steps(me, sends, mine_two, two_ref, store_sems.at[pl.ds(4, 2)], False)
+        yield from spread_steps(me, sends, mine_two, two_ref, store_sems.at[pl.ds(6, 2)], False)
 
     def gate():
         loads[0].wait()
@@ -875,13 +887,18 @@
         yield from sum_steps(me, sends, g_up, mine_up, True, *up_scr)
         yield from spread_steps(me, sends, mine_up, up_ref, store_sems.at[pl.ds(2, 2)], False)
 
-    run_lanes({"k": keys(), "g": gate(), "u": up(), "q": queries()}, ORDER)
+    def down():
+        yield from narrow_steps(me, sends, sums_ref, mine_down, True, *down_scr)
+        yield from spread_steps(me, sends, mine_down, down_ref, store_sems.at[pl.ds(4, 2)], False)
+
+    run_lanes({"k": keys(), "g": gate(), "u": up(), "d": down(), "q": queries()}, "".join(ORDER))
     sends.finish()
 
 
 ORDER = (
-    "kuqgkkuuqgkkqkkgguuqkkguugqukqgkguqkuguq"
-    "gquqgukguqugqqgkgqqgukgqqkgguugqquqqgk"
+    "gkdqukddkuudgggkkuggqduqdkkuudggqqkududk",
+    "ggqduqggukqgkukgqudgqgkuuqqqkddgqqgkuuqd",
+    "qgkqudgqqgkuq",
 )
 
 
@@ -893,13 +910,14 @@
         out_shape=(
             jax.ShapeDtypeStruct((ROWS, WIDE), BF),
             jax.ShapeDtypeStruct((ROWS, WIDE), BF),
+            jax.ShapeDtypeStruct((ROWS, WIDE), BF),
             jax.ShapeDtypeStruct((ROWS, REST), BF),
             jax.ShapeDtypeStruct((ROWS, 640), BF),
             jax.ShapeDtypeStruct((8, 1024), F32),
             jax.ShapeDtypeStruct((PAIR, 2 * D), BF),
         ),
         in_specs=[vmem, hbm] + [vmem] * (len(args) - 5) + [hbm] * 3,
-        out_specs=(hbm,) * 3 + (vmem,) * 3,
+        out_specs=(hbm,) * 4 + (vmem,) * 3,
         scratch_shapes=[
             pltpu.VMEM((T, 640), F32),
             pltpu.VMEM((T, 2 * D), BF),
@@ -917,6 +935,7 @@
             pltpu.VMEM((9, 8, 1024), F32),
             pltpu.VMEM((2, HALF // 8, WIDE // 4), BF),
             pltpu.VMEM((2, HALF // 4, WIDE // 4), BF),
+            pltpu.VMEM((2, HALF // 4, WIDE // 4), BF),
             pltpu.VMEM((2, HALF // 4, REST // 4), BF),
             pltpu.VMEM((3, 64, 640), BF),
             pltpu.VMEM((3, 16, 640), BF),
@@ -931,13 +950,14 @@
             pltpu.VMEM((4, 320, 240), BF),
             pltpu.VMEM((4, 320, 240), BF),
             pltpu.SemaphoreType.DMA((6,)),
-            pltpu.SemaphoreType.DMA((6,)),
+            pltpu.SemaphoreType.DMA((8,)),
         ]
         + key_scratch()
         + sum_scratch(WIDE, HALF // 2)
         + sum_scratch(WIDE, HALF)
         + sum_scratch(REST, HALF)
-        + sems(190),
+        + sum_scratch(WIDE, HALF)[4:]
+        + sems(230),
         compiler_params=pltpu.CompilerParams(
             collective_id=2, has_side_effects=True, vmem_limit_bytes=VMEM_LIMIT
         ),
@@ -946,18 +966,19 @@
 
 
 def finish_kernel(
-    g_gate_ref, g_up_ref, two_ref, three_ref, vec_ref, both_ref, place_ref, hidden_ref, d_out_ref,
+    g_gate_ref, g_up_ref, g_down_ref, two_ref, three_ref, vec_ref, both_ref, place_ref, hidden_ref, d_out_ref,
     out_ref, d_hidden_ref, query_ref, key_ref, value_ref, output_ref, gate_ref, up_ref, down_ref, vec_out_ref,
-    low_one, low_two, low_three, wide_one, wide_two, wide_down, wide_kv, rows, load_sems, store_sems,
+    low_one, low_down, low_two, low_three, wide_one, wide_two, wide_down, wide_kv, rows, load_sems, store_sems,
 ):
     keep = pl.ds(0, 240)
     runs_one = [pl.ds(1280 * k, 1280) for k in range(2)]
-    runs_two = [pl.ds(640 * k, 640) for k in range(4)] + [pl.ds(FF, 2 * D)]
+    runs_down = [pl.ds(640 * k, 640) for k in range(4)]
     loads = []
     for src, dst, runs in (
         (g_gate_ref, low_one.at[0], runs_one),
         (g_up_ref, low_one.at[1], runs_one),
-        (two_ref, low_two, runs_two),
+        (g_down_ref, low_down, runs_down),
+        (two_ref, low_two, [pl.ds(0, 2 * D)]),
         (three_ref, low_three, [pl.ds(0, 640)]),
     ):
         for c in runs:
@@ -980,11 +1001,11 @@
     for k in range(4):
         loads[4 + k].wait()
         r = pl.ds(240 * k, 240)
-        wide_down[r] = low_two[:, runs_two[k]].astype(F32)
+        wide_down[r] = low_down[:, runs_down[k]].astype(F32)
         store(wide_down.at[r], down_ref.at[r])
     loads[8].wait()
     for k, to in enumerate((query_ref, output_ref)):
-        wide_two[k] = low_two[:, FF + D * k : FF + D * (k + 1)].astype(F32)
+        wide_two[k] = low_two[:, D * k : D * (k + 1)].astype(F32)
         store(wide_two.at[k], to)
     loads[9].wait()
     for k, to in enumerate((key_ref, value_ref)):
@@ -1004,10 +1025,11 @@
         finish_kernel,
         name="finish",
         out_shape=tuple(jax.ShapeDtypeStruct(shape, F32) for shape in shapes),
-        in_specs=[hbm] * 4 + [vmem] * 5,
+        in_specs=[hbm] * 5 + [vmem] * 5,
         out_specs=(hbm,) * 9 + (vmem,),
         scratch_shapes=[
             pltpu.VMEM((2, 240, WIDE), BF),
+            pltpu.VMEM((240, WIDE), BF),
             pltpu.VMEM((240, REST), BF),
             pltpu.VMEM((240, 640), BF),
             pltpu.VMEM((2, 240, WIDE), F32),
@@ -1072,10 +1094,10 @@
 def dense_kernel(
     mix_ref, q_ref, prob_in, kv_in, h_ref, up_ref, vec_ref,
     wo_ref, wg_ref, wu_ref, wd_ref, wos_ref, wgs_ref, wus_ref, wds_ref,
-    dq_ref, dkv_out, g_out, d_attn_ref, mixture_ref, d_mid_ref, out_ref, logit_ref, vec_out_ref,
+    dq_ref, dkv_out, g_out, sums_ref, d_attn_ref, mixture_ref, d_mid_ref, out_ref, logit_ref, vec_out_ref,
     wo, wg, wu, wd, mixf, gate_s, up_s, inner, dgu, dffn, xs, do_s, d_mix_s,
     dgu_all, dffn_all, xs_all, inner_all, xs_relay, inner_relay,
-    prob_ref, kv_ref, dkv_ref, g_ref,
+    prob_ref, kv_ref, dkv_ref, g_ref, g_down, low, out_b, full,
     load_sems, store_sems, send_sems, recv_sems,
 ):
     me = here()
@@ -1099,7 +1121,7 @@
     )
     for copy in loads[4]:
         copy.start()
-    greet(me, WEIGHT)
+    greet(me, NEAR[:4] + WEIGHT)
     sends = Sends(me, send_sems, recv_sems)
     down = [
         sends.start(wd_ref, wd.at[1], "core", 1),
@@ -1109,9 +1131,6 @@
 
     def run640(k):
         return pl.ds(pl.multiple_of(shards[k] * 640, 128), 640)
-
-    def run640_up(k):
-        return pl.ds(pl.multiple_of(FF + shards[k] * 640, 128), 640)
 
     def loaded(k):
         for copy in loads[k]:
@@ -1135,6 +1154,8 @@
     xs[...] = jnp.zeros_like(xs)
     for k in range(4):
         xs[k, :, :240] = x2_k[k]
+    shares = [everyone_steps(sends, (("one", [xs.at[k] for k in range(4)], xs_all, xs_relay),))]
+    next(shares[0])
     loaded(1)
     gate_s[...] = sum(dot(x2_k[k], wg[k]) for k in range(4))
     loaded(2)
@@ -1142,6 +1163,10 @@
     gate = gate_s[...]
     inner[...] = (gate * jax.nn.sigmoid(gate) * up_s[...]).astype(BF)
     loaded(3)
+    shares.append(
+        everyone_steps(sends, (("one", [inner.at[:, run640(k)] for k in range(4)], inner_all, inner_relay),))
+    )
+    next(shares[1])
     for copy in down:
         copy.wait_recv()
     ffn_out = sum(dot(inner[:, run640(k)], wd[k], NT) for k in range(4))
@@ -1159,25 +1184,25 @@
     dffn[...] = jnp.zeros_like(dffn)
     for k in range(4):
         dffn[:, 256 * k : 256 * k + 240] = d_branch[:, 240 * k : 240 * (k + 1)].astype(BF)
-    share_one = everyone_steps(
-        sends,
-        (
-            ("all", dffn, dffn_all, None),
-            ("one", [inner.at[:, run640(k)] for k in range(4)], inner_all, inner_relay),
-            ("one", [xs.at[k] for k in range(4)], xs_all, xs_relay),
-        ),
-    )
-    next(share_one)
+    shares.append(everyone_steps(sends, (("all", dffn, dffn_all, None),)))
+    next(shares[2])
     dffn_all[own], xs_all[own], inner_all[own] = dffn[...], xs[0], inner[:, run640(0)]
-    for k in range(4):
-        d_inner = dot(d_ffn, wd[k])
-        gate, up = gate_s[:, run640(k)], up_s[:, run640(k)]
-        sg = jax.nn.sigmoid(gate)
-        dgu[:, run640(k)] = (d_inner * up * (sg + gate * sg * (1.0 - sg))).astype(BF)
-        dgu[:, run640_up(k)] = (d_inner * (gate * sg)).astype(BF)
-    share_two = everyone_steps(sends, (("all", dgu, dgu_all, None),))
-    next(share_two)
-    next(share_one)
+    late = []
+    for p in range(2):
+        first = 2 * lax.rem(me[0] + p, 2)
+        for b in range(2):
+            at = (2 * p + (me[1] if b == 0 else 1 - me[1])) * 640
+            run, run_up = (pl.ds(pl.multiple_of(c + at, 128), 640) for c in (0, FF))
+            d_inner = dot(d_ffn, wd[first + b])
+            gate, up = gate_s[:, run], up_s[:, run]
+            sg = jax.nn.sigmoid(gate)
+            dgu[:, run] = (d_inner * up * (sg + gate * sg * (1.0 - sg))).astype(BF)
+            dgu[:, run_up] = (d_inner * (gate * sg)).astype(BF)
+        cols = [pl.ds(c + 1280 * p, 1280) for c in (0, FF)]
+        late.append(everyone_steps(sends, tuple(("all", dgu.at[:, c], dgu_all.at[:, c], None) for c in cols)))
+        next(late[-1])
+    for share in shares:
+        next(share)
     dgu_all[own] = dgu[...]
     d_gate, d_up = dgu[:, :FF], dgu[:, FF:]
     d_x2 = jnp.concatenate(
@@ -1198,19 +1223,18 @@
     stores = []
 
     def store(a, b):
-        stores.append(pltpu.make_async_copy(a, b, store_sems.at[KV_HEADS + len(stores)]))
+        stores.append(pltpu.make_async_copy(a, b, store_sems.at[len(stores)]))
         stores[-1].start()
 
-    together(share_one)
+    together(*shares)
     for k in range(4):
-        c = pl.ds(2 * FF + 640 * k, 640)
-        g_ref[:, c] = dot(dffn_all[:, 256 * k : 256 * (k + 1)], inner_all[...], TN).astype(BF)
-        store(g_ref.at[:, c], g_out.at[:, c])
+        c = pl.ds(640 * k, 640)
+        g_down[:, c] = dot(dffn_all[:, 256 * k : 256 * (k + 1)], inner_all[...], TN).astype(BF)
+    wide = wide_steps(me, sends, g_down, low, out_b, full, sums_ref)
+    next(wide)
     loaded(4)
-
-    @pl.loop(0, KV_HEADS)
-    def _(j):
-        c = pl.ds(pl.multiple_of(j * 128, 128), 128)
+    for j in range(KV_HEADS):
+        c = pl.ds(j * 128, 128)
         tile = kv_ref[:, :, :, :, c].reshape(KEYS, 128)
         prob, d_out = prob_ref[j], do_s[j]
         d_prob = dot(d_out, tile, NT)
@@ -1219,16 +1243,16 @@
         dq_ref[j] = dot(d_score, tile) * SCALE
         grad = dot(d_score, q_ref[j], TN) * SCALE + dot(prob, d_out, TN)
         dkv_ref[:, :, :, :, c] = grad.astype(BF).reshape(2, 4, 4, T, 128)
-        pltpu.make_async_copy(dkv_ref.at[:, :, :, :, c], dkv_out.at[:, :, :, :, c], store_sems.at[j]).start()
-
-    together(share_two)
+        store(dkv_ref.at[:, :, :, :, c], dkv_out.at[:, :, :, :, c])
+        if j == 3:
+            next(wide)
+            next(wide)
+    together(*late)
     for at in range(0, 2 * FF, 1280):
         c = pl.ds(at, 1280)
         g_ref[:, c] = dot(xs_all[...], dgu_all[:, c], TN).astype(BF)
         store(g_ref.at[:, c], g_out.at[:, c])
-    for j in range(KV_HEADS):
-        c = pl.ds(j * 128, 128)
-        pltpu.make_async_copy(dkv_ref.at[:, :, :, :, c], dkv_out.at[:, :, :, :, c], store_sems.at[j]).wait()
+    together(wide)
     for copy in stores:
         copy.wait()
     sends.finish()
@@ -1243,7 +1267,8 @@
         out_shape=(
             jax.ShapeDtypeStruct((KV_HEADS, rows, 128), F32),
             jax.ShapeDtypeStruct((2, 4, 4, T, 640), BF),
-            jax.ShapeDtypeStruct((ROWS, 3 * FF), BF),
+            jax.ShapeDtypeStruct((ROWS, 2 * FF), BF),
+            jax.ShapeDtypeStruct((ROWS, FF // 4), BF),
             jax.ShapeDtypeStruct((T, D), BF),
             jax.ShapeDtypeStruct((T, D), BF),
             jax.ShapeDtypeStruct((T, D), F32),
@@ -1252,7 +1277,7 @@
             jax.ShapeDtypeStruct((8, 1024), F32),
         ),
         in_specs=[vmem] * 2 + [hbm] * 2 + [vmem] * 3 + [hbm] * 8,
-        out_specs=(vmem,) + (hbm,) * 2 + (vmem,) * 6,
+        out_specs=(vmem,) + (hbm,) * 2 + (vmem,) * 7,
         scratch_shapes=[
             pltpu.VMEM((4, 240, D), BF),
             pltpu.VMEM((4, 240, FF), BF),
@@ -1276,11 +1301,13 @@
             pltpu.VMEM((KV_HEADS, rows, KEYS), BF),
             pltpu.VMEM((2, 4, 4, T, 640), BF),
             pltpu.VMEM((2, 4, 4, T, 640), BF),
-            pltpu.VMEM((ROWS, 3 * FF), BF),
+            pltpu.VMEM((ROWS, 2 * FF), BF),
+            pltpu.VMEM((ROWS, FF), BF),
+            *sum_scratch(FF, HALF)[:3],
             pltpu.SemaphoreType.DMA((10,)),
             pltpu.SemaphoreType.DMA((13,)),
         ]
-        + sems(28),
+        + sems(56),
         compiler_params=pltpu.CompilerParams(
             collective_id=4, has_side_effects=True, vmem_limit_bytes=VMEM_LIMIT
         ),
@@ -1293,23 +1320,23 @@
 def per_device(hidden, chosen, positions, w_query, w_key, w_value, w_output, w_gate, w_up, w_down, gain_attn, gain_ffn, router, d_out):
     tokens, upstream = hidden[0], d_out[0]
     own_w = (w_output, w_gate, w_up, w_down.T)
-    frequency = THETA ** (-jnp.arange(0, HEAD_DIM // 2).astype(F32) * 2.0 / HEAD_DIM)
+    frequency = (THETA ** (-np.arange(0, HEAD_DIM // 2) * 2.0 / HEAD_DIM)).astype(np.float32)
     vec = jnp.stack([gain_attn, gain_ffn, router]).astype(F32)
     vec = jnp.pad(vec, ((0, 5), (0, 16)))
     (
         mix_heads, prob, q_heads, kv_all, h, up_c, x1, cosine, sine, place, vec_in, wq, wk, wv, *rest_w
     ) = front(
-        tokens.T, upstream.T, chosen, positions, jnp.tile(frequency, 4)[None, :], vec,
+        tokens.T, upstream.T, chosen, positions, np.tile(frequency, 4)[None, :], vec,
         w_query, w_key.T, w_value.T, *own_w
     )
-    d_q_heads, d_kv, g_one, d_attn, mixture, d_mid, out_c, d_logit, vec_out = dense(
+    d_q_heads, d_kv, g_one, sums_down, d_attn, mixture, d_mid, out_c, d_logit, vec_out = dense(
         mix_heads, q_heads, prob, kv_all, h, up_c, vec_in, own_w, rest_w
     )
-    s_gate, s_up, s_two, s_three, vector, both = back(
-        d_kv, g_one, d_q_heads, d_attn, mixture, x1, h, d_mid, out_c, d_logit, vec_in, vec_out, cosine, sine, wq, wk, wv
+    s_gate, s_up, s_down, s_two, s_three, vector, both = back(
+        d_kv, g_one, sums_down, d_q_heads, d_attn, mixture, x1, h, d_mid, out_c, d_logit, vec_in, vec_out, cosine, sine, wq, wk, wv
     )
     output, d_tokens, g_query, g_key, g_value, g_output, g_gate, g_up, g_down, vectors = finish(
-        s_gate, s_up, s_two, s_three, vector, both, place, tokens.T, upstream.T
+        s_gate, s_up, s_down, s_two, s_three, vector, both, place, tokens.T, upstream.T
     )
     return (
         output.T[None],

time: 192 us -> 179 us (0.932)
  Pallas kernels: 186 us -> 174 us
    pallas_call x1, Pallas kernels: 91 us -> 79.9 us  [back(): pl.pallas_call(back_kernel, name='back', out_shape=(jax.ShapeDtypeStruct(...]
where the time goes in v3:
time: 179 us
  Pallas kernels  174 us (97%)
  local copies, waits for them, and re-layouts  3.36 us (2%)
    pallas_call x1, Pallas kernels, back(): pl.pallas_call(back_kernel, name='back', out_shape=(jax.ShapeDtypeStruct(...  79.9 us
    pallas_call x1, Pallas kernels, front(): pl.pallas_call(front_kernel, name='front', out_shape=(jax.ShapeDtypeStruc...  55.5 us
    pallas_call x1, Pallas kernels, dense(): pl.pallas_call(dense_kernel, name='dense', out_shape=(jax.ShapeDtypeStruc...  31.2 us
    pallas_call x1, Pallas kernels, finish(): pl.pallas_call(finish_kernel, name='finish', out_shape=tuple((jax.ShapeDt...  7.78 us

profile of v3, /device:TPU:0, one launch (start us, length us, event | category | flops | bytes accessed | tf_op | source)
XLA Modules:
  0.0 179.1 jit_solution(12982612940182885303)
XLA Ops:
  0.6 0.7 stack.12
  1.3 0.7 stack.13
  2.0 0.7 stack.14
  2.6 0.6 fusion.9.vec_ref
  3.2 55.5 %front.1 = (f32[5,192,128]{2,1,0:T(8,128)}, bf16[5,192,2048]{2,1,0:T(8,128)(2,1)}, bf16[5,192,128]{2,1,0:T(8,128)(2,1)}, bf16[2,4,4,64,640]{4,3,2,1,0:T(8,128)(2...) custom-call(f32[960,128]{1,0:T(8,128)} %bitcast.21, ...), custom_call_target="tpu_custom_call" | custom-call | flops 5000000000 | bytes 90000000 | tf_op jit(solution)/shard_map/front/pallas_call | solution.py:397
  58.7 31.2 %dense.1 = (f32[5,192,128]{2,1,0:T(8,128)}, bf16[2,4,4,64,640]{4,3,2,1,0:T(8,128)(2,1)}, bf16[256,5120]{1,0:T(8,128)(2,1)}, bf16[256,640]{1,0:T(8,128)(2,1)}, bf...) custom-call(f32[5,192,128]{2,1,0:T(8,128)} %get-tuple-element.57.mix, ...), custom_call_target="tpu_custom_call" | custom-call | flops 20000000000 | bytes 40000000 | tf_op jit(solution)/shard_map/dense/pallas_call | solution.py:1264
  89.9 79.9 %back.1 = (bf16[256,2560]{1,0:T(8,128)(2,1)}, bf16[256,2560]{1,0:T(8,128)(2,1)}, bf16[256,2560]{1,0:T(8,128)(2,1)}, bf16[256,2048]{1,0:T(8,128)(2,1)}, bf16[256,...) custom-call(bf16[2,4,4,64,640]{4,3,2,1,0:T(8,128)(2,1)} %get-tuple-element.68.part_ref, ...), custom_call_target="tpu_custom_call" | custom-call | flops 2000000000 | bytes 200000000 | tf_op jit(solution)/shard_map/back/pallas_call | solution.py:907
  169.9 7.8 %finish.1 = (f32[960,128]{1,0:T(8,128)}, f32[960,128]{1,0:T(8,128)}, f32[240,960]{1,0:T(8,128)}, f32[320,240]{1,0:T(8,128)}, f32[320,240]{1,0:T(8,128)}, /*index...) custom-call(bf16[256,2560]{1,0:T(8,128)(2,1)} %get-tuple-element.84.g_gat, ...), custom_call_target="tpu_custom_call" | custom-call | bytes 16000000 | tf_op jit(solution)/shard_map/finish/pallas_call | solution.py:1024
  177.7 1.4 fusion.10

commit v4 on v3

--- a/solution.py
+++ b/solution.py
@@ -67,13 +67,16 @@
 FAR = (("x", 2), ("z", 2))
 
 
-def greet(me, partners):
+def hail(me, partners):
     barrier = pltpu.get_barrier_semaphore()
     for axis, step in partners:
         pl.semaphore_signal(
             barrier, inc=1, device_id=neighbour(me, axis, step), device_id_type=MESH
         )
-    pl.semaphore_wait(barrier, len(partners))
+
+
+def meet(partners):
+    pl.semaphore_wait(pltpu.get_barrier_semaphore(), len(partners))
 
 
 class Sends:
@@ -252,7 +255,7 @@
 
 
 def front_kernel(
-    hidden_ref, d_out_ref, chosen_ref, pos_ref, freq_ref, vec_ref, wq_ref, wk_ref, wv_ref,
+    hidden_ref, d_out_ref, chosen_ref, pos_ref, freq_ref, gain_a_ref, gain_f_ref, router_ref, wq_ref, wk_ref, wv_ref,
     wo_ref, wg_ref, wu_ref, wd_ref,
     mix_ref, prob_out, q_ref, kv_out, h_ref, up_ref, x1_ref, cos_ref, sin_ref, place_ref, vec_out_ref,
     wq_out, wk_out, wv_out, wos_ref, wgs_ref, wus_ref, wds_ref,
@@ -266,7 +269,7 @@
     for k, (own, to) in enumerate(((wq_ref, wq), (wk_ref, wk), (wv_ref, wv))):
         loads.append(pltpu.make_async_copy(own, to.at[0], load_sems.at[k]))
         loads[-1].start()
-    greet(me, NEAR + WEIGHT)
+    hail(me, NEAR + WEIGHT)
     sends = Sends(me, send_sems, recv_sems)
     early, query, late = Shards(sends), Shards(sends), Shards(sends)
     odd = lax.rem(x, 2)
@@ -280,15 +283,6 @@
         stores[-1].start()
 
     def main():
-        vec_far = sends.start(vec_ref, vecs.at[2], "y", 1)
-        early.far(wk_ref, wk, 160)
-        early.far(wv_ref, wv, 160)
-        vec_near = sends.start(vec_ref, vecs.at[1], "core", 1)
-        early.near(wk_ref, wk)
-        early.near(wv_ref, wv)
-        query.far(wq_ref, wq, 128)
-        query.near(wq_ref, wq)
-        vecs[0] = vec_ref[...]
         flag = jnp.where(chosen_ref[...] > 0, 1.0, 0.0)
         token = lax.broadcasted_iota(jnp.int32, (PAIR, PAIR), 0)
         lane = lax.broadcasted_iota(jnp.int32, (PAIR, PAIR), 1)
@@ -303,6 +297,18 @@
             jnp.sum(place * pos_ref[...].astype(F32), axis=1, keepdims=True), (PAIR, PAIR)
         )
         compact_h[...] = dot(place_low, hidden_ref[...].astype(BF), NT).astype(BF)
+        vecs[0] = jnp.zeros((8, 256), F32)
+        for k, ref in enumerate((gain_a_ref, gain_f_ref, router_ref)):
+            vecs[0, k : k + 1, :240] = ref[...].astype(F32).reshape(1, 240)
+        meet(NEAR + WEIGHT)
+        vec_far = sends.start(vecs.at[0], vecs.at[2], "y", 1)
+        early.far(wk_ref, wk, 160)
+        early.far(wv_ref, wv, 160)
+        vec_near = sends.start(vecs.at[0], vecs.at[1], "core", 1)
+        early.near(wk_ref, wk)
+        early.near(wv_ref, wv)
+        query.far(wq_ref, wq, 128)
+        query.near(wq_ref, wq)
         swaps = [sends.start(c.at[give], g, "pair", 1) for c, g in ((compact_h, got_h), (compact_p, got_p))]
         yield
         compact_d[...] = dot(place_low, d_out_ref[...].astype(BF), NT).astype(BF)
@@ -387,11 +393,11 @@
 
 
 FRONT_ORDER = (
-    "mmmommtmmoumdmommmtummdmmtumdm",
+    "mmmotmmummommmomdmtummtdmmumdm",
 )
 
 
-def front(hidden, d_out, chosen, pos, freq, vec, w_query, w_key, w_value, *later):
+def front(hidden, d_out, chosen, pos, freq, gain_a, gain_f, router, w_query, w_key, w_value, *later):
     vmem, hbm = pl.BlockSpec(memory_space=pltpu.VMEM), pl.BlockSpec(memory_space=pl.ANY)
     rows = GROUPS * T
     return pl.pallas_call(
@@ -415,7 +421,7 @@
         )
         + tuple(jax.ShapeDtypeStruct((3,) + w.shape, BF) for w in later[:3])
         + (jax.ShapeDtypeStruct((1,) + later[3].shape, BF),),
-        in_specs=[vmem] * 6 + [hbm] * 7,
+        in_specs=[vmem] * 8 + [hbm] * 7,
         out_specs=(vmem, hbm, vmem, hbm) + (vmem,) * 7 + (hbm,) * 7,
         scratch_shapes=[
             pltpu.VMEM((PAIR, D), BF),
@@ -440,7 +446,7 @@
             collective_id=1, has_side_effects=True, vmem_limit_bytes=VMEM_LIMIT
         ),
         cost_estimate=pl.CostEstimate(flops=5_000_000_000, bytes_accessed=90_000_000, transcendentals=0),
-    )(hidden, d_out, chosen, pos, freq, vec, w_query, w_key, w_value, *later)
+    )(hidden, d_out, chosen, pos, freq, gain_a, gain_f, router, w_query, w_key, w_value, *later)
 
 
 def key_steps(me, sends, part_ref, out_ref, low, out_b, full, sums, nlow, nout, nfull, mine, y_in):
@@ -773,7 +779,7 @@
 
 
 def back_kernel(
-    part_ref, g_in, sums_ref, dq_ref, d_attn_ref, mixture_ref, x1_ref, h_ref, d_mid_ref, out_ref, logit_ref, vec_ref, vec_part_ref,
+    part_ref, g_in, sums_ref, dq_ref, d_attn_ref, mixture_ref, x1_ref, h_ref, d_mid_ref, logit_ref, vec_ref, vec_part_ref,
     cos_ref, sin_ref, wq_in, wk_in, wv_in,
     gate_ref, up_ref, down_ref, two_ref, three_ref, vec_out_ref, both_ref,
     own, ra, rb, xs, ra_all, rb_all, xs_all, xs_relay, g_two, g_three, d_x1_s, vec_all, keep_v, got_v,
@@ -798,7 +804,7 @@
     ]
     for copy in loads:
         copy.start()
-    greet(me, NEAR + WEIGHT + FAR)
+    hail(me, NEAR + WEIGHT + FAR)
     sends = Sends(me, *scratch[-2:])
     odd = lax.rem(me[4], 2)
     keep = pl.ds(pl.multiple_of(odd * T, T), T)
@@ -807,6 +813,17 @@
 
     def turned_back(tile):
         return tile * cosine - swapped(tile) * sine
+
+    for j in range(KV_HEADS):
+        for g in range(GROUPS):
+            at = HEAD_DIM * (GROUPS * j + g)
+            ra[:, at : at + HEAD_DIM] = turned_back(dq_ref[j, g * T : (g + 1) * T]).astype(BF)[:, :HEAD_DIM]
+    ra[:, D:] = d_attn_ref[...]
+    xs[...] = jnp.zeros_like(xs)
+    for k, (a, b) in enumerate(zip(our_order(me, cut_four(x1_ref)), our_order(me, cut_four(mixture_ref)))):
+        xs[k, :, :240] = a
+        xs[k, :, 256:496] = b
+    meet(NEAR + WEIGHT + FAR)
 
     def keys():
         yield from key_steps(me, sends, part_ref, own, *key_scr)
@@ -825,8 +842,7 @@
         r1 = lax.rsqrt(jnp.mean(h * h, axis=-1, keepdims=True) + EPS)
         d_first, g_gain_a = norm_back_rows(h, r1, vec_ref[0:1, :D], d_x1)
         d_h = d_mid_ref[...] + d_first + logit_ref[:, 0:1] * vec_ref[2:3, :D]
-        both_ref[keep, :D] = out_ref[...]
-        both_ref[keep, D:] = d_h.astype(BF)
+        both_ref[keep] = d_h.astype(BF)
         swap = sends.start(both_ref.at[keep], both_ref.at[keep], "pair", 1)
         vec_all[...] = vec_part_ref[...]
         vec_all[0:1, :D] = g_gain_a
@@ -847,15 +863,6 @@
         swap.wait_recv()
 
     def queries():
-        for j in range(KV_HEADS):
-            for g in range(GROUPS):
-                at = HEAD_DIM * (GROUPS * j + g)
-                ra[:, at : at + HEAD_DIM] = turned_back(dq_ref[j, g * T : (g + 1) * T]).astype(BF)[:, :HEAD_DIM]
-        ra[:, D:] = d_attn_ref[...]
-        xs[...] = jnp.zeros_like(xs)
-        for k, (a, b) in enumerate(zip(our_order(me, cut_four(x1_ref)), our_order(me, cut_four(mixture_ref)))):
-            xs[k, :, :240] = a
-            xs[k, :, 256:496] = b
         share = everyone_steps(
             sends, (("all", ra, ra_all, None), ("one", [xs.at[k] for k in range(4)], xs_all, xs_relay))
         )
@@ -896,9 +903,9 @@
 
 
 ORDER = (
-    "gkdqukddkuudgggkkuggqduqdkkuudggqqkududk",
-    "ggqduqggukqgkukgqudgqgkuuqqqkddgqqgkuuqd",
-    "qgkqudgqqgkuq",
+    "kgdukkquugkkgddguukkqdqgdukgkdqudqggkqdk",
+    "qgkguqgdqugddqqgukguqqgugdudqqkuguqqdkuu",
+    "gdgkuuqgqgqqk",
 )
 
 
@@ -914,7 +921,7 @@
             jax.ShapeDtypeStruct((ROWS, REST), BF),
             jax.ShapeDtypeStruct((ROWS, 640), BF),
             jax.ShapeDtypeStruct((8, 1024), F32),
-            jax.ShapeDtypeStruct((PAIR, 2 * D), BF),
+            jax.ShapeDtypeStruct((PAIR, D), BF),
         ),
         in_specs=[vmem, hbm] + [vmem] * (len(args) - 5) + [hbm] * 3,
         out_specs=(hbm,) * 4 + (vmem,) * 3,
@@ -966,8 +973,8 @@
 
 
 def finish_kernel(
-    g_gate_ref, g_up_ref, g_down_ref, two_ref, three_ref, vec_ref, both_ref, place_ref, hidden_ref, d_out_ref,
-    out_ref, d_hidden_ref, query_ref, key_ref, value_ref, output_ref, gate_ref, up_ref, down_ref, vec_out_ref,
+    g_gate_ref, g_up_ref, g_down_ref, two_ref, three_ref, vec_ref, out_rows_ref, d_rows_ref, place_ref, hidden_ref, d_out_ref,
+    out_ref, d_hidden_ref, query_ref, key_ref, value_ref, output_ref, gate_ref, up_ref, down_ref, vec_a_ref, vec_f_ref, vec_r_ref,
     low_one, low_down, low_two, low_three, wide_one, wide_two, wide_down, wide_kv, rows, load_sems, store_sems,
 ):
     keep = pl.ds(0, 240)
@@ -990,8 +997,10 @@
         stores.append(pltpu.make_async_copy(a, b, store_sems.at[len(stores)]))
         stores[-1].start()
 
-    for k, (base, to) in enumerate(((hidden_ref, out_ref), (d_out_ref, d_hidden_ref))):
-        rows[k] = base[...] + dot(both_ref[:, D * k : D * (k + 1)], place_ref[...], TN)
+    for k, (base, at_rank, to) in enumerate(
+        ((hidden_ref, out_rows_ref, out_ref), (d_out_ref, d_rows_ref, d_hidden_ref))
+    ):
+        rows[k] = base[...] + dot(at_rank[...], place_ref[...], TN)
         store(rows.at[k], to)
     for k in range(4):
         loads[k].wait()
@@ -1013,20 +1022,22 @@
         store(wide_kv.at[k], to)
     core, ylo = lax.axis_index("core") == 1, lax.axis_index("ylo") == 1
     p = [vec_ref[:, 240 * k : 240 * (k + 1)] for k in range(4)]
-    vec_out_ref[...] = jnp.where(ylo, jnp.where(core, p[3], p[2]), jnp.where(core, p[1], p[0]))
+    p = jnp.where(ylo, jnp.where(core, p[3], p[2]), jnp.where(core, p[1], p[0]))
+    for k, ref in enumerate((vec_a_ref, vec_f_ref, vec_r_ref)):
+        ref[...] = p[k : k + 1].reshape(240)
     for copy in stores:
         copy.wait()
 
 
 def finish(*args):
     vmem, hbm = pl.BlockSpec(memory_space=pltpu.VMEM), pl.BlockSpec(memory_space=pl.ANY)
-    shapes = [(D, PAIR), (D, PAIR), (240, D), (320, 240), (320, 240), (240, D), (240, FF), (240, FF), (D, 640), (8, 240)]
+    shapes = [(D, PAIR), (D, PAIR), (240, D), (320, 240), (320, 240), (240, D), (240, FF), (240, FF), (D, 640), (240,), (240,), (240,)]
     return pl.pallas_call(
         finish_kernel,
         name="finish",
         out_shape=tuple(jax.ShapeDtypeStruct(shape, F32) for shape in shapes),
-        in_specs=[hbm] * 5 + [vmem] * 5,
-        out_specs=(hbm,) * 9 + (vmem,),
+        in_specs=[hbm] * 5 + [vmem] * 6,
+        out_specs=(hbm,) * 9 + (vmem,) * 3,
         scratch_shapes=[
             pltpu.VMEM((2, 240, WIDE), BF),
             pltpu.VMEM((240, WIDE), BF),
@@ -1121,12 +1132,8 @@
     )
     for copy in loads[4]:
         copy.start()
-    greet(me, NEAR[:4] + WEIGHT)
+    hail(me, NEAR[:4] + WEIGHT)
     sends = Sends(me, send_sems, recv_sems)
-    down = [
-        sends.start(wd_ref, wd.at[1], "core", 1),
-        sends.start(wds_ref.at[0], wd.at[3], "core", 1),
-    ]
     shards = [shard_of(me, k) for k in range(4)]
 
     def run640(k):
@@ -1154,6 +1161,11 @@
     xs[...] = jnp.zeros_like(xs)
     for k in range(4):
         xs[k, :, :240] = x2_k[k]
+    meet(NEAR[:4] + WEIGHT)
+    down = [
+        sends.start(wd_ref, wd.at[1], "core", 1),
+        sends.start(wds_ref.at[0], wd.at[3], "core", 1),
+    ]
     shares = [everyone_steps(sends, (("one", [xs.at[k] for k in range(4)], xs_all, xs_relay),))]
     next(shares[0])
     loaded(1)
@@ -1172,7 +1184,10 @@
     ffn_out = sum(dot(inner[:, run640(k)], wd[k], NT) for k in range(4))
     route = jax.nn.sigmoid(jnp.sum(hidden * route_w, axis=-1, keepdims=True))
     branch = attn_out + ffn_out
-    out_ref[...] = (route * branch).astype(BF)
+    odd = lax.rem(me[4], 2)
+    keep = pl.ds(pl.multiple_of(odd * T, T), T)
+    out_ref[keep] = (route * branch).astype(BF)
+    swap = sends.start(out_ref.at[keep], out_ref.at[keep], "pair", 1)
     upstream = up_ref[...]
     d_branch = upstream * route
     d_logit = route * (1.0 - route) * jnp.sum(upstream * branch, axis=-1, keepdims=True)
@@ -1253,6 +1268,7 @@
         g_ref[:, c] = dot(xs_all[...], dgu_all[:, c], TN).astype(BF)
         store(g_ref.at[:, c], g_out.at[:, c])
     together(wide)
+    swap.wait_recv()
     for copy in stores:
         copy.wait()
     sends.finish()
@@ -1272,7 +1288,7 @@
             jax.ShapeDtypeStruct((T, D), BF),
             jax.ShapeDtypeStruct((T, D), BF),
             jax.ShapeDtypeStruct((T, D), F32),
-            jax.ShapeDtypeStruct((T, D), BF),
+            jax.ShapeDtypeStruct((PAIR, D), BF),
             jax.ShapeDtypeStruct((T, 128), F32),
             jax.ShapeDtypeStruct((8, 1024), F32),
         ),
@@ -1307,7 +1323,7 @@
             pltpu.SemaphoreType.DMA((10,)),
             pltpu.SemaphoreType.DMA((13,)),
         ]
-        + sems(56),
+        + sems(57),
         compiler_params=pltpu.CompilerParams(
             collective_id=4, has_side_effects=True, vmem_limit_bytes=VMEM_LIMIT
         ),
@@ -1321,22 +1337,20 @@
     tokens, upstream = hidden[0], d_out[0]
     own_w = (w_output, w_gate, w_up, w_down.T)
     frequency = (THETA ** (-np.arange(0, HEAD_DIM // 2) * 2.0 / HEAD_DIM)).astype(np.float32)
-    vec = jnp.stack([gain_attn, gain_ffn, router]).astype(F32)
-    vec = jnp.pad(vec, ((0, 5), (0, 16)))
     (
         mix_heads, prob, q_heads, kv_all, h, up_c, x1, cosine, sine, place, vec_in, wq, wk, wv, *rest_w
     ) = front(
-        tokens.T, upstream.T, chosen, positions, np.tile(frequency, 4)[None, :], vec,
+        tokens.T, upstream.T, chosen, positions, np.tile(frequency, 4)[None, :], gain_attn, gain_ffn, router,
         w_query, w_key.T, w_value.T, *own_w
     )
     d_q_heads, d_kv, g_one, sums_down, d_attn, mixture, d_mid, out_c, d_logit, vec_out = dense(
         mix_heads, q_heads, prob, kv_all, h, up_c, vec_in, own_w, rest_w
     )
-    s_gate, s_up, s_down, s_two, s_three, vector, both = back(
-        d_kv, g_one, sums_down, d_q_heads, d_attn, mixture, x1, h, d_mid, out_c, d_logit, vec_in, vec_out, cosine, sine, wq, wk, wv
+    s_gate, s_up, s_down, s_two, s_three, vector, d_rows = back(
+        d_kv, g_one, sums_down, d_q_heads, d_attn, mixture, x1, h, d_mid, d_logit, vec_in, vec_out, cosine, sine, wq, wk, wv
     )
-    output, d_tokens, g_query, g_key, g_value, g_output, g_gate, g_up, g_down, vectors = finish(
-        s_gate, s_up, s_down, s_two, s_three, vector, both, place, tokens.T, upstream.T
+    output, d_tokens, g_query, g_key, g_value, g_output, g_gate, g_up, g_down, *vectors = finish(
+        s_gate, s_up, s_down, s_two, s_three, vector, out_c, d_rows, place, tokens.T, upstream.T
     )
     return (
         output.T[None],

time: 179 us -> 177 us (0.989)
  local copies, waits for them, and re-layouts: 3.36 us -> 0 us
  Pallas kernels: 174 us -> 176 us
    another operation x3 -> x0, local copies, waits for them, and re-layouts: 1.98 us -> none  [per_device(): vec = jnp.stack([gain_attn, gain_ffn, router]).astype(F32)]
where the time goes in v4:
time: 177 us
  Pallas kernels  176 us (99%)
    pallas_call x1, Pallas kernels, back(): pl.pallas_call(back_kernel, name='back', out_shape=(jax.ShapeDtypeStruct(...  81.5 us
    pallas_call x1, Pallas kernels, front(): pl.pallas_call(front_kernel, name='front', out_shape=(jax.ShapeDtypeStruc...  55.7 us
    pallas_call x1, Pallas kernels, dense(): pl.pallas_call(dense_kernel, name='dense', out_shape=(jax.ShapeDtypeStruc...  31.3 us
    pallas_call x1, Pallas kernels, finish(): pl.pallas_call(finish_kernel, name='finish', out_shape=tuple((jax.ShapeDt...  7.77 us

profile of v4, /device:TPU:0, one launch (start us, length us, event | category | flops | bytes accessed | tf_op | source)
XLA Modules:
  0.0 177.0 jit_solution(896836113375942117)
XLA Ops:
  0.6 55.7 %front.1 = (f32[5,192,128]{2,1,0:T(8,128)}, bf16[5,192,2048]{2,1,0:T(8,128)(2,1)}, bf16[5,192,128]{2,1,0:T(8,128)(2,1)}, bf16[2,4,4,64,640]{4,3,2,1,0:T(8,128)(2...) custom-call(f32[960,128]{1,0:T(8,128)} %bitcast.18, ...), custom_call_target="tpu_custom_call" | custom-call | flops 5000000000 | bytes 90000000 | tf_op jit(solution)/shard_map/front/pallas_call | solution.py:403
  56.3 31.3 %dense.1 = (f32[5,192,128]{2,1,0:T(8,128)}, bf16[2,4,4,64,640]{4,3,2,1,0:T(8,128)(2,1)}, bf16[256,5120]{1,0:T(8,128)(2,1)}, bf16[256,640]{1,0:T(8,128)(2,1)}, bf...) custom-call(f32[5,192,128]{2,1,0:T(8,128)} %get-tuple-element.59.mix, ...), custom_call_target="tpu_custom_call" | custom-call | flops 20000000000 | bytes 40000000 | tf_op jit(solution)/shard_map/dense/pallas_call | solution.py:1280
  87.6 81.5 %back.1 = (bf16[256,2560]{1,0:T(8,128)(2,1)}, bf16[256,2560]{1,0:T(8,128)(2,1)}, bf16[256,2560]{1,0:T(8,128)(2,1)}, bf16[256,2048]{1,0:T(8,128)(2,1)}, bf16[256,...) custom-call(bf16[2,4,4,64,640]{4,3,2,1,0:T(8,128)(2,1)} %get-tuple-element.70.part_ref, ...), custom_call_target="tpu_custom_call" | custom-call | flops 2000000000 | bytes 200000000 | tf_op jit(solution)/shard_map/back/pallas_call | solution.py:914
  169.1 7.8 %finish.1 = (f32[960,128]{1,0:T(8,128)}, f32[960,128]{1,0:T(8,128)}, f32[240,960]{1,0:T(8,128)}, f32[320,240]{1,0:T(8,128)}, f32[320,240]{1,0:T(8,128)}, /*index...) custom-call(bf16[256,2560]{1,0:T(8,128)(2,1)} %get-tuple-element.85., ...), custom_call_target="tpu_custom_call" | custom-call | bytes 16000000 | tf_op jit(solution)/shard_map/finish/pallas_call | solution.py:1035

commit v5 on v4

--- a/solution.py
+++ b/solution.py
@@ -360,14 +360,14 @@
             for g in range(GROUPS):
                 at = HEAD_DIM * (GROUPS * j + g)
                 tile = jnp.concatenate([q_pre[:, at : at + HEAD_DIM], zero], axis=1)
-                q_ref[j, g * T : (g + 1) * T] = (tile * cosine + swapped(tile) * sine).astype(BF)
+                q_ref[j, g * T : (g + 1) * T] = ((tile * cosine + swapped(tile) * sine) * SCALE).astype(BF)
         yield
         yield from gather
         for a, b in ((kv_ref, kv_out), (wq, wq_out), (wk, wk_out), (wv, wv_out)):
             store(a, b)
         for j in range(KV_HEADS):
             tile = kv_ref[:, :, :, :, 128 * j : 128 * (j + 1)].reshape(KEYS, 128)
-            scores = dot(q_ref[j], tile, NT) * SCALE
+            scores = dot(q_ref[j], tile, NT)
             column = lax.broadcasted_iota(jnp.int32, scores.shape, 1)
             scores = jnp.where(column < limit, scores, -1e30)
             exponent = jnp.exp(scores - jnp.max(scores, axis=-1, keepdims=True))
@@ -393,7 +393,7 @@
 
 
 FRONT_ORDER = (
-    "mmmotmmummommmomdmtummtdmmumdm",
+    "mmmotmmmmmomummdmotummtdmmumdm",
 )
 
 
@@ -975,7 +975,7 @@
 def finish_kernel(
     g_gate_ref, g_up_ref, g_down_ref, two_ref, three_ref, vec_ref, out_rows_ref, d_rows_ref, place_ref, hidden_ref, d_out_ref,
     out_ref, d_hidden_ref, query_ref, key_ref, value_ref, output_ref, gate_ref, up_ref, down_ref, vec_a_ref, vec_f_ref, vec_r_ref,
-    low_one, low_down, low_two, low_three, wide_one, wide_two, wide_down, wide_kv, rows, load_sems, store_sems,
+    low_one, low_down, low_two, low_three, wide_one, wide_two, wide_down, wide_kv, rows, ranked, load_sems, store_sems,
 ):
     keep = pl.ds(0, 240)
     runs_one = [pl.ds(1280 * k, 1280) for k in range(2)]
@@ -991,17 +991,16 @@
         for c in runs:
             loads.append(pltpu.make_async_copy(src.at[keep, c], dst.at[:, c], load_sems.at[len(loads)]))
             loads[-1].start()
+    for k, (base, at_rank) in enumerate(((hidden_ref, out_rows_ref), (d_out_ref, d_rows_ref))):
+        for src, dst in ((base, rows.at[k]), (at_rank, ranked.at[k])):
+            loads.append(pltpu.make_async_copy(src, dst, load_sems.at[len(loads)]))
+            loads[-1].start()
     stores = []
 
     def store(a, b):
         stores.append(pltpu.make_async_copy(a, b, store_sems.at[len(stores)]))
         stores[-1].start()
 
-    for k, (base, at_rank, to) in enumerate(
-        ((hidden_ref, out_rows_ref, out_ref), (d_out_ref, d_rows_ref, d_hidden_ref))
-    ):
-        rows[k] = base[...] + dot(at_rank[...], place_ref[...], TN)
-        store(rows.at[k], to)
     for k in range(4):
         loads[k].wait()
         c = runs_one[k % 2]
@@ -1020,6 +1019,11 @@
     for k, to in enumerate((key_ref, value_ref)):
         wide_kv[k] = low_three[:, 320 * k : 320 * (k + 1)].astype(F32).T
         store(wide_kv.at[k], to)
+    for k, to in enumerate((out_ref, d_hidden_ref)):
+        loads[10 + 2 * k].wait()
+        loads[11 + 2 * k].wait()
+        rows[k] = rows[k] + dot(ranked[k], place_ref[...], TN)
+        store(rows.at[k], to)
     core, ylo = lax.axis_index("core") == 1, lax.axis_index("ylo") == 1
     p = [vec_ref[:, 240 * k : 240 * (k + 1)] for k in range(4)]
     p = jnp.where(ylo, jnp.where(core, p[3], p[2]), jnp.where(core, p[1], p[0]))
@@ -1036,7 +1040,7 @@
         finish_kernel,
         name="finish",
         out_shape=tuple(jax.ShapeDtypeStruct(shape, F32) for shape in shapes),
-        in_specs=[hbm] * 5 + [vmem] * 6,
+        in_specs=[hbm] * 5 + [vmem] + [hbm] * 2 + [vmem] + [hbm] * 2,
         out_specs=(hbm,) * 9 + (vmem,) * 3,
         scratch_shapes=[
             pltpu.VMEM((2, 240, WIDE), BF),
@@ -1048,7 +1052,8 @@
             pltpu.VMEM((D, 640), F32),
             pltpu.VMEM((2, 320, 240), F32),
             pltpu.VMEM((2, D, PAIR), F32),
-            pltpu.SemaphoreType.DMA((10,)),
+            pltpu.VMEM((2, PAIR, D), BF),
+            pltpu.SemaphoreType.DMA((14,)),
             pltpu.SemaphoreType.DMA((14,)),
         ],
         compiler_params=pltpu.CompilerParams(vmem_limit_bytes=VMEM_LIMIT),
@@ -1256,7 +1261,9 @@
         delta = jnp.sum(d_out.astype(F32) * mix_ref[j], axis=-1, keepdims=True)
         d_score = (prob.astype(F32) * (d_prob - delta)).astype(BF)
         dq_ref[j] = dot(d_score, tile) * SCALE
-        grad = dot(d_score, q_ref[j], TN) * SCALE + dot(prob, d_out, TN)
+        grad = dot(
+            jnp.concatenate([d_score, prob], axis=0), jnp.concatenate([q_ref[j], d_out], axis=0), TN
+        )
         dkv_ref[:, :, :, :, c] = grad.astype(BF).reshape(2, 4, 4, T, 128)
         store(dkv_ref.at[:, :, :, :, c], dkv_out.at[:, :, :, :, c])
         if j == 3:

time: 177 us -> 176 us (level)
  no operation moved by 1% of the time
where the time goes in v5:
time: 176 us; the launch traced here: 175 us
  Pallas kernels  175 us (99%)
    pallas_call x1, Pallas kernels, back(): pl.pallas_call(back_kernel, name='back', out_shape=(jax.ShapeDtypeStruct(...  80.8 us
    pallas_call x1, Pallas kernels, front(): pl.pallas_call(front_kernel, name='front', out_shape=(jax.ShapeDtypeStruc...  55 us
    pallas_call x1, Pallas kernels, dense(): pl.pallas_call(dense_kernel, name='dense', out_shape=(jax.ShapeDtypeStruc...  31.3 us
    pallas_call x1, Pallas kernels, finish(): pl.pallas_call(finish_kernel, name='finish', out_shape=tuple((jax.ShapeDt...  7.37 us

profile of v5, /device:TPU:0, one launch (start us, length us, event | category | flops | bytes accessed | tf_op | source)
XLA Modules:
  0.0 175.4 jit_solution(2300229415955234856)
XLA Ops:
  0.6 55.0 %front.1 = (f32[5,192,128]{2,1,0:T(8,128)}, bf16[5,192,2048]{2,1,0:T(8,128)(2,1)}, bf16[5,192,128]{2,1,0:T(8,128)(2,1)}, bf16[2,4,4,64,640]{4,3,2,1,0:T(8,128)(2...) custom-call(f32[960,128]{1,0:T(8,128)} %bitcast.18, ...), custom_call_target="tpu_custom_call" | custom-call | flops 5000000000 | bytes 90000000 | tf_op jit(solution)/shard_map/front/pallas_call | solution.py:403
  55.7 31.3 %dense.1 = (f32[5,192,128]{2,1,0:T(8,128)}, bf16[2,4,4,64,640]{4,3,2,1,0:T(8,128)(2,1)}, bf16[256,5120]{1,0:T(8,128)(2,1)}, bf16[256,640]{1,0:T(8,128)(2,1)}, bf...) custom-call(f32[5,192,128]{2,1,0:T(8,128)} %get-tuple-element.59.mix, ...), custom_call_target="tpu_custom_call" | custom-call | flops 20000000000 | bytes 40000000 | tf_op jit(solution)/shard_map/dense/pallas_call | solution.py:1287
  87.0 80.8 %back.1 = (bf16[256,2560]{1,0:T(8,128)(2,1)}, bf16[256,2560]{1,0:T(8,128)(2,1)}, bf16[256,2560]{1,0:T(8,128)(2,1)}, bf16[256,2048]{1,0:T(8,128)(2,1)}, bf16[256,...) custom-call(bf16[2,4,4,64,640]{4,3,2,1,0:T(8,128)(2,1)} %get-tuple-element.70.part_ref, ...), custom_call_target="tpu_custom_call" | custom-call | flops 2000000000 | bytes 200000000 | tf_op jit(solution)/shard_map/back/pallas_call | solution.py:914
  167.8 7.4 %finish.1 = (f32[960,128]{1,0:T(8,128)}, f32[960,128]{1,0:T(8,128)}, f32[240,960]{1,0:T(8,128)}, f32[320,240]{1,0:T(8,128)}, f32[320,240]{1,0:T(8,128)}, /*index...) custom-call(bf16[256,2560]{1,0:T(8,128)(2,1)} %get-tuple-element.85., ...), custom_call_target="tpu_custom_call" | custom-call | bytes 16000000 | tf_op jit(solution)/shard_map/finish/pallas_call | solution.py:1039

commit v6 on v5

--- a/solution.py
+++ b/solution.py
@@ -844,8 +844,10 @@
         d_h = d_mid_ref[...] + d_first + logit_ref[:, 0:1] * vec_ref[2:3, :D]
         both_ref[keep] = d_h.astype(BF)
         swap = sends.start(both_ref.at[keep], both_ref.at[keep], "pair", 1)
-        vec_all[...] = vec_part_ref[...]
-        vec_all[0:1, :D] = g_gain_a
+        vec_all[...] = jnp.zeros_like(vec_all)
+        for k, row in enumerate((g_gain_a, vec_part_ref[1:2, :D], vec_part_ref[2:3, :D])):
+            for i in range(2):
+                vec_all[2 * k + i : 2 * k + i + 1, :480] = row[:, 480 * i : 480 * (i + 1)]
         vectors = vector_steps(sends, vec_all, vec_out_ref, keep_v, got_v)
         next(vectors)
         yield
@@ -920,7 +922,7 @@
             jax.ShapeDtypeStruct((ROWS, WIDE), BF),
             jax.ShapeDtypeStruct((ROWS, REST), BF),
             jax.ShapeDtypeStruct((ROWS, 640), BF),
-            jax.ShapeDtypeStruct((8, 1024), F32),
+            jax.ShapeDtypeStruct((8, 512), F32),
             jax.ShapeDtypeStruct((PAIR, D), BF),
         ),
         in_specs=[vmem, hbm] + [vmem] * (len(args) - 5) + [hbm] * 3,
@@ -937,9 +939,9 @@
             pltpu.VMEM((ROWS, REST), BF),
             pltpu.VMEM((ROWS, 640), BF),
             pltpu.VMEM((T, D), F32),
-            pltpu.VMEM((8, 1024), F32),
-            pltpu.VMEM((6, 8, 1024), F32),
-            pltpu.VMEM((9, 8, 1024), F32),
+            pltpu.VMEM((8, 512), F32),
+            pltpu.VMEM((6, 8, 512), F32),
+            pltpu.VMEM((9, 8, 512), F32),
             pltpu.VMEM((2, HALF // 8, WIDE // 4), BF),
             pltpu.VMEM((2, HALF // 4, WIDE // 4), BF),
             pltpu.VMEM((2, HALF // 4, WIDE // 4), BF),
@@ -1025,10 +1027,10 @@
         rows[k] = rows[k] + dot(ranked[k], place_ref[...], TN)
         store(rows.at[k], to)
     core, ylo = lax.axis_index("core") == 1, lax.axis_index("ylo") == 1
-    p = [vec_ref[:, 240 * k : 240 * (k + 1)] for k in range(4)]
-    p = jnp.where(ylo, jnp.where(core, p[3], p[2]), jnp.where(core, p[1], p[0]))
-    for k, ref in enumerate((vec_a_ref, vec_f_ref, vec_r_ref)):
-        ref[...] = p[k : k + 1].reshape(240)
+    for v, ref in enumerate((vec_a_ref, vec_f_ref, vec_r_ref)):
+        p = [vec_ref[2 * v + k // 2 : 2 * v + k // 2 + 1, 240 * (k % 2) : 240 * (k % 2 + 1)] for k in range(4)]
+        row = jnp.where(ylo, jnp.where(core, p[3], p[2]), jnp.where(core, p[1], p[0]))
+        ref[...] = row.reshape(240)
     for copy in stores:
         copy.wait()
 

time: 176 us -> 175 us (level)
  no operation moved by 1% of the time
where the time goes in v6:
time: 175 us
  Pallas kernels  174 us (99%)
    pallas_call x1, Pallas kernels, back(): pl.pallas_call(back_kernel, name='back', out_shape=(jax.ShapeDtypeStruct(...  80.4 us
    pallas_call x1, Pallas kernels, front(): pl.pallas_call(front_kernel, name='front', out_shape=(jax.ShapeDtypeStruc...  55 us
    pallas_call x1, Pallas kernels, dense(): pl.pallas_call(dense_kernel, name='dense', out_shape=(jax.ShapeDtypeStruc...  31.3 us
    pallas_call x1, Pallas kernels, finish(): pl.pallas_call(finish_kernel, name='finish', out_shape=tuple((jax.ShapeDt...  7.35 us

profile of v6, /device:TPU:0, one launch (start us, length us, event | category | flops | bytes accessed | tf_op | source)
XLA Modules:
  0.0 174.9 jit_solution(9081314203767482499)
XLA Ops:
  0.6 55.0 %front.1 = (f32[5,192,128]{2,1,0:T(8,128)}, bf16[5,192,2048]{2,1,0:T(8,128)(2,1)}, bf16[5,192,128]{2,1,0:T(8,128)(2,1)}, bf16[2,4,4,64,640]{4,3,2,1,0:T(8,128)(2...) custom-call(f32[960,128]{1,0:T(8,128)} %bitcast.18, ...), custom_call_target="tpu_custom_call" | custom-call | flops 5000000000 | bytes 90000000 | tf_op jit(solution)/shard_map/front/pallas_call | solution.py:403
  55.7 31.3 %dense.1 = (f32[5,192,128]{2,1,0:T(8,128)}, bf16[2,4,4,64,640]{4,3,2,1,0:T(8,128)(2,1)}, bf16[256,5120]{1,0:T(8,128)(2,1)}, bf16[256,640]{1,0:T(8,128)(2,1)}, bf...) custom-call(f32[5,192,128]{2,1,0:T(8,128)} %get-tuple-element.59.mix, ...), custom_call_target="tpu_custom_call" | custom-call | flops 20000000000 | bytes 40000000 | tf_op jit(solution)/shard_map/dense/pallas_call | solution.py:1289
  87.0 80.4 %back.1 = (bf16[256,2560]{1,0:T(8,128)(2,1)}, bf16[256,2560]{1,0:T(8,128)(2,1)}, bf16[256,2560]{1,0:T(8,128)(2,1)}, bf16[256,2048]{1,0:T(8,128)(2,1)}, bf16[256,...) custom-call(bf16[2,4,4,64,640]{4,3,2,1,0:T(8,128)(2,1)} %get-tuple-element.70.part_ref, ...), custom_call_target="tpu_custom_call" | custom-call | flops 2000000000 | bytes 200000000 | tf_op jit(solution)/shard_map/back/pallas_call | solution.py:916
  167.4 7.4 %finish.1 = (f32[960,128]{1,0:T(8,128)}, f32[960,128]{1,0:T(8,128)}, f32[240,960]{1,0:T(8,128)}, f32[320,240]{1,0:T(8,128)}, f32[320,240]{1,0:T(8,128)}, /*index...) custom-call(bf16[256,2560]{1,0:T(8,128)(2,1)} %get-tuple-element.85., ...), custom_call_target="tpu_custom_call" | custom-call | bytes 16000000 | tf_op jit(solution)/shard_map/finish/pallas_call | solution.py:1041

commit v7 on v6

--- a/solution.py
+++ b/solution.py
@@ -1268,7 +1268,7 @@
         )
         dkv_ref[:, :, :, :, c] = grad.astype(BF).reshape(2, 4, 4, T, 128)
         store(dkv_ref.at[:, :, :, :, c], dkv_out.at[:, :, :, :, c])
-        if j == 3:
+        if j == 2:
             next(wide)
             next(wide)
     together(*late)

time: 175 us -> 175 us (level)
  no operation moved by 1% of the time
where the time goes in v7:
time: 175 us
  Pallas kernels  174 us (99%)
    pallas_call x1, Pallas kernels, back(): pl.pallas_call(back_kernel, name='back', out_shape=(jax.ShapeDtypeStruct(...  80.6 us
    pallas_call x1, Pallas kernels, front(): pl.pallas_call(front_kernel, name='front', out_shape=(jax.ShapeDtypeStruc...  55 us
    pallas_call x1, Pallas kernels, dense(): pl.pallas_call(dense_kernel, name='dense', out_shape=(jax.ShapeDtypeStruc...  31.3 us
    pallas_call x1, Pallas kernels, finish(): pl.pallas_call(finish_kernel, name='finish', out_shape=tuple((jax.ShapeDt...  7.35 us

profile of v7, /device:TPU:0, one launch (start us, length us, event | category | flops | bytes accessed | tf_op | source)
XLA Modules:
  0.0 175.2 jit_solution(16737752477375120270)
XLA Ops:
  0.6 55.0 %front.1 = (f32[5,192,128]{2,1,0:T(8,128)}, bf16[5,192,2048]{2,1,0:T(8,128)(2,1)}, bf16[5,192,128]{2,1,0:T(8,128)(2,1)}, bf16[2,4,4,64,640]{4,3,2,1,0:T(8,128)(2...) custom-call(f32[960,128]{1,0:T(8,128)} %bitcast.18, ...), custom_call_target="tpu_custom_call" | custom-call | flops 5000000000 | bytes 90000000 | tf_op jit(solution)/shard_map/front/pallas_call | solution.py:403
  55.7 31.3 %dense.1 = (f32[5,192,128]{2,1,0:T(8,128)}, bf16[2,4,4,64,640]{4,3,2,1,0:T(8,128)(2,1)}, bf16[256,5120]{1,0:T(8,128)(2,1)}, bf16[256,640]{1,0:T(8,128)(2,1)}, bf...) custom-call(f32[5,192,128]{2,1,0:T(8,128)} %get-tuple-element.59.mix, ...), custom_call_target="tpu_custom_call" | custom-call | flops 20000000000 | bytes 40000000 | tf_op jit(solution)/shard_map/dense/pallas_call | solution.py:1289
  87.0 80.6 %back.1 = (bf16[256,2560]{1,0:T(8,128)(2,1)}, bf16[256,2560]{1,0:T(8,128)(2,1)}, bf16[256,2560]{1,0:T(8,128)(2,1)}, bf16[256,2048]{1,0:T(8,128)(2,1)}, bf16[256,...) custom-call(bf16[2,4,4,64,640]{4,3,2,1,0:T(8,128)(2,1)} %get-tuple-element.70.part_ref, ...), custom_call_target="tpu_custom_call" | custom-call | flops 2000000000 | bytes 200000000 | tf_op jit(solution)/shard_map/back/pallas_call | solution.py:916
  167.6 7.4 %finish.1 = (f32[960,128]{1,0:T(8,128)}, f32[960,128]{1,0:T(8,128)}, f32[240,960]{1,0:T(8,128)}, f32[320,240]{1,0:T(8,128)}, f32[320,240]{1,0:T(8,128)}, /*index...) custom-call(bf16[256,2560]{1,0:T(8,128)(2,1)} %get-tuple-element.85., ...), custom_call_target="tpu_custom_call" | custom-call | bytes 16000000 | tf_op jit(solution)/shard_map/finish/pallas_call | solution.py:1041
